TPU v7x, 32 devices: a whole 2x2x4 slice. The times are simulated.
32 devices in a mesh: dp: 4 (over y, x), row: 4 (over z), col: 2 (over core).
Axes of the slice: x: 2, y: 2, z: 4, core: 2. Of those that a mesh axis runs over, the one named last changes fastest.
Arguments:
- tokens_in: bfloat16 [16384, 1024], P(('dp', 'row'), 'col'), may hold values from -6 to 6
- cotangent: bfloat16 [16384, 1024], P(('dp', 'row'), 'col'), may hold values from -6 to 6
- prefix_length: int32 [16], P(('dp', 'row')), may hold values from 102 to 512
- first_gain: float32 [1024], P('col'), may hold values from 0.1 to 1.9
- first_shift: float32 [1024], P('col'), may hold values from -4 to 4
- joint_weight: bfloat16 [1024, 3072], P('row', 'col'), may hold values from -0.1875 to 0.1875
- joint_bias: float32 [2048], P('col'), may hold values from -6 to 6
- output_weight: bfloat16 [1024, 1024], P('col', 'row'), may hold values from -3 to 3
- output_bias: float32 [1024], P('col'), may hold values from -4 to 4
- second_gain: float32 [1024], P('col'), may hold values from 0.1 to 1.9
- second_shift: float32 [1024], P('col'), may hold values from -4 to 4
- up_weight: bfloat16 [1024, 4096], P('row', 'col'), may hold values from -0.1875 to 0.1875
- up_bias: float32 [4096], P('col'), may hold values from -6 to 6
- down_weight: bfloat16 [4096, 1024], P('col', 'row'), may hold values from -0.09375 to 0.09375
- down_bias: float32 [1024], P('col'), may hold values from -4 to 4
Outputs:
- layer_out: bfloat16 [16384, 1024], P(('dp', 'row'), 'col')
- tokens_grad: bfloat16 [16384, 1024], P(('dp', 'row'), 'col')
- grad_first_gain: float32 [1024], P('col')
- grad_first_shift: float32 [1024], P('col')
- grad_joint_weight: float32 [1024, 3072], P('row', 'col')
- grad_joint_bias: float32 [2048], P('col')
- grad_output_weight: float32 [1024, 1024], P('col', 'row')
- grad_output_bias: float32 [1024], P('col')
- grad_second_gain: float32 [1024], P('col')
- grad_second_shift: float32 [1024], P('col')
- grad_up_weight: float32 [1024, 4096], P('row', 'col')
- grad_up_bias: float32 [4096], P('col')
- grad_down_weight: float32 [4096, 1024], P('col', 'row')
- grad_down_bias: float32 [1024], P('col')
All inputs are finite; a program needn't handle non-finite values.
Results may differ from a plain program's by a relative error of at most 0.015.
Values may be sent and summed in bfloat16 or wider, within the bound.
No kernel may reach another device: no remote copies, remote signals or barrier semaphores. Data moves between devices by JAX's collectives and lax.ppermute only.
A program may use at most 128 MiB of HBM per device.

v0:
```python
import math

import jax
import jax.numpy as jnp
from jax import lax
from jax.sharding import PartitionSpec as P

D = 1024
HDIM = 128
LEN = 1024


EPSILON = 1e-05
NEGATIVE = -1e30


def feature_sums(left_sum, right_sum):
    return lax.psum((left_sum, right_sum), "col")


def norm_forward(values, gain_vec, offset):
    totals, squares = feature_sums(jnp.sum(values, axis=1), jnp.sum(values * values, axis=1))
    average = totals / D
    spread = squares / D - average * average
    factor = lax.rsqrt(spread + EPSILON)
    centered = (values - average[:, None]) * factor[:, None]
    return (centered * gain_vec + offset, centered, factor)


def norm_backward(gradient, centered, factor, gain_vec):
    scaled = gradient * gain_vec
    left_sum, right_sum = feature_sums(jnp.sum(scaled, axis=1), jnp.sum(scaled * centered, axis=1))
    back = factor[:, None] * (scaled - left_sum[:, None] / D - centered * (right_sum[:, None] / D))
    return (back, jnp.sum(gradient * centered, axis=0), jnp.sum(gradient, axis=0))


def spread_features(normed):
    return lax.all_gather(normed, "col", axis=1, tiled=True)


def spread_grads(gradient):
    return lax.all_gather(gradient, "col", axis=1, tiled=True)


def rows_forward(full_rows, weight):
    return jnp.dot(
        full_rows,
        lax.all_gather(weight, "row", axis=0, tiled=True),
        preferred_element_type=jnp.float32,
    )


def cols_forward(values, weight):
    partials = jnp.dot(
        values,
        lax.all_gather(weight, "row", axis=1, tiled=True),
        preferred_element_type=jnp.float32,
    )
    return lax.psum_scatter(
        partials.astype(jnp.bfloat16), "col", scatter_dimension=1, tiled=True
    ).astype(jnp.float32)


def cols_backward(grads_full, weight):
    return lax.dot_general(
        grads_full,
        lax.all_gather(weight, "row", axis=1, tiled=True),
        (((1,), (1,)), ((), ())),
        preferred_element_type=jnp.float32,
    )


def rows_backward(gradient, weight):
    partials = lax.dot_general(
        gradient,
        lax.all_gather(weight, "row", axis=0, tiled=True),
        (((1,), (1,)), ((), ())),
        preferred_element_type=jnp.float32,
    )
    return lax.psum_scatter(
        partials.astype(jnp.bfloat16), "col", scatter_dimension=1, tiled=True
    ).astype(jnp.float32)


def score_block(query_part, key_rows, first_row, prefix_end):
    scores = jnp.einsum(
        "qhd,khd->hqk", query_part, key_rows, preferred_element_type=jnp.float32
    ) * HDIM ** (-0.5)
    places = jnp.arange(key_rows.shape[0])
    row_ids = first_row + jnp.arange(query_part.shape[0])
    visible = (places[None, :] <= row_ids[:, None]) | (places[None, :] < prefix_end)
    return jnp.where(visible[None], scores, NEGATIVE)


def attend_forward(packed):
    queries, key_rows, value_rows, prefix_end = packed
    length = queries.shape[0]
    block_size = min(512, length)
    block_count = length // block_size
    query_blocks = queries.reshape(block_count, block_size, queries.shape[1], queries.shape[2])
    block_starts = jnp.arange(block_count) * block_size

    def one_block(inner):
        query_part, first_row = inner
        scores = score_block(query_part, key_rows, first_row, prefix_end)
        maximum = jnp.max(scores, axis=2, keepdims=True)
        weights = jnp.exp(scores - maximum)
        denominator = jnp.sum(weights, axis=2, keepdims=True)
        rounded = (weights / denominator).astype(jnp.bfloat16)
        mixed_rows = jnp.einsum(
            "hqk,khd->qhd", rounded, value_rows, preferred_element_type=jnp.float32
        )
        return (mixed_rows.astype(jnp.bfloat16), (maximum + jnp.log(denominator))[:, :, 0])

    attended, log_total = lax.map(one_block, (query_blocks, block_starts))
    return (attended.reshape(queries.shape), log_total)


def attend_backward(packed):
    queries, key_rows, value_rows, grad_rows, log_total, prefix_end = packed
    length = queries.shape[0]
    block_size = min(512, length)
    block_count = length // block_size
    query_blocks = queries.reshape(block_count, block_size, queries.shape[1], queries.shape[2])
    grad_blocks = grad_rows.reshape(query_blocks.shape)
    block_starts = jnp.arange(block_count) * block_size
    factor = HDIM ** (-0.5)

    def one_block(running, inner):
        key_grad, value_grad = running
        query_part, grad_part, total_part, first_row = inner
        scores = score_block(query_part, key_rows, first_row, prefix_end)
        weights = jnp.exp(scores - total_part[:, :, None])
        weight_grad = jnp.einsum(
            "qhd,khd->hqk", grad_part, value_rows, preferred_element_type=jnp.float32
        )
        score_grad = weights * (weight_grad - jnp.sum(weights * weight_grad, axis=2, keepdims=True))
        score_grad = score_grad.astype(jnp.bfloat16)
        query_grad = (
            jnp.einsum("hqk,khd->qhd", score_grad, key_rows, preferred_element_type=jnp.float32)
            * factor
        )
        key_grad = (
            key_grad
            + jnp.einsum("hqk,qhd->khd", score_grad, query_part, preferred_element_type=jnp.float32)
            * factor
        )
        value_grad = value_grad + jnp.einsum(
            "hqk,qhd->khd",
            weights.astype(jnp.bfloat16),
            grad_part,
            preferred_element_type=jnp.float32,
        )
        return ((key_grad, value_grad), query_grad)

    zeroes = jnp.zeros(key_rows.shape, jnp.float32)
    (key_grad, value_grad), query_grad = lax.scan(
        one_block, (zeroes, zeroes), (query_blocks, grad_blocks, log_total, block_starts)
    )
    return (query_grad.reshape(queries.shape), key_grad, value_grad)


def contract_rows(left_side, right_side):
    return lax.dot_general(
        left_side, right_side, (((0,), (0,)), ((), ())), preferred_element_type=jnp.float32
    )


def shards(
    tokens_in,
    cotangent,
    prefix_length,
    first_gain,
    first_shift,
    joint_weight,
    joint_bias,
    output_weight,
    output_bias,
    second_gain,
    second_shift,
    up_weight,
    up_bias,
    down_weight,
    down_bias,
):
    row_count = tokens_in.shape[0]
    sequences = row_count // LEN
    head_count = joint_bias.shape[0] // (2 * HDIM)
    inputs = tokens_in.astype(jnp.float32)
    normed_one, centered_one, factor_one = norm_forward(inputs, first_gain, first_shift)
    full_one = spread_features(normed_one.astype(jnp.bfloat16))
    projected = rows_forward(full_one, joint_weight).reshape(row_count, head_count, 3, HDIM)
    bias_rows = joint_bias.reshape(head_count, 2, HDIM)
    projected = projected + jnp.stack(
        [bias_rows[:, 0], jnp.zeros_like(bias_rows[:, 0]), bias_rows[:, 1]], axis=1
    )
    projected = projected.astype(jnp.bfloat16)
    seq_shape = (sequences, LEN, head_count, HDIM)
    queries = projected[:, :, 0].reshape(seq_shape)
    key_rows = projected[:, :, 1].reshape(seq_shape)
    value_rows = projected[:, :, 2].reshape(seq_shape)
    attended, log_total = lax.map(attend_forward, (queries, key_rows, value_rows, prefix_length))
    attended_flat = attended.reshape(row_count, head_count * HDIM)
    residual = inputs + (cols_forward(attended_flat, output_weight) + output_bias)
    normed_two, centered_two, factor_two = norm_forward(residual, second_gain, second_shift)
    full_two = spread_features(normed_two.astype(jnp.bfloat16))
    hidden = rows_forward(full_two, up_weight) + up_bias
    normal_cdf = 0.5 * (1.0 + jax.scipy.special.erf(hidden * 2.0 ** (-0.5)))
    active = (hidden * normal_cdf).astype(jnp.bfloat16)
    layer_out = (residual + (cols_forward(active, down_weight) + down_bias)).astype(jnp.bfloat16)
    out_grad = cotangent.astype(jnp.float32)
    grad_down_bias = jnp.sum(out_grad, axis=0)
    grads_ffn = spread_grads(cotangent)
    grad_down_weight = contract_rows(active, grads_ffn)
    active_grad = cols_backward(grads_ffn, down_weight)
    slope = normal_cdf + hidden * jnp.exp(-0.5 * hidden * hidden) * (1.0 / math.sqrt(2.0 * math.pi))
    hidden_grad = (active_grad * slope).astype(jnp.bfloat16)
    grad_up_bias = jnp.sum(hidden_grad.astype(jnp.float32), axis=0)
    grad_up_weight = contract_rows(full_two, hidden_grad)
    normed_two_grad = rows_backward(hidden_grad, up_weight)
    back_two, grad_second_gain, grad_second_shift = norm_backward(
        normed_two_grad, centered_two, factor_two, second_gain
    )
    residual_grad = out_grad + back_two
    branch_grad = residual_grad.astype(jnp.bfloat16)
    grad_output_bias = jnp.sum(branch_grad.astype(jnp.float32), axis=0)
    grads_attn = spread_grads(branch_grad)
    grad_output_weight = contract_rows(attended_flat, grads_attn)
    attended_grad = cols_backward(grads_attn, output_weight).astype(jnp.bfloat16).reshape(seq_shape)
    query_grad, key_grad, value_grad = lax.map(
        attend_backward, (queries, key_rows, value_rows, attended_grad, log_total, prefix_length)
    )
    projected_grad = jnp.stack([query_grad, key_grad, value_grad], axis=3).astype(jnp.bfloat16)
    projected_grad = projected_grad.reshape(row_count, head_count * 3 * HDIM)
    bias_parts = projected_grad.astype(jnp.float32).reshape(row_count, head_count, 3, HDIM)[
        :, :, 0::2
    ]
    grad_joint_bias = jnp.sum(bias_parts, axis=0).reshape(-1)
    grad_joint_weight = contract_rows(full_one, projected_grad)
    normed_one_grad = rows_backward(projected_grad, joint_weight)
    back_one, grad_first_gain, grad_first_shift = norm_backward(
        normed_one_grad, centered_one, factor_one, first_gain
    )
    tokens_grad = (residual_grad + back_one).astype(jnp.bfloat16)
    groups = lax.axis_size("dp")
    stripes = lax.axis_size("row")

    def reorder(matrix, axis_at):
        shape = matrix.shape
        split = (
            shape[:axis_at]
            + (stripes, groups, shape[axis_at] // (stripes * groups))
            + shape[axis_at + 1 :]
        )
        return jnp.swapaxes(matrix.reshape(split), axis_at, axis_at + 1).reshape(shape)

    stripes_sum = (
        lax.psum_scatter(
            reorder(grad_joint_weight, 0), ("dp", "row"), scatter_dimension=0, tiled=True
        ),
        lax.psum_scatter(
            reorder(grad_output_weight, 1), ("dp", "row"), scatter_dimension=1, tiled=True
        ),
        lax.psum_scatter(
            reorder(grad_up_weight, 0), ("dp", "row"), scatter_dimension=0, tiled=True
        ),
        lax.psum_scatter(
            reorder(grad_down_weight, 1), ("dp", "row"), scatter_dimension=1, tiled=True
        ),
    )
    summed = (
        lax.all_gather(stripes_sum[0].astype(jnp.bfloat16), "dp", axis=0, tiled=True).astype(
            jnp.float32
        ),
        lax.all_gather(stripes_sum[1].astype(jnp.bfloat16), "dp", axis=1, tiled=True).astype(
            jnp.float32
        ),
        lax.all_gather(stripes_sum[2].astype(jnp.bfloat16), "dp", axis=0, tiled=True).astype(
            jnp.float32
        ),
        lax.all_gather(stripes_sum[3].astype(jnp.bfloat16), "dp", axis=1, tiled=True).astype(
            jnp.float32
        ),
    )
    small = lax.psum(
        (
            grad_first_gain,
            grad_first_shift,
            grad_joint_bias,
            grad_output_bias,
            grad_second_gain,
            grad_second_shift,
            grad_up_bias,
            grad_down_bias,
        ),
        ("dp", "row"),
    )
    return (
        layer_out,
        tokens_grad,
        small[0],
        small[1],
        summed[0],
        small[2],
        summed[1],
        small[3],
        small[4],
        small[5],
        summed[2],
        small[6],
        summed[3],
        small[7],
    )


def solution(mesh):
    return jax.shard_map(
        shards,
        mesh=mesh,
        in_specs=(
            P(("dp", "row"), "col"),
            P(("dp", "row"), "col"),
            P(("dp", "row")),
            P("col"),
            P("col"),
            P("row", "col"),
            P("col"),
            P("col", "row"),
            P("col"),
            P("col"),
            P("col"),
            P("row", "col"),
            P("col"),
            P("col", "row"),
            P("col"),
        ),
        out_specs=(
            P(("dp", "row"), "col"),
            P(("dp", "row"), "col"),
            P("col"),
            P("col"),
            P("row", "col"),
            P("col"),
            P("col", "row"),
            P("col"),
            P("col"),
            P("col"),
            P("row", "col"),
            P("col"),
            P("col", "row"),
            P("col"),
        ),
        check_vma=False,
    )
```

profile of v0, /device:TPU:0, one launch (start us, length us, event | category | flops | bytes accessed | tf_op | source)
XLA Modules:
  0.0 1080.1 jit_solution(9593470863402023250)
XLA Ops:
  16.5 11.6 %all-gather.11.cloned.1.call-done = bf16[1024,1024]{1,0:T(8,128)(2,1)} async-done(((bf16[1024,512]{1,0:T(8,128)(2,1)}), bf16[1024,1024]{1,0:T(8,128)(2,1)}) %all-gather.11.cloned.1.call-update) | async-done | bytes 2097168 | tf_op jit(solution)/shard_map/all_gather | solution.py:38
  28.1 66.3 %all-gather.13.cloned.1.call-done = bf16[1024,1536]{1,0:T(8,128)(2,1)} async-done(((bf16[256,1536]{1,0:T(8,128)(2,1)}), bf16[1024,1536]{1,0:T(8,128)(2,1)}) %all-gather.13.cloned.1.call-update) | async-done | bytes 3145744 | tf_op jit(solution)/shard_map/all_gather | solution.py:48
  94.3 6.2 fusion.68
  104.0 22.4 %while.47 = (s32[]{:T(128)}, bf16[2,512,4,128]{3,2,1,0:T(4,128)(2,1)}, f32[2,4,512]{2,1,0:T(4,128)S(1)}, s32[2]{0:T(128)S(1)}, s32[]{:T(128)}, /*index=5*/bf16[2...) while((s32[]{:T(128)}, ...), condition=%wide.region_7.8_spmd, body=%wide.region_4.7_spmd.sunk | while | flops 1100217856 | bytes 44112088 | solution.py:115
  126.4 4.5 convolution_convert_fusion.3
  131.6 7.8 reduce-scatter.9.cloned.1.call-done
  148.5 74.3 %all-gather.19.cloned.1.call-done = bf16[1024,2048]{1,0:T(8,128)(2,1)} async-done(((bf16[256,2048]{1,0:T(8,128)(2,1)}), bf16[1024,2048]{1,0:T(8,128)(2,1)}) %all-gather.19.cloned.1.call-update) | async-done | bytes 4194320 | tf_op jit(solution)/shard_map/all_gather | solution.py:48
  222.8 11.2 %all-gather.17.cloned.1.call-done = bf16[1024,1024]{1,0:T(8,128)(2,1)} async-done(((bf16[1024,512]{1,0:T(8,128)(2,1)}), bf16[1024,1024]{1,0:T(8,128)(2,1)}) %all-gather.17.cloned.1.call-update) | async-done | bytes 2097168 | tf_op jit(solution)/shard_map/all_gather | solution.py:38
  234.0 10.2 multiply_convert_fusion.1
  247.4 83.4 %all-gather.21.cloned.1.call-done = bf16[2048,1024]{1,0:T(8,128)(2,1)} async-done(((bf16[2048,256]{1,0:T(8,128)(2,1)}), bf16[2048,1024]{1,0:T(8,128)(2,1)}) %all-gather.21.cloned.1.call-update) | async-done | bytes 4194320 | tf_op jit(solution)/shard_map/all_gather | solution.py:56
  330.8 11.5 %convert_reduce_fusion = (f32[2048]{0:T(1024)}, bf16[1024,2048]{1,0:T(8,128)(2,1)S(1)}) fusion(f32[1024,2048]{1,0:T(8,128)} %get-tuple-element.403, f32[2048]{0:T(1024)S(1)} %copy-done.33, bf16[1024,1024]{1,0:T(8,128)(2,1)} %all-gather.23.cloned.1.call-done, bf16[2048,1024]{1,0:T(8,128)(2,1)} %all-gather.21.cloned.1.call-done), kind=kOutput, calls=%fused_computation.58 | convolution fusion | flops 4322228224 | bytes 18890752 | tf_op jit(solution)/shard_map/dot_general | solution.py:65
  344.2 5.7 convolution_convert_fusion.1
  350.0 9.3 convolution_convert_fusion.2
  365.4 5.9 reduce-scatter.11.cloned.1.call-done
  371.4 4.9 convert_reduce_fusion.6
  376.3 7.2 fusion.70
  383.5 4.0 copy.111
  389.1 6.5 fusion.69
  401.8 4.1 convolution_convert_fusion.4
  408.1 3.9 copy.108
  416.9 38.1 %while.48 = (s32[]{:T(128)}, f32[1024,4,128]{0,2,1:T(8,128)S(1)}, f32[1024,4,128]{0,2,1:T(8,128)}, bf16[2,512,4,128]{3,1,0,2:T(8,128)(2,1)}, bf16[2,512,4,128]{3...) while((s32[]{:T(128)}, f32[1024,4,128]{0,2,1:T(8,128)S(1)}, ...), condition=%wide.region_21.22_spmd.clone, body=%wide.region_19.21_spmd.clone.sunk | while | flops 2719743488 | bytes 97581352 | solution.py:157
  441.3 5.1 bitcast_add_fusion.5
  464.4 7.7 convolution_convert_fusion
  472.1 101.8 %reduce-scatter.23.cloned.1.call-done = f32[2048,64]{0,1:T(8,128)} async-done(((f32[2048,1024]{0,1:T(8,128)}), f32[2048,64]{0,1:T(8,128)}) %reduce-scatter.23.cloned.1.call-update) | async-done | bytes 524304 | tf_op jit(solution)/shard_map/reduce_scatter | solution.py:267
  575.8 180.4 %reduce-scatter.21.cloned.1.call-done = f32[64,2048]{1,0:T(8,128)} async-done(((f32[1024,2048]{1,0:T(8,128)}), f32[64,2048]{1,0:T(8,128)}) %reduce-scatter.21.cloned.1.call-update) | async-done | bytes 524304 | tf_op jit(solution)/shard_map/reduce_scatter | solution.py:264
  758.0 4.0 copy.104
  762.0 5.0 convolution_bitcast_fusion
  772.8 67.8 %reduce-scatter.19.cloned.1.call-done = f32[512,64]{0,1:T(8,128)} async-done(((f32[512,1024]{0,1:T(8,128)}), f32[512,64]{0,1:T(8,128)}) %reduce-scatter.19.cloned.1.call-update) | async-done | bytes 131088 | tf_op jit(solution)/shard_map/reduce_scatter | solution.py:261
  841.4 7.5 all_gather.49
  852.4 77.4 %all-reduce = (f32[512]{0:T(512)}, f32[512]{0:T(512)}, f32[1024]{0:T(1024)}, f32[512]{0:T(512)}, f32[512]{0:T(512)}, /*index=5*/f32[512]{0:T(512)}, f32[2048]{0:T(1024)}, f32[512]{0:T(512)}) all-reduce(f32[512]{0:T(512)S(1)} %get-tuple-element.320, ...), channel_id=1, replica_groups=mesh['dp'=4,'row'=4,'col'=2] {'dp','row'}, use_global_device_ids=true, to_apply=%region_28.29 | all-reduce | flops 6144 | bytes 49152 | tf_op jit(solution)/shard_map/psum | solution.py:285
  940.4 118.4 %reduce-scatter.17.cloned.1.call-done = f32[64,1536]{1,0:T(8,128)} async-done(((f32[1024,1536]{1,0:T(8,128)}), f32[64,1536]{1,0:T(8,128)}) %reduce-scatter.17.cloned.1.call-update) | async-done | bytes 393232 | tf_op jit(solution)/shard_map/reduce_scatter | solution.py:258
  1059.9 11.6 %all_gather.48 = bf16[256,1536]{1,0:T(8,128)(2,1)S(1)} all-gather(bf16[64,1536]{1,0:T(8,128)(2,1)S(1)} %convert_element_type.152), channel_id=1, replica_groups=mesh['dp'=4,'row'=4,'col'=2] {'dp'}, dimensions={0}, use_global_device_ids=true | all-gather | bytes 983040 | tf_op jit(solution)/shard_map/all_gather | solution.py:272
  (220 shorter events, 139.3 us)
Async XLA Ops:
  7.2 20.9 %all-gather.11.cloned.1.call-start = ((), (), s32[]{:S(2)}) async-start(), calls=%async_computation.8 | async-start | bytes 3145728 | tf_op jit(solution)/shard_map/all_gather | solution.py:38
  14.7 79.6 %all-gather.13.cloned.1.call-start = ((), (), s32[]{:S(2)}) async-start(), calls=%async_computation.9 | async-start | bytes 3932160 | tf_op jit(solution)/shard_map/all_gather | solution.py:48
  15.5 110.9 %all-gather.15.cloned.1.call-start = ((), (), s32[]{:S(2)}) async-start(), calls=%async_computation.10 | async-start | bytes 1310720 | tf_op jit(solution)/shard_map/all_gather | solution.py:56
  16.2 123.1 %reduce-scatter.9.cloned.1.call-start = ((), (), s32[]{:S(2)}) async-start(), calls=%async_computation.11 | async-start | bytes 3145728 | tf_op jit(solution)/shard_map/reduce_scatter | solution.py:59
  130.9 13.2 %copy-start.30 = (f32[512]{0:T(512)S(1)}, f32[512]{0:T(512)}, u32[]{:S(2)}) copy-start(f32[512]{0:T(512)} %param.29) | copy-start | bytes 6148
  130.9 91.9 %all-gather.19.cloned.1.call-start = ((), (), s32[]{:S(2)}) async-start(), calls=%async_computation.13 | async-start | bytes 5242880 | tf_op jit(solution)/shard_map/all_gather | solution.py:48
  131.5 102.5 %all-gather.17.cloned.1.call-start = ((), (), s32[]{:S(2)}) async-start(), calls=%async_computation.12 | async-start | bytes 3145728 | tf_op jit(solution)/shard_map/all_gather | solution.py:38
  144.1 89.9 %copy-start.33 = (f32[2048]{0:T(1024)S(1)}, f32[2048]{0:T(1024)}, u32[]{:S(2)}) copy-start(f32[2048]{0:T(1024)} %param.31) | copy-start | bytes 24580
  146.9 100.5 %all-gather.23.cloned.1.call-start = ((), (), s32[]{:S(2)}) async-start(), calls=%async_computation.16 | async-start | bytes 3145728 | tf_op jit(solution)/shard_map/all_gather | solution.py:42
  147.7 183.1 %all-gather.21.cloned.1.call-start = ((), (), s32[]{:S(2)}) async-start(), calls=%async_computation.14 | async-start | bytes 5242880 | tf_op jit(solution)/shard_map/all_gather | solution.py:56
  148.4 211.2 %reduce-scatter.13.cloned.1.call-start = ((), (), s32[]{:S(2)}) async-start(), calls=%async_computation.17 | async-start | bytes 3145728 | tf_op jit(solution)/shard_map/reduce_scatter | solution.py:80
  330.8 13.4 %copy-start.31 = (bf16[1024,2048]{1,0:T(8,128)(2,1)S(1)}, bf16[1024,2048]{1,0:T(8,128)(2,1)}, u32[]{:S(2)}) copy-start(bf16[1024,2048]{1,0:T(8,128)(2,1)} %all-gather.19.cloned.1.call-done) | copy-start | bytes 12582916
  350.0 21.4 %reduce-scatter.11.cloned.1.call-start = ((), (), s32[]{:S(2)}) async-start(), calls=%async_computation.15 | async-start | bytes 3145728 | tf_op jit(solution)/shard_map/reduce_scatter | solution.py:59
  359.4 42.4 %all-gather.25.cloned.1.call-start = ((), (), s32[]{:S(2)}) async-start(), calls=%async_computation.18 | async-start | bytes 3145728 | tf_op jit(solution)/shard_map/all_gather | solution.py:42
  376.3 197.7 %reduce-scatter.23.cloned.1.call-start = ((), (), s32[]{:S(2)}) async-start(), calls=%async_computation.24 | async-start | bytes 8912896 | tf_op jit(solution)/shard_map/reduce_scatter | solution.py:267
  387.6 368.6 %reduce-scatter.21.cloned.1.call-start = ((), (), s32[]{:S(2)}) async-start(), calls=%async_computation.22 | async-start | bytes 8912896 | tf_op jit(solution)/shard_map/reduce_scatter | solution.py:264
  399.4 441.1 %reduce-scatter.19.cloned.1.call-start = ((), (), s32[]{:S(2)}) async-start(), calls=%async_computation.21 | async-start | bytes 2228224 | tf_op jit(solution)/shard_map/reduce_scatter | solution.py:261
  416.7 433.2 %reduce-scatter.15.cloned.1.call-start = ((), (), s32[]{:S(2)}) async-start(), calls=%async_computation.19 | async-start | bytes 3145728 | tf_op jit(solution)/shard_map/reduce_scatter | solution.py:80
  472.1 289.9 %copy-start.13 = (bf16[1,1024,4,3,128]{1,4,3,2,0:T(8,128)(2,1)S(1)}, bf16[1,1024,4,3,128]{1,4,3,2,0:T(8,128)(2,1)}, u32[]{:S(2)}) copy-start(bf16[1,1024,4,3,128]{1,4,3,2,0:T(8,128)(2,1)} %copy.103) | copy-start | bytes 9437188
  472.1 463.0 %all-gather.29.cloned.1.call-start = ((), (), s32[]{:S(2)}) async-start(), calls=%async_computation.25 | async-start | bytes 1310720 | tf_op jit(solution)/shard_map/all_gather | solution.py:281
  575.7 361.9 %all-gather.27.cloned.1.call-start = ((), (), s32[]{:S(2)}) async-start(), calls=%async_computation.23 | async-start | bytes 1310720 | tf_op jit(solution)/shard_map/all_gather | solution.py:278
  758.0 300.8 %reduce-scatter.17.cloned.1.call-start = ((), (), s32[]{:S(2)}) async-start(), calls=%async_computation.20 | async-start | bytes 6684672 | tf_op jit(solution)/shard_map/reduce_scatter | solution.py:258
  772.4 77.5 %copy-start.3 = (bf16[1024,512]{1,0:T(8,128)(2,1)S(1)}, bf16[1024,512]{1,0:T(8,128)(2,1)}, u32[]{:S(2)}) copy-start(bf16[1024,512]{1,0:T(8,128)(2,1)} %param.19) | copy-start | bytes 3145732
  772.4 77.5 %copy-start.17 = (f32[1024]{0:T(1024)S(1)}, f32[1024]{0:T(1024)}, u32[]{:S(2)}) copy-start(f32[1024]{0:T(1024)} %copy-done.16) | copy-start | bytes 12292
  772.4 77.5 %copy-start.19 = (f32[1024]{0:T(1024)S(1)}, f32[1024]{0:T(1024)}, u32[]{:S(2)}) copy-start(f32[1024]{0:T(1024)} %copy-done.18) | copy-start | bytes 12292
  772.4 77.5 %copy-start.22 = (f32[512]{0:T(512)S(1)}, f32[512]{0:T(512)}, u32[]{:S(2)}) copy-start(f32[512]{0:T(512)} %param.22) | copy-start | bytes 6148
  772.4 80.0 %copy-start.23 = (f32[512]{0:T(512)S(1)}, f32[512]{0:T(512)}, u32[]{:S(2)}) copy-start(f32[512]{0:T(512)} %get-tuple-element.318) | copy-start | bytes 6148
  772.4 80.0 %copy-start.24 = (f32[512]{0:T(512)S(1)}, f32[512]{0:T(512)}, u32[]{:S(2)}) copy-start(f32[512]{0:T(512)} %get-tuple-element.326) | copy-start | bytes 6148
  772.4 80.0 %copy-start.25 = (f32[512]{0:T(512)S(1)}, f32[512]{0:T(512)}, u32[]{:S(2)}) copy-start(f32[512]{0:T(512)} %get-tuple-element.384) | copy-start | bytes 6148
  772.4 80.0 %copy-start.26 = (f32[512]{0:T(512)S(1)}, f32[512]{0:T(512)}, u32[]{:S(2)}) copy-start(f32[512]{0:T(512)} %get-tuple-element.395) | copy-start | bytes 6148
  772.4 80.0 %copy-start.27 = (f32[2048]{0:T(1024)S(1)}, f32[2048]{0:T(1024)}, u32[]{:S(2)}) copy-start(f32[2048]{0:T(1024)} %get-tuple-element.404) | copy-start | bytes 24580
  772.5 159.9 %copy-start.9 = (f32[1024,512]{1,0:T(8,128)S(1)}, f32[1024,512]{1,0:T(8,128)}, u32[]{:S(2)}) copy-start(f32[1024,512]{1,0:T(8,128)} %get-tuple-element.386) | copy-start | bytes 6291460
  (28 other events, 107.5 us)
Sparse Core Ops, SparseCore 0:
  14.9 13.1 all-gather.10
  29.6 64.6 all-gather.12
  95.9 28.8 all-gather.14
  131.0 8.2 reduce-scatter.8
  140.8 81.9 all-gather.18
  224.9 9.0 all-gather.16
  235.6 11.7 all-gather.22
  249.0 81.7 all-gather.20
  350.1 7.7 reduce-scatter.12
  360.6 10.7 reduce-scatter.10
  376.4 11.7 all-gather.24
  390.4 183.4 reduce-scatter.22
  576.3 179.8 reduce-scatter.20
  758.4 82.0 reduce-scatter.18
  843.3 6.0 reduce-scatter.14
  851.1 27.9 all-gather.28
  880.9 26.7 all-gather.26
  912.8 146.0 reduce-scatter.16
where the time goes:
time: 1090 us; the launch traced here: 1080 us
  waiting for transfers between devices  736 us (68%)
  matrix products  117 us (11%)
  blocking collectives  107 us (10%)
  local copies, waits for them, and re-layouts  52.1 us (5%)
  other arithmetic  51.7 us (5%)
  between operations  15.2 us (1%)
    reduce_scatter x1, waiting for transfers between devices, shards(): lax.psum_scatter(reorder(grad_up_weight, 0), ('dp', 'row'), scatter_dimen...  180 us
    all_gather x2, waiting for transfers between devices, rows_forward(): lax.all_gather(weight, 'row', axis=0, tiled=True)  141 us
    reduce_scatter x1, waiting for transfers between devices, shards(): lax.psum_scatter(reorder(grad_joint_weight, 0), ('dp', 'row'), scatter_di...  118 us
    reduce_scatter x1, waiting for transfers between devices, shards(): lax.psum_scatter(reorder(grad_down_weight, 1), ('dp', 'row'), scatter_dim...  102 us
    all_gather x2, waiting for transfers between devices, cols_forward(): lax.all_gather(weight, 'row', axis=1, tiled=True)  83.4 us
    psum x1, blocking collectives, shards(): lax.psum((grad_first_gain, grad_first_shift, grad_joint_bias, grad_output...  77.4 us
    reduce_scatter x1, waiting for transfers between devices, shards(): lax.psum_scatter(reorder(grad_output_weight, 1), ('dp', 'row'), scatter_d...  67.8 us
    all_gather x2, waiting for transfers between devices, spread_features(): return lax.all_gather(normed, 'col', axis=1, tiled=True)  22.8 us
  transfers between devices with their start and end apart: 18, of which 12 were waited for; matrix products, arithmetic and copies ran while one was open for 17% of the time, Pallas kernels for 0%

commit v1 on v0

v1 whole, which is shorter than its diff:
```python
import math

import jax
import jax.numpy as jnp
from jax import lax
from jax.experimental import pallas as pl
from jax.experimental.pallas import tpu as pltpu
from jax.sharding import PartitionSpec as P

D = 1024
HALF = 512
HDIM = 128
LEN = 1024
MAX_PREFIX = 512
EPSILON = 1e-05
NEGATIVE = -1e30
LOG2E = math.log2(math.e)
SCALE = HDIM**-0.5
TILE = 256

BF = jnp.bfloat16
F32 = jnp.float32
NT = (((1,), (1,)), ((), ()))
TN = (((0,), (0,)), ((), ()))


def vmem():
    return pl.BlockSpec(memory_space=pltpu.VMEM)


def smem():
    return pl.BlockSpec(memory_space=pltpu.SMEM)


def anywhere():
    return pl.BlockSpec(memory_space=pl.ANY)


def params(mib=60):
    return pltpu.CompilerParams(vmem_limit_bytes=mib << 20)


def shape(dims, kind=BF):
    return jax.ShapeDtypeStruct(tuple(dims), kind)


def dot(left, right, dims=(((1,), (0,)), ((), ()))):
    return lax.dot_general(left, right, dims, preferred_element_type=F32)


class Layout:
    def __init__(self, mesh):
        self.R = mesh.shape["row"]
        self.Q = mesh.shape["dp"]
        self.block = D // self.R
        s = self.Q
        while self.block // s < 16:
            s //= 2
        self.s = s
        self.piece = self.block // s
        bits = self.Q.bit_length() - 1
        low = [1 << b for b in range(bits // 2)]
        high = [1 << b for b in range(bits // 2, bits)]
        mixed = []
        while low or high:
            if low:
                mixed.append(low.pop(0))
            if high:
                mixed.append(high.pop(0))
        k = s.bit_length() - 1
        self.split_bits = mixed[:k]
        self.rest_bits = mixed[k:]
        self.order_a = list(range(k))
        self.order_b = [1, 0] + list(range(2, k)) if k >= 2 else list(range(k))
        self.row_bits = [1 << b for b in range(self.R.bit_length() - 1)]


def swap(value, axis, size, bit):
    return lax.ppermute(value, axis, [(i, i ^ bit) for i in range(size)])


def swap_cores(value):
    return lax.ppermute(value, "col", [(0, 1), (1, 0)])


def device_ids(lay):
    z = lax.axis_index("row")
    d = lax.axis_index("dp")
    c = lax.axis_index("col")
    q = sum(((d // bit) % 2) << i for i, bit in enumerate(lay.split_bits))
    return jnp.stack([z ^ (c * (lay.R // 2)), q, c]).astype(jnp.int32)


def gather_row(lay, quarter):
    held = quarter[None]
    offsets = [0]
    for bit in reversed(lay.row_bits):
        got = swap(held, "row", lay.R, bit)
        held = jnp.concatenate([held, got], axis=0)
        offsets = offsets + [o ^ bit for o in offsets]
    return held[1:], offsets[1:]


def gather_dp(lay, part, order):
    held = part[None]
    offsets = [0]
    got, got_offsets = None, []
    for i in order:
        if got is not None:
            held = jnp.concatenate([held, got], axis=0)
            offsets = offsets + got_offsets
        got = swap(held, "dp", lay.Q, lay.split_bits[i])
        got_offsets = [o ^ (1 << i) for o in offsets]
    return (held, got), (offsets, got_offsets)


def gather_weight(lay, quarter, axis):
    others, z_offsets = gather_row(lay, quarter)
    middle = others.shape[axis] // 2
    left = lax.slice_in_dim(others, 0, middle, axis=axis)
    right = lax.slice_in_dim(others, middle, 2 * middle, axis=axis)
    (a0, a1), (qa0, qa1) = gather_dp(lay, left, lay.order_a)
    (b0, b1), (qb0, qb1) = gather_dp(lay, right, lay.order_b)
    return (a0, a1, b0, b1), (qa0, qa1, qb0, qb1), z_offsets


def piece_copies(lay, ids, refs, offsets, z_offsets, place):
    pairs = []
    for which, (ref, q_offsets) in enumerate(zip(refs, offsets)):
        for i, qo in enumerate(q_offsets):
            for k, zo in enumerate(z_offsets):
                q = ids[1] ^ qo
                z = ids[0] ^ zo
                pairs.extend(place(ref.at[i, k], which // 2, q, z))
    return pairs


def start_copies(pairs, sems):
    copies = [pltpu.make_async_copy(a, b, sems.at[i]) for i, (a, b) in enumerate(pairs)]
    for copy in copies:
        copy.start()
    return copies


def wait_copies(copies):
    for copy in copies:
        copy.wait()


def aligned(value, multiple):
    return pl.multiple_of(value * multiple, multiple)


def split_store(lay, ids, block, z, refs, first_a, first_b):
    keep_a, send_a, keep_b, send_b = refs
    half = block.shape[1] // 2
    for q in range(lay.s):
        rows = block[q * lay.piece : (q + 1) * lay.piece].astype(BF)
        for keep, send, bit, part in (
            (keep_a, send_a, first_a, rows[:, :half]),
            (keep_b, send_b, first_b, rows[:, half:]),
        ):
            mine = ((ids[1] >> bit) & 1) == ((q >> bit) & 1)
            spot = z * (lay.s // 2) + ((q >> (bit + 1)) << bit) + (q & ((1 << bit) - 1))

            def to_keep(keep=keep, spot=spot, part=part):
                keep[spot] = part

            def to_send(send=send, spot=spot, part=part):
                send[spot] = part

            pl.when(mine)(to_keep)
            pl.when(jnp.logical_not(mine))(to_send)


def grad_shapes(lay, columns):
    return [shape((lay.R * lay.s // 2, lay.piece, columns // 2))] * 4


def add_split(ids_bits, groups):
    flat = [a for group in groups for pair in group for a in pair]
    outs = []
    for group in groups:
        g, _, m, _ = group[0][0].shape
        columns = sum(pair[0].shape[3] for pair in group)
        outs += [shape((g, m, columns))] * 2

    def kernel(bits, *refs):
        ins, results = refs[: len(flat)], refs[len(flat) :]
        at = 0
        for n, group in enumerate(groups):
            mine = bits[n]
            keep, send = results[2 * n], results[2 * n + 1]
            column = 0
            for _ in group:
                a, b = ins[at], ins[at + 1]
                at += 2
                width = a.shape[3]
                for g in range(a.shape[0]):
                    for target, bit in ((send, 1 - mine), (keep, mine)):
                        total = a[g, bit].astype(F32) + b[g, bit].astype(F32)
                        target[g, :, column : column + width] = total.astype(BF)
                column += width

    return pl.pallas_call(
        kernel,
        in_specs=[smem()] + [vmem()] * len(flat),
        out_specs=[vmem()] * len(outs),
        out_shape=outs,
        compiler_params=params(32),
        name="add_split",
    )(ids_bits, *flat)


def reduce_group(lay, ids, parts):
    keep_a, send_a, keep_b, send_b = parts
    k = len(lay.split_bits)
    left_a = sorted(set(range(k)) - {lay.order_a[0]}, reverse=True)
    left_b = sorted(set(range(k)) - {lay.order_b[0]}, reverse=True)
    half = keep_a.shape[2]
    for step in range(1, k + 1):
        got_a = swap(send_a, "dp", lay.Q, lay.split_bits[lay.order_a[step - 1]])
        got_b = swap(send_b, "dp", lay.Q, lay.split_bits[lay.order_b[step - 1]])
        if step == k:
            break

        def view(value, left, bit):
            before = lay.R * 2 ** left.index(bit)
            after = 2 ** (len(left) - 1 - left.index(bit))
            return value.reshape(before, 2, after * lay.piece, half)

        bit_a, bit_b = lay.order_a[step], lay.order_b[step]
        keep_a, send_a, keep_b, send_b = add_split(
            jnp.stack([(ids[1] >> bit_a) & 1, (ids[1] >> bit_b) & 1]),
            [
                [(view(keep_a, left_a, bit_a), view(got_a, left_a, bit_a))],
                [(view(keep_b, left_b, bit_b), view(got_b, left_b, bit_b))],
            ],
        )
        left_a = [b for b in left_a if b != bit_a]
        left_b = [b for b in left_b if b != bit_b]
    pairs = [(keep_a, got_a), (keep_b, got_b)]
    rows = lay.R
    for i, bit in enumerate(lay.row_bits):
        keep, send = add_split(
            ((ids[0] >> i) & 1)[None],
            [[tuple(v.reshape(rows // 2, 2, lay.piece, v.shape[-1]) for v in pair) for pair in pairs]],
        )
        pairs = [(keep, swap(send, "row", lay.R, bit))]
        rows //= 2
    total = pairs[0][0].astype(F32) + pairs[0][1].astype(F32)
    total = total.reshape(lay.piece, -1)
    for bit in lay.rest_bits:
        total = total + swap(total.astype(BF), "dp", lay.Q, bit).astype(F32)
    return total.astype(BF)


def spread_group(lay, total):
    held, offsets = total[None], [0]
    for i in lay.order_a:
        got = swap(held, "dp", lay.Q, lay.split_bits[i])
        held = jnp.concatenate([held, got], axis=0)
        offsets = offsets + [o ^ (1 << i) for o in offsets]
    return held, offsets


def finish_group(lay, ids, held, offsets, plan):
    outs = [shape((n, lay.block) if t else (lay.block, n), F32) for _, n, t in plan]
    columns = held.shape[2]

    def kernel(ids, held_ref, *refs):
        results, scratch = refs[:-1], refs[-1]
        for i, offset in enumerate(offsets):
            at = aligned(ids[1] ^ offset, lay.piece)
            scratch[pl.ds(at, lay.piece), :] = held_ref[i].astype(F32)
        for result, (first, n, transposed) in zip(results, plan):
            value = scratch[:, first : first + n]
            result[...] = value.T if transposed else value

    return pl.pallas_call(
        kernel,
        in_specs=[smem(), vmem()],
        out_specs=[vmem()] * len(outs),
        out_shape=outs,
        scratch_shapes=[pltpu.VMEM((lay.block, columns), F32)],
        compiler_params=params(32),
        name="finish_group",
    )(ids, held)


def both(own, other):
    return jnp.concatenate([own, other], axis=1)


def row_stats(values):
    average = jnp.mean(values, axis=1, keepdims=True)
    square = jnp.mean(values * values, axis=1, keepdims=True)
    return average, lax.rsqrt(square - average * average + EPSILON)


def norm_grad(gradient, centered, factor, gain):
    scaled = gradient * gain
    first = jnp.mean(scaled, axis=1, keepdims=True)
    second = jnp.mean(scaled * centered, axis=1, keepdims=True)
    return factor * (scaled - first - centered * second)


def tiles():
    return [slice(i, i + TILE) for i in range(0, LEN, TILE)]


V_GAIN1, V_SHIFT1, V_GAIN2, V_SHIFT2, V_OBIAS = range(5)


def pair_row(own_ref, other_ref, i):
    return both(own_ref[i : i + 1, :], other_ref[i : i + 1, :])


def first_norm_project(lay, ids, x_own, x_other, vec_own, vec_other, bias, joint_block, output_block, gathered):
    refs_j, q_offsets, z_offsets = gathered
    width = joint_block.shape[1]
    o_rows = output_block.shape[0]
    block, piece = lay.block, lay.piece
    half = refs_j[0].shape[3]

    def place(source, which, q, z):
        row = aligned(z * lay.s + q, piece)
        if which == 0:
            return [(source, ("j", row, 0, half))]
        out = [(source.at[:, : width - half], ("j", row, half, width - half))]
        per = o_rows // lay.s
        for b in range(per // piece):
            first = width - half + b * block
            out.append((source.at[:, first : first + block], ("o", q * per + b * piece, z * block, block)))
        return out

    def kernel(ids, xo, xt, vo, vt, bias, jb, ob, a0, a1, b0, b1, full, qkv, j_full, o_full, sems):
        def target(t):
            kind, row, col, n = t
            if kind == "j":
                return j_full.at[pl.ds(row, piece), col : col + n]
            return o_full.at[pl.ds(pl.multiple_of(row, piece), piece), pl.ds(pl.multiple_of(col, block), n)]

        pairs = [(a, target(t)) for a, t in piece_copies(lay, ids, (a0, a1, b0, b1), q_offsets, z_offsets, place)]
        pairs.append((jb, j_full.at[pl.ds(aligned(ids[0], block), block), :]))
        pairs.append((ob, o_full.at[:, pl.ds(aligned(ids[0], block), block)]))
        copies = start_copies(pairs, sems)
        gain = pair_row(vo, vt, V_GAIN1)
        shift = pair_row(vo, vt, V_SHIFT1)
        for t in tiles():
            x = both(xo[t, :], xt[t, :]).astype(F32)
            average, factor = row_stats(x)
            full[t, :] = ((x - average) * factor * gain + shift).astype(BF)
        wait_copies(copies)
        for t in tiles():
            qkv[t, :] = (dot(full[t, :], j_full[...]) + bias[...]).astype(BF)

    pieces_n = lay.s * (lay.R - 1)
    n_copies = 2 * pieces_n + pieces_n * (o_rows // lay.s // piece) + 2
    return pl.pallas_call(
        kernel,
        in_specs=[smem()] + [vmem()] * 5 + [anywhere()] * 6,
        out_specs=[vmem()] * 4,
        out_shape=[shape((LEN, D)), shape((LEN, width)), shape((D, width)), shape((o_rows, D))],
        scratch_shapes=[pltpu.SemaphoreType.DMA((n_copies,))],
        compiler_params=params(),
        name="first_norm_project",
    )(ids, x_own, x_other, vec_own, vec_other, bias, joint_block, output_block, *refs_j)


def visible_mask(lo, rows, queries, prefix):
    key_id = lax.broadcasted_iota(jnp.int32, (rows, queries), 0) + lo
    query_id = lax.broadcasted_iota(jnp.int32, (rows, queries), 1) + lo
    return (key_id <= query_id) | (key_id < prefix)


def attention_forward(prefix, qkv, heads):
    bq, per = 512, 2

    def kernel(prefix_ref, qkv_ref, out_ref, log_ref):
        prefix_end = prefix_ref[0]
        for h in range(per):
            base = h * 3 * HDIM
            keys = qkv_ref[:, base + HDIM : base + 2 * HDIM]
            values_t = qkv_ref[:, base + 2 * HDIM : base + 3 * HDIM].T
            for lo in range(0, LEN, bq):
                n = max(MAX_PREFIX, lo + bq)
                query = qkv_ref[lo : lo + bq, base : base + HDIM]
                scores = dot(keys[:n], query, NT)
                tail = jnp.where(visible_mask(lo, n - lo, bq, prefix_end), scores[lo:], NEGATIVE)
                scores = tail if lo == 0 else jnp.concatenate([scores[:lo], tail], axis=0)
                top = jnp.max(scores, axis=0, keepdims=True) * (SCALE * LOG2E)
                weights = jnp.exp2(scores * (SCALE * LOG2E) - top)
                total = jnp.sum(weights, axis=0, keepdims=True)
                mixed = dot(values_t[:, :n], weights.astype(BF)) * (1.0 / total)
                out_ref[lo : lo + bq, h * HDIM : (h + 1) * HDIM] = mixed.T.astype(BF)
                log_ref[h, :, lo : lo + bq] = top + jnp.log2(total)

    return pl.pallas_call(
        kernel,
        grid=(heads // per,),
        in_specs=[smem(), pl.BlockSpec((LEN, 3 * HDIM * per), lambda h: (0, h))],
        out_specs=[
            pl.BlockSpec((LEN, HDIM * per), lambda h: (0, h)),
            pl.BlockSpec((per, 1, LEN), lambda h: (h, 0, 0)),
        ],
        out_shape=[shape((LEN, HDIM * heads)), shape((heads, 1, LEN), F32)],
        compiler_params=params(),
        name="attention_forward",
    )(prefix, qkv)


def output_project(attended, o_full):
    def kernel(a_ref, o_ref, out_ref):
        for t in tiles():
            out_ref[t, :] = dot(a_ref[t, :], o_ref[...]).astype(BF)

    return pl.pallas_call(
        kernel,
        in_specs=[vmem()] * 2,
        out_specs=vmem(),
        out_shape=shape((LEN, D)),
        compiler_params=params(),
        name="output_project",
    )(attended, o_full)


def second_norm_up(lay, ids, x_own, x_other, part_own, part_other, vec_own, vec_other, bias, up_block, gathered):
    refs_u, q_offsets, z_offsets = gathered
    width = up_block.shape[1]
    piece, block = lay.piece, lay.block
    half = refs_u[0].shape[3]

    def place(source, which, q, z):
        return [(source, (aligned(z * lay.s + q, piece), which * half))]

    def kernel(ids, xo, xt, po, pt, vo, vt, bias, ub, a0, a1, b0, b1, residual, centered, factor_ref, full, active, slope, u_full, sems):
        pairs = [
            (a, u_full.at[pl.ds(row, piece), col : col + half])
            for a, (row, col) in piece_copies(lay, ids, (a0, a1, b0, b1), q_offsets, z_offsets, place)
        ]
        pairs.append((ub, u_full.at[pl.ds(aligned(ids[0], block), block), :]))
        copies = start_copies(pairs, sems)
        gain = pair_row(vo, vt, V_GAIN2)
        shift = pair_row(vo, vt, V_SHIFT2)
        out_bias = pair_row(vo, vt, V_OBIAS)
        for t in tiles():
            x = both(xo[t, :], xt[t, :]).astype(F32)
            branch = po[t, :].astype(F32) + both(pt[t, HALF:], pt[t, :HALF]).astype(F32)
            res = x + (branch + out_bias)
            residual[t, :] = res[:, :HALF]
            average, factor = row_stats(res)
            cent = (res - average) * factor
            centered[t, :] = cent.astype(BF)
            factor_ref[t, :] = factor
            full[t, :] = (cent * gain + shift).astype(BF)
        wait_copies(copies)
        for t in tiles():
            hidden = dot(full[t, :], u_full[...]) + bias[...]
            bell = jnp.exp(-0.5 * hidden * hidden) * (1.0 / math.sqrt(2.0 * math.pi))
            phi = 0.5 * (1.0 + lax.erf(hidden * 2.0**-0.5))
            active[t, :] = (hidden * phi).astype(BF)
            slope[t, :] = (phi + hidden * bell).astype(BF)

    n_copies = 2 * lay.s * (lay.R - 1) + 1
    return pl.pallas_call(
        kernel,
        in_specs=[smem()] + [vmem()] * 7 + [anywhere()] * 5,
        out_specs=[vmem()] * 7,
        out_shape=[
            shape((LEN, HALF), F32),
            shape((LEN, D)),
            shape((LEN, 1), F32),
            shape((LEN, D)),
            shape((LEN, width)),
            shape((LEN, width)),
            shape((D, width)),
        ],
        scratch_shapes=[pltpu.SemaphoreType.DMA((n_copies,))],
        compiler_params=params(),
        name="second_norm_up",
    )(ids, x_own, x_other, part_own, part_other, vec_own, vec_other, bias, up_block, *refs_u)


def weight_grad(lay, ids, sides, name):
    columns = sum(right.shape[1] for _, right in sides)
    flat = [ids]
    for left, right in sides:
        flat += list(left) + [right]
    lefts = [len(left) for left, _ in sides]
    first_a, first_b = lay.order_a[0], lay.order_b[0]

    def kernel(ids, *refs):
        ins, outs = refs[: len(flat) - 1], refs[len(flat) - 1 :]
        for z in range(lay.R):
            parts, at = [], 0
            for n in lefts:
                feature = z * lay.block
                ref = ins[at + (feature * n) // D]
                column = feature % (D // n)
                parts.append(dot(ref[:, column : column + lay.block], ins[at + n][...], TN))
                at += n + 1
            block = parts[0] if len(parts) == 1 else jnp.concatenate(parts, axis=1)
            split_store(lay, ids, block, z, outs, first_a, first_b)

    return pl.pallas_call(
        kernel,
        in_specs=[smem()] + [vmem()] * (len(flat) - 1),
        out_specs=[vmem()] * 4,
        out_shape=grad_shapes(lay, columns),
        compiler_params=params(),
        name=name,
    )(*flat)


def hidden_backward(lay, ids, cot_own, cot_other, slope, u_full, down_block, gathered):
    refs_d, q_offsets, z_offsets = gathered
    width = down_block.shape[0]
    block = lay.block
    rows = width // lay.s
    half = rows // 2

    def place(source, which, q, z):
        return [(source, (q * rows + which * half, z * block))]

    def kernel(ids, co, ct, slope_ref, u_full, db, a0, a1, b0, b1, hidden_grad, partial, bias_grad, d_full, sems):
        pairs = [
            (a, d_full.at[pl.ds(pl.multiple_of(row, half), half), pl.ds(pl.multiple_of(col, block), block)])
            for a, (row, col) in piece_copies(lay, ids, (a0, a1, b0, b1), q_offsets, z_offsets, place)
        ]
        pairs.append((db, d_full.at[:, pl.ds(aligned(ids[0], block), block)]))
        wait_copies(start_copies(pairs, sems))
        sums = jnp.zeros((1, width), F32)
        for t in tiles():
            grad = dot(both(co[t, :], ct[t, :]), d_full[...], NT) * slope_ref[t, :].astype(F32)
            low = grad.astype(BF)
            hidden_grad[t, :] = low
            sums = sums + jnp.sum(low.astype(F32), axis=0, keepdims=True)
            partial[t, :] = dot(low, u_full[...], NT).astype(BF)
        bias_grad[...] = sums

    n_copies = 2 * lay.s * (lay.R - 1) + 1
    return pl.pallas_call(
        kernel,
        in_specs=[smem()] + [vmem()] * 4 + [anywhere()] * 5,
        out_specs=[vmem()] * 4,
        out_shape=[shape((LEN, width)), shape((LEN, D)), shape((1, width), F32), shape((width, D))],
        scratch_shapes=[pltpu.SemaphoreType.DMA((n_copies,))],
        compiler_params=params(),
        name="hidden_backward",
    )(ids, cot_own, cot_other, slope, u_full, down_block, *refs_d)


def second_norm_backward(cot_own, cot_other, part_own, part_other, centered, factor, vec_own, vec_other, o_full):
    heads_width = o_full.shape[0]

    def kernel(co, ct, po, pt, cent_ref, factor_ref, vo, vt, o_ref, branch, res_grad, att_grad, sums_ref):
        gain = pair_row(vo, vt, V_GAIN2)
        sums = [jnp.zeros((1, HALF), F32)] * 4
        for t in tiles():
            grad = po[t, :].astype(F32) + both(pt[t, HALF:], pt[t, :HALF]).astype(F32)
            cent = cent_ref[t, :].astype(F32)
            cot = both(co[t, :], ct[t, :]).astype(F32)
            total = cot + norm_grad(grad, cent, factor_ref[t, :], gain)
            low = total.astype(BF)
            branch[t, :] = low
            res_grad[t, :] = total[:, :HALF]
            att_grad[t, :] = dot(low, o_ref[...], NT).astype(BF)
            news = (grad[:, :HALF] * cent[:, :HALF], grad[:, :HALF], low[:, :HALF].astype(F32), cot[:, :HALF])
            sums = [s + jnp.sum(v, axis=0, keepdims=True) for s, v in zip(sums, news)]
        for i in range(4):
            sums_ref[i : i + 1, :] = sums[i]

    return pl.pallas_call(
        kernel,
        in_specs=[vmem()] * 9,
        out_specs=[vmem()] * 4,
        out_shape=[shape((LEN, D)), shape((LEN, HALF), F32), shape((LEN, heads_width)), shape((4, HALF), F32)],
        compiler_params=params(),
        name="second_norm_backward",
    )(cot_own, cot_other, part_own, part_other, centered, factor, vec_own, vec_other, o_full)


def attention_backward(prefix, qkv, grads, logs, attended, heads):
    bq, per = 256, 1

    def kernel(prefix_ref, qkv_ref, grad_ref, log_ref, att_ref, out_ref, sums_ref, key_sum, value_sum):
        prefix_end = prefix_ref[0]
        keys = qkv_ref[:, HDIM : 2 * HDIM]
        values = qkv_ref[:, 2 * HDIM : 3 * HDIM]
        keys_t = keys.T
        query_total = jnp.zeros((1, HDIM), F32)
        for lo in reversed(range(0, LEN, bq)):
            n = max(MAX_PREFIX, lo + bq)
            query = qkv_ref[lo : lo + bq, 0:HDIM]
            grad = grad_ref[lo : lo + bq, :]
            scores = dot(keys[:n], query, NT) * (SCALE * LOG2E)
            weights = jnp.exp2(scores - log_ref[0, :, lo : lo + bq])
            tail = jnp.where(visible_mask(lo, n - lo, bq, prefix_end), weights[lo:], 0.0)
            weights = tail if lo == 0 else jnp.concatenate([weights[:lo], tail], axis=0)
            weight_grad_t = dot(values[:n], grad, NT)
            mixed = grad.astype(F32) * att_ref[lo : lo + bq, :].astype(F32)
            delta = jnp.sum(mixed.T, axis=0, keepdims=True)
            score_grad = (weights * (weight_grad_t - delta)).astype(BF)
            value_part = dot(weights.astype(BF), grad)
            key_part = dot(score_grad, query)
            if lo + bq == LEN:
                value_sum[...] = value_part
                key_sum[...] = key_part
            else:
                value_sum[:n, :] += value_part
                key_sum[:n, :] += key_part
            query_part = (dot(keys_t[:, :n], score_grad).T * SCALE).astype(BF)
            out_ref[lo : lo + bq, 0:HDIM] = query_part
            query_total = query_total + jnp.sum(query_part.astype(F32), axis=0, keepdims=True)
        out_ref[:, HDIM : 2 * HDIM] = (key_sum[...] * SCALE).astype(BF)
        value_low = value_sum[...].astype(BF)
        out_ref[:, 2 * HDIM : 3 * HDIM] = value_low
        sums_ref[0] = both(query_total, jnp.sum(value_low.astype(F32), axis=0, keepdims=True))

    return pl.pallas_call(
        kernel,
        grid=(heads,),
        in_specs=[
            smem(),
            pl.BlockSpec((LEN, 3 * HDIM), lambda h: (0, h)),
            pl.BlockSpec((LEN, HDIM), lambda h: (0, h)),
            pl.BlockSpec((1, 1, LEN), lambda h: (h, 0, 0)),
            pl.BlockSpec((LEN, HDIM), lambda h: (0, h)),
        ],
        out_specs=[
            pl.BlockSpec((LEN, 3 * HDIM), lambda h: (0, h)),
            pl.BlockSpec((1, 1, 2 * HDIM), lambda h: (h, 0, 0)),
        ],
        out_shape=[shape((LEN, 3 * HDIM * heads)), shape((heads, 1, 2 * HDIM), F32)],
        scratch_shapes=[pltpu.VMEM((LEN, HDIM), F32), pltpu.VMEM((LEN, HDIM), F32)],
        compiler_params=params(),
        name="attention_backward",
    )(prefix, qkv, grads, logs, attended)


def project_backward(grads, weight):
    def kernel(g_ref, w_ref, out_ref):
        for t in tiles():
            out_ref[t, :] = dot(g_ref[t, :], w_ref[...], NT).astype(BF)

    return pl.pallas_call(
        kernel,
        in_specs=[vmem()] * 2,
        out_specs=vmem(),
        out_shape=shape((LEN, D)),
        compiler_params=params(),
        name="project_backward",
    )(grads, weight)


def down_project(active, d_full):
    def kernel(a_ref, d_ref, own, other):
        for t in tiles():
            value = dot(a_ref[t, :], d_ref[...]).astype(BF)
            own[t, :] = value[:, :HALF]
            other[t, :] = value[:, HALF:]

    return pl.pallas_call(
        kernel,
        in_specs=[vmem()] * 2,
        out_specs=[vmem()] * 2,
        out_shape=[shape((LEN, HALF))] * 2,
        compiler_params=params(),
        name="down_project",
    )(active, d_full)


def first_norm_backward(x_own, x_other, part_own, part_other, vec_own, vec_other, res_grad):
    def kernel(xo, xt, po, pt, vo, vt, res_ref, out, sums_ref):
        gain = pair_row(vo, vt, V_GAIN1)
        sums = [jnp.zeros((1, HALF), F32)] * 2
        for t in tiles():
            x = both(xo[t, :], xt[t, :]).astype(F32)
            average, factor = row_stats(x)
            cent = (x - average) * factor
            grad = po[t, :].astype(F32) + both(pt[t, HALF:], pt[t, :HALF]).astype(F32)
            back = norm_grad(grad, cent, factor, gain)
            out[t, :] = (res_ref[t, :] + back[:, :HALF]).astype(BF)
            news = (grad[:, :HALF] * cent[:, :HALF], grad[:, :HALF])
            sums = [s + jnp.sum(v, axis=0, keepdims=True) for s, v in zip(sums, news)]
        for i in range(2):
            sums_ref[i : i + 1, :] = sums[i]

    return pl.pallas_call(
        kernel,
        in_specs=[vmem()] * 7,
        out_specs=[vmem()] * 2,
        out_shape=[shape((LEN, HALF)), shape((2, HALF), F32)],
        compiler_params=params(),
        name="first_norm_backward",
    )(x_own, x_other, part_own, part_other, vec_own, vec_other, res_grad)


def own_piece(lay, ids, block, pieces):
    rows = block.shape[0] // pieces
    return lax.dynamic_slice_in_dim(block, ids[1] * rows, rows, axis=0)


def layer(lay, tokens_in, cotangent, prefix_length, first_gain, first_shift, joint_weight, joint_bias,
          output_weight, output_bias, second_gain, second_shift, up_weight, up_bias, down_weight, down_bias):
    heads = joint_bias.shape[0] // (2 * HDIM)
    ids = device_ids(lay)

    x_own, x_other = tokens_in, swap_cores(tokens_in)
    zero_row = jnp.zeros_like(first_gain)
    vec_own = jnp.stack(
        [first_gain, first_shift, second_gain, second_shift, output_bias, zero_row, zero_row, zero_row]
    )
    vec_other = swap_cores(vec_own)

    output_piece = own_piece(lay, ids, output_weight, lay.s)
    output_piece = jnp.concatenate(
        [output_piece[i : i + lay.piece] for i in range(0, output_piece.shape[0], lay.piece)], axis=1
    )
    joint_out = gather_weight(
        lay, jnp.concatenate([own_piece(lay, ids, joint_weight, lay.s), output_piece], axis=1), 2
    )
    up_parts = gather_weight(lay, own_piece(lay, ids, up_weight, lay.s), 2)
    down_parts = gather_weight(lay, own_piece(lay, ids, down_weight, lay.s), 1)

    bias_rows = joint_bias.reshape(heads, 2, HDIM)
    joint_row = jnp.stack([bias_rows[:, 0], jnp.zeros_like(bias_rows[:, 0]), bias_rows[:, 1]], axis=1)
    full_one, qkv, j_full, o_full = first_norm_project(
        lay, ids, x_own, x_other, vec_own, vec_other, joint_row.reshape(1, -1), joint_weight, output_weight, joint_out
    )
    attended, logs = attention_forward(prefix_length, qkv, heads)
    branch_own = output_project(attended, o_full)
    branch_other = swap_cores(branch_own)
    residual, centered, factor, full_two, active, slope, u_full = second_norm_up(
        lay, ids, x_own, x_other, branch_own, branch_other, vec_own, vec_other,
        up_bias.reshape(1, -1), up_weight, up_parts,
    )
    cot_own, cot_other = cotangent, swap_cores(cotangent)
    down_grads = weight_grad(lay, ids, [((cot_own, cot_other), active)], "down_grad")
    down_total = reduce_group(lay, ids, down_grads)
    hidden_grad, norm_part, up_bias_grad, d_full = hidden_backward(
        lay, ids, cot_own, cot_other, slope, u_full, down_weight, down_parts
    )
    norm_other = swap_cores(norm_part)
    up_grads = weight_grad(lay, ids, [((full_two,), hidden_grad)], "up_grad")
    up_total = reduce_group(lay, ids, up_grads)
    branch_grad, res_grad, att_grad, sums_two = second_norm_backward(
        cot_own, cot_other, norm_part, norm_other, centered, factor, vec_own, vec_other, o_full
    )
    qkv_grad, joint_sums = attention_backward(prefix_length, qkv, att_grad, logs, attended, heads)
    joint_grads = weight_grad(
        lay, ids, [((full_one,), qkv_grad), ((branch_grad,), attended)], "joint_grad"
    )
    joint_total = reduce_group(lay, ids, joint_grads)
    first_part = project_backward(qkv_grad, j_full)
    first_other = swap_cores(first_part)
    tokens_grad, sums_one = first_norm_backward(
        x_own, x_other, first_part, first_other, vec_own, vec_other, res_grad
    )
    down_own, down_send = down_project(active, d_full)
    down_got = swap_cores(down_send)
    layer_out = (
        residual + (down_own.astype(F32) + down_got.astype(F32) + down_bias[None, :])
    ).astype(BF)

    small = jnp.concatenate(
        [sums_one.reshape(-1), sums_two.reshape(-1), joint_sums.reshape(-1), up_bias_grad.reshape(-1)]
    ).reshape(-1, HDIM)
    for bit in lay.split_bits + lay.rest_bits:
        small = small + swap(small, "dp", lay.Q, bit)
    for bit in lay.row_bits:
        small = small + swap(small, "row", lay.R, bit)
    small = small.reshape(-1)

    def take(start, n):
        return lax.slice_in_dim(small, start, start + n, axis=0)

    joint_n = joint_bias.shape[0]
    (grad_down,) = finish_group(lay, ids, *spread_group(lay, down_total), [(0, down_weight.shape[0], True)])
    (grad_up,) = finish_group(lay, ids, *spread_group(lay, up_total), [(0, up_weight.shape[1], False)])
    j_width = joint_weight.shape[1]
    grad_joint, grad_output = finish_group(
        lay, ids, *spread_group(lay, joint_total), [(0, j_width, False), (j_width, output_weight.shape[0], True)]
    )
    return (
        layer_out,
        tokens_grad,
        take(0, HALF),
        take(HALF, HALF),
        grad_joint,
        take(6 * HALF, joint_n),
        grad_output,
        take(4 * HALF, HALF),
        take(2 * HALF, HALF),
        take(3 * HALF, HALF),
        grad_up,
        take(6 * HALF + joint_n, up_bias.shape[0]),
        grad_down,
        take(5 * HALF, HALF),
    )


def solution(mesh):
    lay = Layout(mesh)
    vec, rows, cols, flat = P("col"), P("row", "col"), P("col", "row"), P(("dp", "row"), "col")

    def shards(*args):
        return layer(lay, *args)

    return jax.shard_map(
        shards,
        mesh=mesh,
        in_specs=(flat, flat, P(("dp", "row")), vec, vec, rows, vec, cols, vec, vec, vec, rows, vec, cols, vec),
        out_specs=(flat, flat, vec, vec, rows, vec, cols, vec, vec, vec, rows, vec, cols, vec),
        check_vma=False,
    )
```

time: 1090 us -> 412 us (0.38)
  waiting for transfers between devices: 736 us -> 169 us
  Pallas kernels: 0 us -> 154 us
  matrix products: 117 us -> 0 us
  blocking collectives: 107 us -> 0 us
  starting transfers between devices: 1.11 us -> 49.9 us
  other arithmetic: 51.7 us -> 6.8 us
  local copies, waits for them, and re-layouts: 52.1 us -> 23.5 us
  between operations: 15.2 us -> 2.48 us
    reduce_scatter x8 -> x0, waiting for transfers between devices: 482 us -> none  [the longest x1 180 us: shards(): lax.psum_scatter(reorder(grad_up_weight, 0), ('dp', 'row'), scatter_dimen...]
    all_gather x10 -> x0, waiting for transfers between devices: 250 us -> none  [the longest x2 141 us: rows_forward(): lax.all_gather(weight, 'row', axis=0, tiled=True)]
    ppermute x0 -> x53, waiting for transfers between devices: none -> 169 us  [the longest x46 169 us: swap(): return lax.ppermute(value, axis, [(i, i ^ bit) for i in range(size)])]
    pallas_call x0 -> x25, Pallas kernels: none -> 154 us  [the longest x3 33.1 us: weight_grad(): pl.pallas_call(kernel, in_specs=[smem()] + [vmem()] * (len(flat) - 1), ou...]
    dot_general x26 -> x0, matrix products: 117 us -> none  [the longest x4 21.9 us: contract_rows(): lax.dot_general(left_side, right_side, (((0,), (0,)), ((), ())), preferre...]
    psum x5 -> x0, blocking collectives: 87.9 us -> none  [the longest x1 77.4 us: shards(): lax.psum((grad_first_gain, grad_first_shift, grad_joint_bias, grad_output...]
    ppermute x0 -> x53, starting transfers between devices: none -> 49.9 us  [the longest x46 48.7 us: swap(): return lax.ppermute(value, axis, [(i, i ^ bit) for i in range(size)])]
    convert_element_type x14 -> x4, other arithmetic: 25.5 us -> 2.93 us  [the longest x1 2.73 us: layer(): layer_out = (residual + (down_own.astype(F32) + down_got.astype(F32) + do...]
  transfers between devices with their start and end apart: 18 -> 53, of which waited for: 12 -> 22; matrix products, arithmetic and copies ran while one was open for 17% -> 3% of each run, Pallas kernels for 0% -> 33%
where the time goes in v1:
time: 412 us; the launch traced here: 405 us
  waiting for transfers between devices  169 us (41%)
  Pallas kernels  154 us (37%)
  starting transfers between devices  49.9 us (12%)
  local copies, waits for them, and re-layouts  23.5 us (6%)
  other arithmetic  6.8 us (2%)
    ppermute x46, waiting for transfers between devices, swap(): return lax.ppermute(value, axis, [(i, i ^ bit) for i in range(size)])  169 us
    ppermute x46, starting transfers between devices, swap(): return lax.ppermute(value, axis, [(i, i ^ bit) for i in range(size)])  48.7 us
    pallas_call x3, Pallas kernels, weight_grad(): pl.pallas_call(kernel, in_specs=[smem()] + [vmem()] * (len(flat) - 1), ou...  33.1 us
    pallas_call x1, Pallas kernels, second_norm_up(): pl.pallas_call(kernel, in_specs=[smem()] + [vmem()] * 7 + [anywhere()] *...  17.8 us
    pallas_call x1, Pallas kernels, hidden_backward(): pl.pallas_call(kernel, in_specs=[smem()] + [vmem()] * 4 + [anywhere()] *...  17.6 us
    unnamed x99, local copies, waits for them, and re-layouts  15.2 us
    pallas_call x9, Pallas kernels, add_split(): pl.pallas_call(kernel, in_specs=[smem()] + [vmem()] * len(flat), out_spec...  12 us
    pallas_call x1, Pallas kernels, attention_backward(): pl.pallas_call(kernel, grid=(heads,), in_specs=[smem(), pl.BlockSpec((LEN...  10.6 us
  transfers between devices with their start and end apart: 53, of which 22 were waited for; matrix products, arithmetic and copies ran while one was open for 3% of the time, Pallas kernels for 33%

profile of v1, /device:TPU:0, one launch (start us, length us, event | category | flops | bytes accessed | tf_op | source)
XLA Modules:
  0.0 405.0 jit_solution(2919649715170940283)
XLA Ops:
  2.5 4.1 %collective-permute-start.2 = (bf16[1,64,2048]{2,1,0:T(8,128)(2,1)S(1)}, bf16[1,64,2048]{2,1,0:T(8,128)(2,1)S(1)}, u32[]{:S(2)}, u32[]{:S(2)}) collective-permute-start(bf16[1,64,2048]{2,1,0:T(8,128)(2,1)S(1)} %maximum_bitcast_fusion), channel_id=1, source_target_pairs={{0,4},{2,6},{4,0},{6,2},{1,5},{3,7},{5,1},{7,3},{8,12},{10,14},{12... | collective-permute-start | bytes 786440 | tf_op jit(solution)/shard_map/ppermute | solution.py:79
  9.0 15.9 %collective-permute-done.2 = bf16[1,64,2048]{2,1,0:T(8,128)(2,1)S(1)} collective-permute-done((bf16[1,64,2048]{2,1,0:T(8,128)(2,1)S(1)}, bf16[1,64,2048]{2,1,0:T(8,128)(2,1)S(1)}, u32[]{:S(2)}, u32[]{:S(2)}) %collective-permute-start.2) | collective-permute-done | bytes 262176 | tf_op jit(solution)/shard_map/ppermute | solution.py:79
  26.0 3.4 collective-permute-start.16
  29.6 17.0 %collective-permute-done.3 = bf16[2,64,2048]{2,1,0:T(8,128)(2,1)S(1)} collective-permute-done((bf16[2,64,2048]{2,1,0:T(8,128)(2,1)S(1)}, bf16[2,64,2048]{2,1,0:T(8,128)(2,1)S(1)}, u32[]{:S(2)}, u32[]{:S(2)}) %collective-permute-start.3) | collective-permute-done | bytes 524320 | tf_op jit(solution)/shard_map/ppermute | solution.py:79
  50.9 6.9 %collective-permute-done.4 = bf16[1,3,64,1024]{3,2,1,0:T(8,128)(2,1)S(1)} collective-permute-done((bf16[1,3,64,1024]{3,2,1,0:T(8,128)(2,1)S(1)}, bf16[1,3,64,1024]{3,2,1,0:T(8,128)(2,1)S(1)}, u32[]{:S(2)}, u32[]{:S(2)}) %collective-permute-start.4) | collective-permute-done | bytes 393248 | tf_op jit(solution)/shard_map/ppermute | solution.py:79
  67.4 10.3 %collective-permute-done.5.a1 = bf16[2,3,64,1024]{3,2,1,0:T(8,128)(2,1)} collective-permute-done((bf16[2,3,64,1024]{3,2,1,0:T(8,128)(2,1)S(1)}, bf16[2,3,64,1024]{3,2,1,0:T(8,128)(2,1)}, u32[]{:S(2)}, u32[]{:S(2)}) %collective-permute-start.5) | collective-permute-done | bytes 786464 | tf_op jit(solution)/shard_map/ppermute | solution.py:79
  77.7 6.2 %collective-permute-done.7.b1 = bf16[2,3,64,1024]{3,2,1,0:T(8,128)(2,1)} collective-permute-done((bf16[2,3,64,1024]{3,2,1,0:T(8,128)(2,1)S(1)}, bf16[2,3,64,1024]{3,2,1,0:T(8,128)(2,1)}, u32[]{:S(2)}, u32[]{:S(2)}) %collective-permute-start.7) | collective-permute-done | bytes 786464 | tf_op jit(solution)/shard_map/ppermute | solution.py:79
  83.8 10.4 %first_norm_project.1 = (bf16[1024,1024]{1,0:T(8,128)(2,1)}, bf16[1024,1536]{1,0:T(8,128)(2,1)}, bf16[1024,1536]{1,0:T(8,128)(2,1)}, bf16[512,1024]{1,0:T(8,128)(2,1)}) custom-call(s32[3]{0:T(128)} %pad_add_fusion.ids, bf16[1024,512]{1,0:T(8,128)(2,1)} %xo.5, bf16[1024,512]{1,0:T(8,128)(2,1)} %copy-done.27, f32[8,512]{1,0:T(8,128)} %copy-done.40, ...), custom_call_target="tpu_custom_call" | custom-call | tf_op jit(solution)/shard_map/first_norm_project/pallas_call | solution.py:360
  94.2 8.3 %attention_forward.1 = (bf16[1024,512]{1,0:T(8,128)(2,1)}, f32[4,1,1024]{2,1,0:T(1,128)}) custom-call(s32[1]{0:T(128)S(6)} %copy.34.prefix_ref, bf16[1024,1536]{1,0:T(8,128)(2,1)} %get-tuple-element.79.qkv_ref), custom_call_target="tpu_custom_call" | custom-call | tf_op jit(solution)/shard_map/attention_forward/pallas_call | solution.py:399
  102.6 4.2 %output_project.1.po = bf16[1024,1024]{1,0:T(8,128)(2,1)} custom-call(bf16[1024,512]{1,0:T(8,128)(2,1)} %get-tuple-element.80.a_ref.att_ref.refs_3_, bf16[512,1024]{1,0:T(8,128)(2,1)} %get-tuple-element.81.o_ref), custom_call_target="tpu_custom_call" | custom-call | tf_op jit(solution)/shard_map/output_project/pallas_call | solution.py:418
  113.2 5.6 %collective-permute-done.13 = bf16[1,3,64,1024]{3,2,1,0:T(8,128)(2,1)S(1)} collective-permute-done((bf16[1,3,64,1024]{3,2,1,0:T(8,128)(2,1)S(1)}, bf16[1,3,64,1024]{3,2,1,0:T(8,128)(2,1)S(1)}, u32[]{:S(2)}, u32[]{:S(2)}) %collective-permute-start.13) | collective-permute-done | bytes 393248 | tf_op jit(solution)/shard_map/ppermute | solution.py:79
  118.8 3.4 collective-permute-done.18
  122.7 20.9 %collective-permute-done.20 = bf16[1,3,256,256]{3,2,1,0:T(8,128)(2,1)S(1)} collective-permute-done((bf16[1,3,256,256]{3,2,1,0:T(8,128)(2,1)S(1)}, bf16[1,3,256,256]{3,2,1,0:T(8,128)(2,1)S(1)}, u32[]{:S(2)}, u32[]{:S(2)}) %collective-permute-start.20) | collective-permute-done | bytes 393248 | tf_op jit(solution)/shard_map/ppermute | solution.py:79
  147.1 17.8 %second_norm_up.1 = (f32[1024,512]{1,0:T(8,128)}, bf16[1024,1024]{1,0:T(8,128)(2,1)}, f32[1024,1]{1,0:T(8,128)}, bf16[1024,1024]{1,0:T(8,128)(2,1)}, bf16[1024,2...) custom-call(s32[3]{0:T(128)} %pad_add_fusion.ids, bf16[1024,512]{1,0:T(8,128)(2,1)} %xo.5, ...), custom_call_target="tpu_custom_call" | custom-call | tf_op jit(solution)/shard_map/second_norm_up/pallas_call | solution.py:466
  166.0 17.6 %hidden_backward.1 = (bf16[1024,2048]{1,0:T(8,128)(2,1)}, bf16[1024,1024]{1,0:T(8,128)(2,1)}, f32[1,2048]{1,0:T(1,128)}, bf16[2048,1024]{1,0:T(8,128)(2,1)}) custom-call(s32[3]{0:T(128)} %pad_add_fusion.ids, bf16[1024,512]{1,0:T(8,128)(2,1)} %refs_0_.1, bf16[1024,512]{1,0:T(8,128)(2,1)} %copy-done.26, bf16[1024,2048]{1,0:T(8,128)(2,1)} %get-tuple-element.84.slope_ref, ...), custom_call_target="tpu_custom_call" | custom-call | tf_op jit(solution)/shard_map/hidden_backward/pallas_call | solution.py:543
  183.6 10.8 %up_grad.1 = (bf16[8,64,1024]{2,1,0:T(8,128)(2,1)}, bf16[8,64,1024]{2,1,0:T(8,128)(2,1)}, bf16[8,64,1024]{2,1,0:T(8,128)(2,1)}, bf16[8,64,1024]{2,1,0:T(8,128)(2,1)}) custom-call(s32[3]{0:T(128)} %pad_add_fusion.ids, bf16[1024,1024]{1,0:T(8,128)(2,1)} %get-tuple-element.118.refs_0_, bf16[1024,2048]{1,0:T(8,128)(2,1)} %get-tuple-element.119.refs_1_), custom_call_target="tpu_custom_call" | custom-call | tf_op jit(solution)/shard_map/up_grad/pallas_call | solution.py:506
  196.1 10.8 %down_grad.1 = (bf16[8,64,1024]{2,1,0:T(8,128)(2,1)}, bf16[8,64,1024]{2,1,0:T(8,128)(2,1)}, bf16[8,64,1024]{2,1,0:T(8,128)(2,1)}, bf16[8,64,1024]{2,1,0:T(8,128)(2,1)}) custom-call(s32[3]{0:T(128)} %pad_add_fusion.ids, bf16[1024,512]{1,0:T(8,128)(2,1)} %refs_0_.1, bf16[1024,512]{1,0:T(8,128)(2,1)} %copy-done.26, ...), custom_call_target="tpu_custom_call" | custom-call | tf_op jit(solution)/shard_map/down_grad/pallas_call | solution.py:506
  209.4 11.3 %collective-permute-done.37 = bf16[8,64,1024]{2,1,0:T(8,128)(2,1)} collective-permute-done((bf16[8,64,1024]{2,1,0:T(8,128)(2,1)}, bf16[8,64,1024]{2,1,0:T(8,128)(2,1)}, u32[]{:S(2)}, u32[]{:S(2)}) %collective-permute-start.37) | collective-permute-done | bytes 1048608 | tf_op jit(solution)/shard_map/ppermute | solution.py:79
  229.3 13.8 %collective-permute-done.45 = bf16[8,64,1024]{2,1,0:T(8,128)(2,1)S(1)} collective-permute-done((bf16[8,64,1024]{2,1,0:T(8,128)(2,1)}, bf16[8,64,1024]{2,1,0:T(8,128)(2,1)S(1)}, u32[]{:S(2)}, u32[]{:S(2)}) %collective-permute-start.45) | collective-permute-done | bytes 1048608 | tf_op jit(solution)/shard_map/ppermute | solution.py:79
  249.3 9.2 %second_norm_backward.1 = (bf16[1024,1024]{1,0:T(8,128)(2,1)}, f32[1024,512]{1,0:T(8,128)}, bf16[1024,512]{1,0:T(8,128)(2,1)}, f32[4,512]{1,0:T(4,128)}) custom-call(bf16[1024,512]{1,0:T(8,128)(2,1)} %refs_0_.1, bf16[1024,512]{1,0:T(8,128)(2,1)} %copy-done.26, bf16[1024,1024]{1,0:T(8,128)(2,1)} %get-tuple-element.89.po, ...), custom_call_target="tpu_custom_call" | custom-call | tf_op jit(solution)/shard_map/second_norm_backward/pallas_call | solution.py:574
  258.5 10.6 %attention_backward.1 = (bf16[1024,1536]{1,0:T(8,128)(2,1)}, f32[4,1,256]{2,1,0:T(1,128)}) custom-call(s32[1]{0:T(128)S(6)} %copy.34.prefix_ref, bf16[1024,1536]{1,0:T(8,128)(2,1)} %get-tuple-element.79.qkv_ref, bf16[1024,512]{1,0:T(8,128)(2,1)} %get-tuple-element.92.grad_ref, f32[4,1,1024]{2,1,0:T(1,128)} %get-tuple-element.93.log_ref, ...), custom_call_target="tpu_custom_call" | custom-call | tf_op jit(solution)/shard_map/attention_backward/pallas_call | solution.py:621
  269.1 11.4 %joint_grad.1 = (bf16[8,64,1024]{2,1,0:T(8,128)(2,1)}, bf16[8,64,1024]{2,1,0:T(8,128)(2,1)}, bf16[8,64,1024]{2,1,0:T(8,128)(2,1)}, bf16[8,64,1024]{2,1,0:T(8,128)(2,1)}) custom-call(s32[3]{0:T(128)} %pad_add_fusion.ids, bf16[1024,1024]{1,0:T(8,128)(2,1)} %get-tuple-element.102.refs_0_, bf16[1024,1536]{1,0:T(8,128)(2,1)} %get-tuple-element.94.g_ref.refs_1_, ...), custom_call_target="tpu_custom_call" | custom-call | tf_op jit(solution)/shard_map/joint_grad/pallas_call | solution.py:506
  283.2 8.9 %down_project.1 = (bf16[1024,512]{1,0:T(8,128)(2,1)}, bf16[1024,512]{1,0:T(8,128)(2,1)}) custom-call(bf16[1024,2048]{1,0:T(8,128)(2,1)} %get-tuple-element.83.a_ref.refs_2_, bf16[2048,1024]{1,0:T(8,128)(2,1)} %get-tuple-element.86.d_ref), custom_call_target="tpu_custom_call" | custom-call | tf_op jit(solution)/shard_map/down_project/pallas_call | solution.py:664
  292.2 7.7 %project_backward.1.po = bf16[1024,1024]{1,0:T(8,128)(2,1)} custom-call(bf16[1024,1536]{1,0:T(8,128)(2,1)} %get-tuple-element.94.g_ref.refs_1_, bf16[1024,1536]{1,0:T(8,128)(2,1)} %get-tuple-element.95.w_ref), custom_call_target="tpu_custom_call" | custom-call | tf_op jit(solution)/shard_map/project_backward/pallas_call | solution.py:647
  308.4 8.8 %collective-permute-done.41 = bf16[2,64,2048]{2,1,0:T(8,128)(2,1)S(1)} collective-permute-done((bf16[2,64,2048]{2,1,0:T(8,128)(2,1)S(1)}, bf16[2,64,2048]{2,1,0:T(8,128)(2,1)S(1)}, u32[]{:S(2)}, u32[]{:S(2)}) %collective-permute-start.41) | collective-permute-done | bytes 524320 | tf_op jit(solution)/shard_map/ppermute | solution.py:79
  320.5 3.8 collective-permute-start.42
  330.5 6.5 %collective-permute-done.49 = bf16[2,64,2048]{2,1,0:T(8,128)(2,1)} collective-permute-done((bf16[2,64,2048]{2,1,0:T(8,128)(2,1)}, bf16[2,64,2048]{2,1,0:T(8,128)(2,1)}, u32[]{:S(2)}, u32[]{:S(2)}) %collective-permute-start.49) | collective-permute-done | bytes 524320 | tf_op jit(solution)/shard_map/ppermute | solution.py:79
  343.6 7.7 %collective-permute-done.50 = bf16[1,64,2048]{2,1,0:T(8,128)(2,1)S(1)} collective-permute-done((bf16[1,64,2048]{2,1,0:T(8,128)(2,1)S(1)}, bf16[1,64,2048]{2,1,0:T(8,128)(2,1)S(1)}, u32[]{:S(2)}, u32[]{:S(2)}) %collective-permute-start.50) | collective-permute-done | bytes 262176 | tf_op jit(solution)/shard_map/ppermute | solution.py:79
  352.3 7.2 %first_norm_backward.1 = (bf16[1024,512]{1,0:T(8,128)(2,1)}, f32[2,512]{1,0:T(2,128)}) custom-call(bf16[1024,512]{1,0:T(8,128)(2,1)} %xo.5, bf16[1024,512]{1,0:T(8,128)(2,1)} %copy-done.27, bf16[1024,1024]{1,0:T(8,128)(2,1)} %project_backward.1.po, bf16[1024,1024]{1,0:T(8,128)(2,1)} %collective-permute-done.24.pt, f32[8,512]{1,0:T(8,128)} %copy-done.40, ...), custom_call_target="tpu_custom_call" | custom-call | tf_op jit(solution)/shard_map/first_norm_backward/pallas_call | solution.py:690
  366.2 10.9 %collective-permute-done.26 = f32[48,128]{1,0:T(8,128)S(1)} collective-permute-done((f32[48,128]{1,0:T(8,128)S(1)}, f32[48,128]{1,0:T(8,128)S(1)}, u32[]{:S(2)}, u32[]{:S(2)}) %collective-permute-start.26) | collective-permute-done | bytes 24608 | tf_op jit(solution)/shard_map/ppermute | solution.py:79
  382.0 3.8 collective-permute-done.52
  393.1 9.1 %collective-permute-done.36 = bf16[2,64,2048]{2,1,0:T(8,128)(2,1)S(1)} collective-permute-done((bf16[2,64,2048]{2,1,0:T(8,128)(2,1)S(1)}, bf16[2,64,2048]{2,1,0:T(8,128)(2,1)S(1)}, u32[]{:S(2)}, u32[]{:S(2)}) %collective-permute-start.36) | collective-permute-done | bytes 524320 | tf_op jit(solution)/shard_map/ppermute | solution.py:79
  (245 shorter events, 98.2 us)
Async XLA Ops:
  2.5 22.5 %collective-permute-start.2 = (bf16[1,64,2048]{2,1,0:T(8,128)(2,1)S(1)}, bf16[1,64,2048]{2,1,0:T(8,128)(2,1)S(1)}, u32[]{:S(2)}, u32[]{:S(2)}) collective-permute-start(bf16[1,64,2048]{2,1,0:T(8,128)(2,1)S(1)} %maximum_bitcast_fusion), channel_id=1, source_target_pairs={{0,4},{2,6},{4,0},{6,2},{1,5},{3,7},{5,1},{7,3},{8,12},{10,14},{12... | collective-permute-start | bytes 786440 | tf_op jit(solution)/shard_map/ppermute | solution.py:79
  6.6 60.8 %collective-permute-start = (bf16[1024,512]{1,0:T(8,128)(2,1)}, bf16[1024,512]{1,0:T(8,128)(2,1)S(1)}, u32[]{:S(2)}, u32[]{:S(2)}) collective-permute-start(bf16[1024,512]{1,0:T(8,128)(2,1)} %xo.5), channel_id=1, source_target_pairs={{0,1},{1,0},{2,3},{3,2},{4,5},{5,4},{6,7},{7,6},{8,9},{9,8},{10,11... | collective-permute-start | bytes 3145736 | tf_op jit(solution)/shard_map/ppermute | solution.py:83
  7.4 56.3 %collective-permute-start.1 = (f32[8,512]{1,0:T(8,128)S(1)}, f32[8,512]{1,0:T(8,128)S(1)}, u32[]{:S(2)}, u32[]{:S(2)}) collective-permute-start(f32[8,512]{1,0:T(8,128)S(1)} %stack.61.vo), channel_id=1, source_target_pairs={{0,1},{1,0},{2,3},{3,2},{4,5},{5,4},{6,7},{7,6},{8,9},{9,8},{10,11... | collective-permute-start | bytes 49160 | tf_op jit(solution)/shard_map/ppermute | solution.py:83
  8.9 39.4 %collective-permute-start.9 = (bf16[1,64,2048]{2,1,0:T(8,128)(2,1)S(1)}, bf16[1,64,2048]{2,1,0:T(8,128)(2,1)S(1)}, u32[]{:S(2)}, u32[]{:S(2)}) collective-permute-start(bf16[1,64,2048]{2,1,0:T(8,128)(2,1)S(1)} %dynamic-slice_bitcast_fusion.1), channel_id=1, source_target_pairs={{0,4},{2,6},{4,0},{6,2},{1,5},{3,7},{5,1},{7,3},{8,12},{10,14},{12... | collective-permute-start | bytes 786440 | tf_op jit(solution)/shard_map/ppermute | solution.py:79
  25.0 21.6 %collective-permute-start.3 = (bf16[2,64,2048]{2,1,0:T(8,128)(2,1)S(1)}, bf16[2,64,2048]{2,1,0:T(8,128)(2,1)S(1)}, u32[]{:S(2)}, u32[]{:S(2)}) collective-permute-start(bf16[2,64,2048]{2,1,0:T(8,128)(2,1)S(1)} %pad_maximum_fusion.9), channel_id=1, source_target_pairs={{0,2},{2,0},{4,6},{6,4},{1,3},{3,1},{5,7},{7,5},{8,10},{10,8},{12,... | collective-permute-start | bytes 1572872 | tf_op jit(solution)/shard_map/ppermute | solution.py:79
  26.0 22.4 %collective-permute-start.16 = (bf16[1,512,256]{2,1,0:T(8,128)(2,1)S(1)}, bf16[1,512,256]{2,1,0:T(8,128)(2,1)S(1)}, u32[]{:S(2)}, u32[]{:S(2)}) collective-permute-start(bf16[1,512,256]{2,1,0:T(8,128)(2,1)S(1)} %dynamic-slice_bitcast_fusion), channel_id=1, source_target_pairs={{0,4},{2,6},{4,0},{6,2},{1,5},{3,7},{5,1},{7,3},{8,12},{10,14},{12... | collective-permute-start | bytes 786440 | tf_op jit(solution)/shard_map/ppermute | solution.py:79
  57.8 50.6 %collective-permute-start.17 = (bf16[2,512,256]{2,1,0:T(8,128)(2,1)}, bf16[2,512,256]{2,1,0:T(8,128)(2,1)}, u32[]{:S(2)}, u32[]{:S(2)}) collective-permute-start(bf16[2,512,256]{2,1,0:T(8,128)(2,1)} %pad_maximum_fusion.11), channel_id=1, source_target_pairs={{0,2},{2,0},{4,6},{6,4},{1,3},{3,1},{5,7},{7,5},{8,10},{10,8},{12,... | collective-permute-start | bytes 1572872 | tf_op jit(solution)/shard_map/ppermute | solution.py:79
  63.2 20.6 %collective-permute-start.7 = (bf16[2,3,64,1024]{3,2,1,0:T(8,128)(2,1)S(1)}, bf16[2,3,64,1024]{3,2,1,0:T(8,128)(2,1)}, u32[]{:S(2)}, u32[]{:S(2)}) collective-permute-start(bf16[2,3,64,1024]{3,2,1,0:T(8,128)(2,1)S(1)} %pad_maximum_fusion.4.b0), channel_id=1, source_target_pairs={{0,8},{8,0},{16,24},{24,16},{1,9},{9,1},{17,25},{25,17},{2,10},{10... | collective-permute-start | bytes 2359304 | tf_op jit(solution)/shard_map/ppermute | solution.py:79
  63.7 45.7 %collective-permute-start.11 = (bf16[1,3,64,1024]{3,2,1,0:T(8,128)(2,1)S(1)}, bf16[1,3,64,1024]{3,2,1,0:T(8,128)(2,1)}, u32[]{:S(2)}, u32[]{:S(2)}) collective-permute-start(bf16[1,3,64,1024]{3,2,1,0:T(8,128)(2,1)S(1)} %get-tuple-element.147), channel_id=1, source_target_pairs={{0,8},{8,0},{16,24},{24,16},{1,9},{9,1},{17,25},{25,17},{2,10},{10... | collective-permute-start | bytes 1179656 | tf_op jit(solution)/shard_map/ppermute | solution.py:79
  106.7 39.5 %collective-permute-start.8 = (bf16[1024,1024]{1,0:T(8,128)(2,1)}, bf16[1024,1024]{1,0:T(8,128)(2,1)}, u32[]{:S(2)}, u32[]{:S(2)}) collective-permute-start(bf16[1024,1024]{1,0:T(8,128)(2,1)} %output_project.1.po), channel_id=1, source_target_pairs={{0,1},{1,0},{2,3},{3,2},{4,5},{5,4},{6,7},{7,6},{8,9},{9,8},{10,11... | collective-permute-start | bytes 6291464 | tf_op jit(solution)/shard_map/ppermute | solution.py:83
  110.5 34.7 %collective-permute-start.12 = (bf16[2,3,64,1024]{3,2,1,0:T(8,128)(2,1)S(1)}, bf16[2,3,64,1024]{3,2,1,0:T(8,128)(2,1)S(1)}, u32[]{:S(2)}, u32[]{:S(2)}) collective-permute-start(bf16[2,3,64,1024]{3,2,1,0:T(8,128)(2,1)S(1)} %pad_maximum_fusion.5.a0), channel_id=1, source_target_pairs={{0,16},{8,24},{16,0},{24,8},{1,17},{9,25},{17,1},{25,9},{2,18},{10... | collective-permute-start | bytes 2359304 | tf_op jit(solution)/shard_map/ppermute | solution.py:79
  111.5 32.1 %collective-permute-start.20 = (bf16[1,3,256,256]{3,2,1,0:T(8,128)(2,1)S(1)}, bf16[1,3,256,256]{3,2,1,0:T(8,128)(2,1)S(1)}, u32[]{:S(2)}, u32[]{:S(2)}) collective-permute-start(bf16[1,3,256,256]{3,2,1,0:T(8,128)(2,1)S(1)} %get-tuple-element.144), channel_id=1, source_target_pairs={{0,16},{8,24},{16,0},{24,8},{1,17},{9,25},{17,1},{25,9},{2,18},{10... | collective-permute-start | bytes 1179656 | tf_op jit(solution)/shard_map/ppermute | solution.py:79
  118.7 46.2 %collective-permute-start.15 = (bf16[1024,512]{1,0:T(8,128)(2,1)S(1)}, bf16[1024,512]{1,0:T(8,128)(2,1)S(1)}, u32[]{:S(2)}, u32[]{:S(2)}) collective-permute-start(bf16[1024,512]{1,0:T(8,128)(2,1)S(1)} %copy-done.25), channel_id=1, source_target_pairs={{0,1},{1,0},{2,3},{3,2},{4,5},{5,4},{6,7},{7,6},{8,9},{9,8},{10,11... | collective-permute-start | bytes 3145736 | tf_op jit(solution)/shard_map/ppermute | solution.py:83
  122.2 23.5 %collective-permute-start.14 = (bf16[2,3,64,1024]{3,2,1,0:T(8,128)(2,1)S(1)}, bf16[2,3,64,1024]{3,2,1,0:T(8,128)(2,1)S(1)}, u32[]{:S(2)}, u32[]{:S(2)}) collective-permute-start(bf16[2,3,64,1024]{3,2,1,0:T(8,128)(2,1)S(1)} %pad_maximum_fusion.6.b0), channel_id=1, source_target_pairs={{0,8},{8,0},{16,24},{24,16},{1,9},{9,1},{17,25},{25,17},{2,10},{10... | collective-permute-start | bytes 2359304 | tf_op jit(solution)/shard_map/ppermute | solution.py:79
  143.6 21.3 %collective-permute-start.19 = (bf16[2,3,256,256]{3,2,1,0:T(8,128)(2,1)S(1)}, bf16[2,3,256,256]{3,2,1,0:T(8,128)(2,1)}, u32[]{:S(2)}, u32[]{:S(2)}) collective-permute-start(bf16[2,3,256,256]{3,2,1,0:T(8,128)(2,1)S(1)} %pad_maximum_fusion.7.a0), channel_id=1, source_target_pairs={{0,16},{8,24},{16,0},{24,8},{1,17},{9,25},{17,1},{25,9},{2,18},{10... | collective-permute-start | bytes 2359304 | tf_op jit(solution)/shard_map/ppermute | solution.py:79
  145.3 19.7 %collective-permute-start.21 = (bf16[2,3,256,256]{3,2,1,0:T(8,128)(2,1)S(1)}, bf16[2,3,256,256]{3,2,1,0:T(8,128)(2,1)}, u32[]{:S(2)}, u32[]{:S(2)}) collective-permute-start(bf16[2,3,256,256]{3,2,1,0:T(8,128)(2,1)S(1)} %pad_maximum_fusion.8.b0), channel_id=1, source_target_pairs={{0,8},{8,0},{16,24},{24,16},{1,9},{9,1},{17,25},{25,17},{2,10},{10... | collective-permute-start | bytes 2359304 | tf_op jit(solution)/shard_map/ppermute | solution.py:79
  183.6 65.8 %collective-permute-start.23 = (bf16[1024,1024]{1,0:T(8,128)(2,1)}, bf16[1024,1024]{1,0:T(8,128)(2,1)}, u32[]{:S(2)}, u32[]{:S(2)}) collective-permute-start(bf16[1024,1024]{1,0:T(8,128)(2,1)} %get-tuple-element.89.po), channel_id=1, source_target_pairs={{0,1},{1,0},{2,3},{3,2},{4,5},{5,4},{6,7},{7,6},{8,9},{9,8},{10,11... | collective-permute-start | bytes 6291464 | tf_op jit(solution)/shard_map/ppermute | solution.py:83
  194.5 26.3 %collective-permute-start.37 = (bf16[8,64,1024]{2,1,0:T(8,128)(2,1)}, bf16[8,64,1024]{2,1,0:T(8,128)(2,1)}, u32[]{:S(2)}, u32[]{:S(2)}) collective-permute-start(bf16[8,64,1024]{2,1,0:T(8,128)(2,1)} %get-tuple-element.121), channel_id=1, source_target_pairs={{0,8},{8,0},{16,24},{24,16},{1,9},{9,1},{17,25},{25,17},{2,10},{10... | collective-permute-start | bytes 3145736 | tf_op jit(solution)/shard_map/ppermute | solution.py:79
  195.6 26.3 %collective-permute-start.38 = (bf16[8,64,1024]{2,1,0:T(8,128)(2,1)}, bf16[8,64,1024]{2,1,0:T(8,128)(2,1)}, u32[]{:S(2)}, u32[]{:S(2)}) collective-permute-start(bf16[8,64,1024]{2,1,0:T(8,128)(2,1)} %get-tuple-element.123), channel_id=1, source_target_pairs={{0,16},{8,24},{16,0},{24,8},{1,17},{9,25},{17,1},{25,9},{2,18},{10... | collective-permute-start | bytes 3145736 | tf_op jit(solution)/shard_map/ppermute | solution.py:79
  206.9 36.2 %collective-permute-start.45 = (bf16[8,64,1024]{2,1,0:T(8,128)(2,1)}, bf16[8,64,1024]{2,1,0:T(8,128)(2,1)S(1)}, u32[]{:S(2)}, u32[]{:S(2)}) collective-permute-start(bf16[8,64,1024]{2,1,0:T(8,128)(2,1)} %get-tuple-element.133), channel_id=1, source_target_pairs={{0,8},{8,0},{16,24},{24,16},{1,9},{9,1},{17,25},{25,17},{2,10},{10... | collective-permute-start | bytes 3145736 | tf_op jit(solution)/shard_map/ppermute | solution.py:79
  207.8 36.5 %collective-permute-start.46 = (bf16[8,64,1024]{2,1,0:T(8,128)(2,1)}, bf16[8,64,1024]{2,1,0:T(8,128)(2,1)S(1)}, u32[]{:S(2)}, u32[]{:S(2)}) collective-permute-start(bf16[8,64,1024]{2,1,0:T(8,128)(2,1)} %get-tuple-element.135), channel_id=1, source_target_pairs={{0,16},{8,24},{16,0},{24,8},{1,17},{9,25},{17,1},{25,9},{2,18},{10... | collective-permute-start | bytes 3145736 | tf_op jit(solution)/shard_map/ppermute | solution.py:79
  227.9 53.8 %collective-permute-start.39 = (bf16[4,64,1024]{2,1,0:T(8,128)(2,1)}, bf16[4,64,1024]{2,1,0:T(8,128)(2,1)S(1)}, u32[]{:S(2)}, u32[]{:S(2)}) collective-permute-start(bf16[4,64,1024]{2,1,0:T(8,128)(2,1)} %get-tuple-element.125), channel_id=1, source_target_pairs={{0,16},{8,24},{16,0},{24,8},{1,17},{9,25},{17,1},{25,9},{2,18},{10... | collective-permute-start | bytes 1572872 | tf_op jit(solution)/shard_map/ppermute | solution.py:79
  228.4 63.8 %collective-permute-start.40 = (bf16[4,64,1024]{2,1,0:T(8,128)(2,1)}, bf16[4,64,1024]{2,1,0:T(8,128)(2,1)}, u32[]{:S(2)}, u32[]{:S(2)}) collective-permute-start(bf16[4,64,1024]{2,1,0:T(8,128)(2,1)} %get-tuple-element.127), channel_id=1, source_target_pairs={{0,8},{8,0},{16,24},{24,16},{1,9},{9,1},{17,25},{25,17},{2,10},{10... | collective-permute-start | bytes 1572872 | tf_op jit(solution)/shard_map/ppermute | solution.py:79
  247.9 52.0 %collective-permute-start.47 = (bf16[4,64,1024]{2,1,0:T(8,128)(2,1)}, bf16[4,64,1024]{2,1,0:T(8,128)(2,1)S(1)}, u32[]{:S(2)}, u32[]{:S(2)}) collective-permute-start(bf16[4,64,1024]{2,1,0:T(8,128)(2,1)} %get-tuple-element.137), channel_id=1, source_target_pairs={{0,16},{8,24},{16,0},{24,8},{1,17},{9,25},{17,1},{25,9},{2,18},{10... | collective-permute-start | bytes 1572872 | tf_op jit(solution)/shard_map/ppermute | solution.py:79
  248.4 54.9 %collective-permute-start.48 = (bf16[4,64,1024]{2,1,0:T(8,128)(2,1)}, bf16[4,64,1024]{2,1,0:T(8,128)(2,1)}, u32[]{:S(2)}, u32[]{:S(2)}) collective-permute-start(bf16[4,64,1024]{2,1,0:T(8,128)(2,1)} %get-tuple-element.139), channel_id=1, source_target_pairs={{0,8},{8,0},{16,24},{24,16},{1,9},{9,1},{17,25},{25,17},{2,10},{10... | collective-permute-start | bytes 1572872 | tf_op jit(solution)/shard_map/ppermute | solution.py:79
  280.5 40.0 %collective-permute-start.29 = (bf16[8,64,1024]{2,1,0:T(8,128)(2,1)}, bf16[8,64,1024]{2,1,0:T(8,128)(2,1)S(1)}, u32[]{:S(2)}, u32[]{:S(2)}) collective-permute-start(bf16[8,64,1024]{2,1,0:T(8,128)(2,1)} %get-tuple-element.105), channel_id=1, source_target_pairs={{0,8},{8,0},{16,24},{24,16},{1,9},{9,1},{17,25},{25,17},{2,10},{10... | collective-permute-start | bytes 3145736 | tf_op jit(solution)/shard_map/ppermute | solution.py:79
  281.7 42.7 %collective-permute-start.30 = (bf16[8,64,1024]{2,1,0:T(8,128)(2,1)}, bf16[8,64,1024]{2,1,0:T(8,128)(2,1)}, u32[]{:S(2)}, u32[]{:S(2)}) collective-permute-start(bf16[8,64,1024]{2,1,0:T(8,128)(2,1)} %get-tuple-element.107), channel_id=1, source_target_pairs={{0,16},{8,24},{16,0},{24,8},{1,17},{9,25},{17,1},{25,9},{2,18},{10... | collective-permute-start | bytes 3145736 | tf_op jit(solution)/shard_map/ppermute | solution.py:79
  292.1 34.7 %collective-permute-start.22 = (bf16[1024,512]{1,0:T(8,128)(2,1)}, bf16[1024,512]{1,0:T(8,128)(2,1)}, u32[]{:S(2)}, u32[]{:S(2)}) collective-permute-start(bf16[1024,512]{1,0:T(8,128)(2,1)} %get-tuple-element.88), channel_id=1, source_target_pairs={{0,1},{1,0},{2,3},{3,2},{4,5},{5,4},{6,7},{7,6},{8,9},{9,8},{10,11... | collective-permute-start | bytes 3145736 | tf_op jit(solution)/shard_map/ppermute | solution.py:83
  300.7 51.6 %collective-permute-start.24 = (bf16[1024,1024]{1,0:T(8,128)(2,1)}, bf16[1024,1024]{1,0:T(8,128)(2,1)}, u32[]{:S(2)}, u32[]{:S(2)}) collective-permute-start(bf16[1024,1024]{1,0:T(8,128)(2,1)} %project_backward.1.po), channel_id=1, source_target_pairs={{0,1},{1,0},{2,3},{3,2},{4,5},{5,4},{6,7},{7,6},{8,9},{9,8},{10,11... | collective-permute-start | bytes 6291464 | tf_op jit(solution)/shard_map/ppermute | solution.py:83
  339.8 21.6 %collective-permute-start.43 = (bf16[1,64,2048]{2,1,0:T(8,128)(2,1)S(1)}, bf16[1,64,2048]{2,1,0:T(8,128)(2,1)S(1)}, u32[]{:S(2)}, u32[]{:S(2)}) collective-permute-start(bf16[1,64,2048]{2,1,0:T(8,128)(2,1)S(1)} %add_convert_fusion.2), channel_id=1, source_target_pairs={{0,8},{8,0},{16,24},{24,16},{1,9},{9,1},{17,25},{25,17},{2,10},{10... | collective-permute-start | bytes 786440 | tf_op jit(solution)/shard_map/ppermute | solution.py:79
  341.0 21.2 %collective-permute-start.33 = (bf16[2,64,2048]{2,1,0:T(8,128)(2,1)S(1)}, bf16[2,64,2048]{2,1,0:T(8,128)(2,1)S(1)}, u32[]{:S(2)}, u32[]{:S(2)}) collective-permute-start(bf16[2,64,2048]{2,1,0:T(8,128)(2,1)S(1)} %get-tuple-element.113), channel_id=1, source_target_pairs={{0,2},{2,0},{4,6},{6,4},{1,3},{3,1},{5,7},{7,5},{8,10},{10,8},{12,... | collective-permute-start | bytes 1572872 | tf_op jit(solution)/shard_map/ppermute | solution.py:79
  364.6 21.2 %collective-permute-start.52 = (bf16[2,64,2048]{2,1,0:T(8,128)(2,1)S(1)}, bf16[2,64,2048]{2,1,0:T(8,128)(2,1)S(1)}, u32[]{:S(2)}, u32[]{:S(2)}) collective-permute-start(bf16[2,64,2048]{2,1,0:T(8,128)(2,1)S(1)} %pad_maximum_fusion.14), channel_id=1, source_target_pairs={{0,16},{8,24},{16,0},{24,8},{1,17},{9,25},{17,1},{25,9},{2,18},{10... | collective-permute-start | bytes 1572872 | tf_op jit(solution)/shard_map/ppermute | solution.py:79
  (68 other events, 745.8 us)

commit v2 on v0

v2 whole, which is shorter than its diff:
```python
import math

import jax
import jax.numpy as jnp
from jax import lax
from jax.experimental import pallas as pl
from jax.experimental.pallas import tpu as pltpu
from jax.sharding import PartitionSpec as P

D = 1024
HALF = 512
HDIM = 128
LEN = 1024
MAX_PREFIX = 512
EPSILON = 1e-05
NEGATIVE = -1e30
LOG2E = math.log2(math.e)
SCALE = HDIM**-0.5
TILE = 256

BF = jnp.bfloat16
F32 = jnp.float32
NT = (((1,), (1,)), ((), ()))
TN = (((0,), (0,)), ((), ()))


def vmem():
    return pl.BlockSpec(memory_space=pltpu.VMEM)


def smem():
    return pl.BlockSpec(memory_space=pltpu.SMEM)


def anywhere():
    return pl.BlockSpec(memory_space=pltpu.HBM)


def params(mib=60):
    return pltpu.CompilerParams(vmem_limit_bytes=mib << 20)


def shape(dims, kind=BF):
    return jax.ShapeDtypeStruct(tuple(dims), kind)


def hbm(dims, kind=BF):
    return pltpu.HBM(tuple(dims), kind)


def dot(left, right, dims=(((1,), (0,)), ((), ()))):
    return lax.dot_general(left, right, dims, preferred_element_type=F32)


class Layout:
    def __init__(self, mesh):
        self.R = mesh.shape["row"]
        self.Q = mesh.shape["dp"]
        self.block = D // self.R
        s = self.Q
        while self.block // s < 16:
            s //= 2
        self.s = s
        self.piece = self.block // s
        bits = self.Q.bit_length() - 1
        low = [1 << b for b in range(bits // 2)]
        high = [1 << b for b in range(bits // 2, bits)]
        mixed = []
        while low or high:
            if low:
                mixed.append(low.pop(0))
            if high:
                mixed.append(high.pop(0))
        k = s.bit_length() - 1
        self.split_bits = mixed[:k]
        self.rest_bits = mixed[k:]
        self.order_a = list(range(k))
        self.order_b = [1, 0] + list(range(2, k)) if k >= 2 else list(range(k))
        self.row_bits = [1 << b for b in range(self.R.bit_length() - 1)]


def swap(value, axis, size, bit):
    return lax.ppermute(value, axis, [(i, i ^ bit) for i in range(size)])


def swap_cores(value):
    return lax.ppermute(value, "col", [(0, 1), (1, 0)])


def device_ids(lay):
    z = lax.axis_index("row")
    d = lax.axis_index("dp")
    c = lax.axis_index("col")
    q = sum(((d // bit) % 2) << i for i, bit in enumerate(lay.split_bits))
    return jnp.stack([z ^ (c * (lay.R // 2)), q, c]).astype(jnp.int32)


COST = {
    "first_norm_project": 9,
    "attention_first": 5,
    "attention_second": 7,
    "second_norm_up": 15,
    "down_grad": 9,
    "hidden_backward": 17,
    "up_grad": 9,
    "second_norm_backward": 9,
    "attention_backward": 6,
    "joint_grad_a": 8,
    "joint_grad_b": 6,
    "project_backward": 8,
    "first_norm_backward": 6,
    "down_project": 9,
    "joint_sum_a": 32,
    "joint_sum_b": 40,
    "up_rows": 40,
}
COST_SCALE = 0.25 * 3.69e6


def call(kernel, name, ins, outs, grid=(), scratch=(), after=(), passing=(), mib=None):
    n_in, n_after, n_out, n_pass = len(ins), len(after), len(outs), len(passing)

    def body(*refs):
        refs = list(refs)
        first_out = n_in + n_after + n_pass
        token = first_out + n_out + n_pass
        kernel(*refs[:n_in], *refs[first_out : first_out + n_out], *refs[token + 1 :])

    results = pl.pallas_call(
        body,
        grid=grid,
        in_specs=[spec for _, spec in ins] + [anywhere()] * (n_after + n_pass),
        out_specs=[spec for _, spec in outs] + [anywhere()] * (n_pass + 1),
        out_shape=[kind for kind, _ in outs]
        + [shape(a.shape, a.dtype) for a in passing]
        + [shape((8, HDIM), F32)],
        scratch_shapes=list(scratch),
        compiler_params=params(mib or (8 if "sum" in name or "rows" in name else 18 if name in COST else 8)),
        input_output_aliases={n_in + n_after + i: n_out + i for i in range(n_pass)},
        cost_estimate=pl.CostEstimate(
            flops=1, bytes_accessed=int(COST_SCALE * COST.get(name, 2)), transcendentals=0
        ),
        name=name,
    )(*[array for array, _ in ins], *after, *passing)
    return results[:-1], results[-1]


def hold(arrays, after, name):
    return call(lambda: None, name, [], [], after=after, passing=arrays, mib=8)


def row_tile(width):
    return pl.BlockSpec((TILE, width), lambda i: (i, 0))


def whole(*dims):
    return pl.BlockSpec(dims, lambda i: (0,) * len(dims))


ROW_GRID = (LEN // TILE,)


def own_pieces(ids, parts, rows):
    return jnp.concatenate(
        [lax.dynamic_slice_in_dim(block, ids[1] * step + first, rows, axis=0) for block, step, first in parts], axis=1
    )


def extract(lay, ids, block, rows, after):
    def kernel(ids, source, out, sem):
        copy = pltpu.make_async_copy(source.at[pl.ds(pl.multiple_of(ids[1] * rows, 16), rows), :], out, sem)
        copy.start()
        copy.wait()

    (out,), token = call(
        kernel,
        "extract",
        [(ids, smem()), (block, anywhere())],
        [(shape((rows, block.shape[1])), vmem())],
        scratch=[pltpu.SemaphoreType.DMA],
        after=after,
    )
    return out, token


def cut(lay, arrays, axis, after, name):
    n, rows, columns = arrays[0].shape
    rows, columns = (rows // 2, columns) if axis == 1 else (rows, columns // 2)
    kind = shape((n, rows, columns))

    def spec(i):
        return pl.BlockSpec((1, rows, columns), lambda k: (k, i, 0) if axis == 1 else (k, 0, i))

    def kernel(a, b, left, right):
        left[...] = a[...]
        right[...] = b[...]

    out = pl.BlockSpec((1, rows, columns), lambda k: (k, 0, 0))
    return call(
        kernel, name, [(arrays[0], spec(0)), (arrays[1], spec(1))], [(kind, out)] * 2, grid=(n,), after=after
    )


def join(arrays, after, name):
    rows = sum(a.shape[0] for a in arrays)

    def kernel(*refs):
        at = 0
        for ref in refs[:-1]:
            refs[-1][at : at + ref.shape[0]] = ref[...]
            at += ref.shape[0]

    (out,), token = call(
        kernel, name, [(a, vmem()) for a in arrays], [(shape((rows, *arrays[0].shape[1:])), vmem())], after=after
    )
    return out, token


class Gathered:
    def __init__(self, lay, piece, axis, name, at_once):
        self.lay, self.axis, self.name = lay, axis, name
        piece = piece[None]
        if at_once:
            self.z_offsets = list(range(1, lay.R))
            self.got = [swap(piece, "row", lay.R, k) for k in self.z_offsets]
            self.bits = []
        else:
            self.bits = list(reversed(lay.row_bits))
            self.held, self.held_offsets = [piece], [0]
            self.got, self.z_offsets = [], []
            self.step()

    def step(self):
        bit = self.bits.pop(0)
        sent = self.held[0]
        self.got.append(swap(sent, "row", self.lay.R, bit))
        self.z_offsets += [o ^ bit for o in self.held_offsets]
        self.held_offsets = self.held_offsets + [o ^ bit for o in self.held_offsets]

    def double(self, after):
        token = after[0]
        while self.bits:
            self.held[0], token = join([self.held[0], self.got[-1]], (token, *after[1:]), self.name + "_double")
            self.step()
        return token

    def spread(self, after):
        lay = self.lay
        self.others, token = join(self.got, after, self.name + "_join")
        self.size = self.others.shape[self.axis]
        self.pieces = [(self.others, 0, 0, self.size)]
        for i in range(min(2, len(lay.split_bits))):
            self.pieces.append((swap(self.others, "dp", lay.Q, lay.split_bits[i]), 1 << i, 0, self.size))
        return token

    def forward(self, after):
        lay, half = self.lay, self.size // 2
        if len(lay.split_bits) < 2:
            return after[0]
        (left, right), token = cut(
            lay, [self.pieces[1][0], self.pieces[2][0]], self.axis, after, self.name
        )
        self.pieces.append((swap(left, "dp", lay.Q, lay.split_bits[1]), 3, 0, half))
        self.pieces.append((swap(right, "dp", lay.Q, lay.split_bits[0]), 3, half, half))
        for i, bit in list(enumerate(lay.split_bits))[2:]:
            self.pieces += [(swap(a, "dp", lay.Q, bit), q | 1 << i, f, n) for a, q, f, n in self.pieces]
        return token

    def sources(self, ids, refs, first=0):
        at = 0
        for _, qo, begin, size in self.pieces:
            if begin + size <= first:
                continue
            for k, zo in enumerate(self.z_offsets):
                yield refs[at].at[k], begin, size, ids[1] ^ qo, ids[0] ^ zo
            at += 1

    def arrays(self, first=0):
        return [a for a, _, begin, size in self.pieces if begin + size > first]


class Weight:
    def __init__(self, gathered, block, dims, pairs, first=0):
        self.block, self.dims, self.pairs = block, dims, pairs
        arrays = gathered.arrays(first)
        self.operands = [(a, anywhere()) for a in arrays] + [(block, anywhere())]
        self.n = len(self.operands)

        class Fake:
            def __getitem__(self, i):
                return self

            @property
            def at(self):
                return self

        fake = Fake()
        copies_n = len(list(pairs([1, 0], [fake] * self.n, fake)))
        self.scratch = [pltpu.VMEM(dims, BF), pltpu.SemaphoreType.DMA((copies_n,))]

    def copies(self, ids, refs, target, sems):
        return [
            pltpu.make_async_copy(a, b, sems.at[i])
            for i, (a, b) in enumerate(self.pairs(ids, refs, target))
        ]


def start_all(copies):
    for copy in copies:
        copy.start()


def wait_all(copies):
    for copy in copies:
        copy.wait()


def aligned(value, multiple):
    return value * multiple if isinstance(value, int) else pl.multiple_of(value * multiple, multiple)


def joint_weight_of(gathered, block):
    lay = gathered.lay
    width = block.shape[1]

    def pairs(ids, refs, target):
        for source, first, size, q, z in gathered.sources(ids, refs):
            n = min(first + size, width) - first
            rows = pl.ds(aligned(z * lay.s + q, lay.piece), lay.piece)
            yield source.at[:, :n], target.at[rows, first : first + n]
        yield refs[-1], target.at[pl.ds(aligned(ids[0], lay.block), lay.block), :]

    return Weight(gathered, block, (D, width), pairs)


def output_weight_of(gathered, block, column):
    lay = gathered.lay
    rows = block.shape[0]
    per = rows // lay.s

    def pairs(ids, refs, target):
        for source, first, _, q, z in gathered.sources(ids, refs, column):
            for b in range(per // lay.piece):
                at = column + b * lay.block - first
                yield (
                    source.at[:, at : at + lay.block],
                    target.at[
                        pl.ds(aligned(q * (per // lay.piece) + b, lay.piece), lay.piece),
                        pl.ds(aligned(z, lay.block), lay.block),
                    ],
                )
        yield refs[-1], target.at[:, pl.ds(aligned(ids[0], lay.block), lay.block)]

    return Weight(gathered, block, (rows, D), pairs, column)


def up_weight_of(gathered, block):
    lay = gathered.lay

    def pairs(ids, refs, target):
        for source, first, size, q, z in gathered.sources(ids, refs):
            rows = pl.ds(aligned(z * lay.s + q, lay.piece), lay.piece)
            yield source, target.at[rows, first : first + size]
        yield refs[-1], target.at[pl.ds(aligned(ids[0], lay.block), lay.block), :]

    return Weight(gathered, block, (D, block.shape[1]), pairs)


def down_weight_of(gathered, block):
    lay = gathered.lay
    rows = block.shape[0]
    per = rows // lay.s

    def pairs(ids, refs, target):
        for source, first, size, q, z in gathered.sources(ids, refs):
            row = aligned(q * (per // size) + first // size, size)
            yield source, target.at[pl.ds(row, size), pl.ds(aligned(z, lay.block), lay.block)]
        yield refs[-1], target.at[:, pl.ds(aligned(ids[0], lay.block), lay.block)]

    return Weight(gathered, block, (rows, D), pairs)


def weight_grad(lay, ids, sides, orders, name, after=()):
    columns = sum(r.shape[1] for _, rights in sides for r in rights)
    width = columns // len(orders)
    ins = [(ids, smem())]
    for left, rights in sides:
        ins.append((left, pl.BlockSpec((LEN, lay.block), lambda z: (0, z))))
        ins.extend((r, whole(*r.shape)) for r in rights)
    counts = [len(rights) for _, rights in sides]
    n_out = 2 * len(orders)
    out = pl.BlockSpec((lay.s // 2, lay.piece, width), lambda z: (z, 0, 0))

    def kernel(ids, *refs):
        ins, outs = refs[:-n_out], refs[-n_out:]
        parts, at = [], 0
        for n in counts:
            left = ins[at][...]
            parts.extend(dot(left, ins[at + 1 + i][...], TN).astype(BF) for i in range(n))
            at += n + 1
        block = parts[0] if len(parts) == 1 else jnp.concatenate(parts, axis=1)
        for q in range(lay.s):
            rows = block[q * lay.piece : (q + 1) * lay.piece]
            for i, order in enumerate(orders):
                keep, send, bit = outs[2 * i], outs[2 * i + 1], order[0]
                part = rows[:, i * width : (i + 1) * width]
                mine = ((ids[1] >> bit) & 1) == ((q >> bit) & 1)
                spot = ((q >> (bit + 1)) << bit) + (q & ((1 << bit) - 1))

                def to_keep(keep=keep, spot=spot, part=part):
                    keep[spot] = part

                def to_send(send=send, spot=spot, part=part):
                    send[spot] = part

                pl.when(mine)(to_keep)
                pl.when(jnp.logical_not(mine))(to_send)

    kind = shape((lay.R * lay.s // 2, lay.piece, width))
    return call(kernel, name, ins, [(kind, out)] * n_out, grid=(lay.R,), after=after)


class Small:
    def __init__(self, lay, arrays):
        self.lay = lay
        self.bits = [("dp", lay.Q, bit) for bit in lay.split_bits + lay.rest_bits]
        self.bits += [("row", lay.R, bit) for bit in lay.row_bits]
        self.value = jnp.concatenate([a.reshape(-1) for a in arrays]).reshape(-1, HDIM)
        self.send()

    def send(self):
        self.got = swap(self.value, *self.bits.pop(0))

    def add(self, after):
        def kernel(a, b, out):
            out[...] = a[...] + b[...]

        ins = [(self.value, vmem()), (self.got, vmem())]
        (self.value,), token = call(kernel, "small_sum", ins, [(shape(self.value.shape, F32), vmem())], after=after)
        return token

    def step(self, after):
        token = self.add(after)
        self.send()
        return token

    def finish(self, after):
        while self.bits:
            after = (self.step(after),)
        return self.add(after)


class Reduction:
    def __init__(self, lay, ids, orders, parts):
        self.lay, self.ids, self.orders, self.step = lay, ids, orders, 0
        k = len(lay.split_bits)
        self.left = [sorted(set(range(k)) - {order[0]}, reverse=True) for order in orders]
        self.send(parts)

    def send(self, parts):
        self.keep, self.got = list(parts[0::2]), []
        for order, part in zip(self.orders, parts[1::2]):
            self.got.append(swap(part, "dp", self.lay.Q, self.lay.split_bits[order[self.step]]))
        self.step += 1

    def advance(self, after, name, passing=()):
        lay, n = self.lay, len(self.orders)
        bits = [order[self.step] for order in self.orders]
        ins, outs = [(self.ids, smem())], []
        for i, bit in enumerate(bits):
            groups = lay.R * 2 ** self.left[i].index(bit)
            rows = 2 ** (len(self.left[i]) - 1 - self.left[i].index(bit)) * lay.piece
            width = self.keep[i].shape[-1]
            for value in (self.keep[i], self.got[i]):
                ins.append(
                    (value.reshape(groups, 2, rows, width), pl.BlockSpec((1, 2, rows, width), lambda g: (g, 0, 0, 0)))
                )
            outs += [(shape((groups, rows, width)), pl.BlockSpec((1, rows, width), lambda g: (g, 0, 0)))] * 2

        def kernel(ids, *refs):
            ins, outs = refs[: 2 * n], refs[2 * n :]
            for i, bit in enumerate(bits):
                mine = (ids[1] >> bit) & 1
                a, b = ins[2 * i], ins[2 * i + 1]
                for target, which in ((outs[2 * i], mine), (outs[2 * i + 1], 1 - mine)):
                    target[0] = (a[0, which].astype(F32) + b[0, which].astype(F32)).astype(BF)

        parts, token = call(kernel, name, ins, outs, grid=(groups,), after=after, passing=passing)
        self.left = [[b for b in left if b != bit] for left, bit in zip(self.left, bits)]
        self.send(parts[: 2 * n])
        return parts[2 * n :], token


def first_rows(reduction, after, name):
    lay, ids, n = reduction.lay, reduction.ids, len(reduction.orders)
    ins = [(ids, smem())]
    width = reduction.keep[0].shape[-1]
    for i in range(n):
        for value in (reduction.keep[i], reduction.got[i]):
            value = value.reshape(lay.R // 2, 2, lay.piece, width)
            ins.append((value, pl.BlockSpec((1, 2, lay.piece, width), lambda g: (g, 0, 0, 0))))
    out = pl.BlockSpec((1, lay.piece, n * width), lambda g: (g, 0, 0))

    def kernel(ids, *refs):
        ins, (keep, send) = refs[:-2], refs[-2:]
        mine = ids[0] & 1
        for target, bit in ((keep, mine), (send, 1 - mine)):
            for i in range(n):
                a, b = ins[2 * i], ins[2 * i + 1]
                target[0, :, i * width : (i + 1) * width] = (a[0, bit].astype(F32) + b[0, bit].astype(F32)).astype(BF)

    kind = shape((lay.R // 2, lay.piece, n * width))
    (keep, send), token = call(kernel, name, ins, [(kind, out)] * 2, grid=(lay.R // 2,), after=after)
    return (keep, swap(send, "row", lay.R, 1)), token


def next_rows(lay, ids, pair, after, name):
    token = after[0]
    for i, bit in list(enumerate(lay.row_bits))[1:]:
        keep, got = pair
        groups = keep.shape[0] // 2
        columns = keep.shape[-1]
        ins = [(ids, smem())]
        for value in pair:
            value = value.reshape(groups, 2, lay.piece, columns)
            ins.append((value, pl.BlockSpec((1, 2, lay.piece, columns), lambda g: (g, 0, 0, 0))))
        out = pl.BlockSpec((1, lay.piece, columns), lambda g: (g, 0, 0))

        def kernel(ids, a, b, keep, send, i=i):
            mine = (ids[0] >> i) & 1
            for target, which in ((keep, mine), (send, 1 - mine)):
                target[0] = (a[0, which].astype(F32) + b[0, which].astype(F32)).astype(BF)

        kind = shape((groups, lay.piece, columns))
        (keep, send), token = call(kernel, name, ins, [(kind, out)] * 2, grid=(groups,), after=(token, *after[1:]))
        pair = (keep, swap(send, "row", lay.R, bit))
    return pair, token


def row_total(lay, pair, after, name, ready=(), passing=()):
    width = pair[0].shape[-1]
    columns = width + sum(r.shape[1] for r in ready)

    def kernel(*refs):
        (*others, a, b), out = refs[:-1], refs[-1]
        column = 0
        for ref in others:
            out[:, column : column + ref.shape[1]] = ref[...]
            column += ref.shape[1]
        out[:, column:] = (a[...].astype(F32) + b[...].astype(F32)).astype(BF)

    (total, *passed), token = call(
        kernel,
        name,
        [(v, vmem()) for v in ready] + [(v.reshape(lay.piece, width), vmem()) for v in pair],
        [(shape((lay.piece, columns)), vmem())],
        after=after,
        passing=passing,
    )
    return (total, *passed), token


def rest_sum(lay, total):
    for bit in lay.rest_bits:
        total = (total.astype(F32) + swap(total, "dp", lay.Q, bit).astype(F32)).astype(BF)
    return total


def spread(lay, total):
    got = [total]
    for offset in range(1, lay.s):
        mask = sum(bit for i, bit in enumerate(lay.split_bits) if (offset >> i) & 1)
        got.append(swap(total, "dp", lay.Q, mask))
    return got


def finish(lay, ids, pieces, plan, name, after=()):
    outs = []
    for spans, transposed in plan:
        n = sum(c for _, c in spans)
        outs.append((shape((n, lay.block) if transposed else (lay.block, n), F32), vmem()))
    widest = max([HDIM] + [sum(c for _, c in spans) for spans, t in plan if t])

    def kernel(ids, *refs):
        ins, results, scratch = refs[: lay.s], refs[lay.s : -1], refs[-1]
        for (spans, transposed), result in zip(plan, results):
            column = 0
            for first, n in spans:
                for offset in range(lay.s):
                    rows = pl.ds(aligned(ids[1] ^ offset, lay.piece), lay.piece)
                    value = ins[offset][:, first : first + n].astype(F32)
                    if transposed:
                        scratch[rows, column : column + n] = value
                    else:
                        result[rows, column : column + n] = value
                column += n
            if transposed:
                result[...] = scratch[:, :column].T

    return call(
        kernel,
        name,
        [(ids, smem())] + [(p, vmem()) for p in pieces],
        outs,
        scratch=[pltpu.VMEM((lay.block, widest), F32)],
        after=after,
        mib=18,
    )


def both(own, other):
    return jnp.concatenate([own, other], axis=1)


def row_stats(values):
    average = jnp.mean(values, axis=1, keepdims=True)
    square = jnp.mean(values * values, axis=1, keepdims=True)
    return average, lax.rsqrt(square - average * average + EPSILON)


def norm_grad(gradient, centered, factor, gain):
    scaled = gradient * gain
    first = jnp.mean(scaled, axis=1, keepdims=True)
    second = jnp.mean(scaled * centered, axis=1, keepdims=True)
    return factor * (scaled - first - centered * second)


V_GAIN1, V_SHIFT1, V_GAIN2, V_SHIFT2, V_OBIAS = range(5)


def pair_row(own_ref, other_ref, i):
    return both(own_ref[i : i + 1, :], other_ref[i : i + 1, :])


def branch_sum(own, other):
    return own[...].astype(F32) + both(other[:, HALF:], other[:, :HALF]).astype(F32)


def pair_up(pairs, after):
    def kernel(*refs):
        n = len(pairs)
        for i in range(n):
            refs[2 * n + i][:, :HALF] = refs[2 * i][...]
            refs[2 * n + i][:, HALF:] = refs[2 * i + 1][...]

    return call(
        kernel,
        "pair_up",
        [(v, row_tile(HALF)) for pair in pairs for v in pair],
        [(shape((LEN, D)), row_tile(D))] * len(pairs),
        grid=ROW_GRID,
        after=after,
    )


def first_norm_project(ids, x, vecs, bias, joint, after):
    width = bias.shape[1]

    def kernel(ids, x_ref, vo, vt, bias, *refs):
        pieces, full, qkv, weight, sems = refs[: joint.n], *refs[joint.n :]
        copies = joint.copies(ids, pieces, weight, sems)
        first = pl.program_id(0) == 0
        pl.when(first)(lambda: start_all(copies))
        values = x_ref[...].astype(F32)
        average, factor = row_stats(values)
        normed = (values - average) * factor * pair_row(vo, vt, V_GAIN1) + pair_row(vo, vt, V_SHIFT1)
        low = normed.astype(BF)
        full[...] = low
        pl.when(first)(lambda: wait_all(copies))
        qkv[...] = (dot(low, weight[...]) + bias[...]).astype(BF)

    return call(
        kernel,
        "first_norm_project",
        [(ids, smem()), (x, row_tile(D)), *[(v, whole(8, HALF)) for v in vecs], (bias, whole(1, width))]
        + joint.operands,
        [(hbm((LEN, D)), row_tile(D)), (shape((LEN, width)), row_tile(width))],
        grid=ROW_GRID,
        scratch=joint.scratch,
        after=after,
    )


def visible_mask(lo, rows, queries, prefix):
    key_id = lax.broadcasted_iota(jnp.int32, (rows, queries), 0) + lo
    query_id = lax.broadcasted_iota(jnp.int32, (rows, queries), 1) + lo
    return (key_id <= query_id) | (key_id < prefix)


def attend(prefix_ref, qkv_ref, out_ref, log_ref):
    bq = 512
    prefix_end = prefix_ref[0]
    for h in range(log_ref.shape[0]):
        base = h * 3 * HDIM
        keys = qkv_ref[:, base + HDIM : base + 2 * HDIM]
        values_t = qkv_ref[:, base + 2 * HDIM : base + 3 * HDIM].T
        for lo in range(0, LEN, bq):
            n = max(MAX_PREFIX, lo + bq)
            query = qkv_ref[lo : lo + bq, base : base + HDIM]
            scores = dot(keys[:n], query, NT)
            tail = jnp.where(visible_mask(lo, n - lo, bq, prefix_end), scores[lo:], NEGATIVE)
            scores = tail if lo == 0 else jnp.concatenate([scores[:lo], tail], axis=0)
            top = jnp.max(scores, axis=0, keepdims=True) * (SCALE * LOG2E)
            weights = jnp.exp2(scores * (SCALE * LOG2E) - top)
            total = jnp.sum(weights, axis=0, keepdims=True)
            mixed = dot(values_t[:, :n], weights.astype(BF)) * (1.0 / total)
            out_ref[lo : lo + bq, h * HDIM : (h + 1) * HDIM] = mixed.T.astype(BF)
            log_ref[h, :, lo : lo + bq] = top + jnp.log2(total)


def attention_first(prefix, qkv, heads, after):
    return call(
        attend,
        "attention_first",
        [(prefix, smem()), (qkv, pl.BlockSpec((LEN, 3 * HDIM * heads), lambda i: (0, 0)))],
        [
            (shape((LEN, HDIM * heads)), whole(LEN, HDIM * heads)),
            (shape((heads, 1, LEN), F32), whole(heads, 1, LEN)),
        ],
        grid=(1,),
        after=after,
    )


def attention_second(ids, prefix, qkv, heads, attended_first, output, after):
    width = HDIM * heads

    def kernel(ids, prefix_ref, qkv_ref, first_ref, *refs):
        pieces, (out_ref, log_ref, branch, weight, sems) = refs[: output.n], refs[output.n :]
        copies = output.copies(ids, pieces, weight, sems)
        start_all(copies)
        attend(prefix_ref, qkv_ref, out_ref, log_ref)
        wait_all(copies)
        for lo in range(0, LEN, TILE):
            rows = slice(lo, lo + TILE)
            branch[rows, :] = dot(both(first_ref[rows, :], out_ref[rows, :]), weight[...]).astype(BF)

    return call(
        kernel,
        "attention_second",
        [(ids, smem()), (prefix, smem()), (qkv, pl.BlockSpec((LEN, 3 * HDIM * heads), lambda i: (0, 1))),
         (attended_first, whole(LEN, width))]
        + output.operands,
        [
            (shape((LEN, width)), whole(LEN, width)),
            (shape((heads, 1, LEN), F32), whole(heads, 1, LEN)),
            (shape((LEN, D)), whole(LEN, D)),
        ],
        grid=(1,),
        scratch=output.scratch,
        after=after,
    )


def second_norm_up(ids, x, parts, vecs, bias, up, after):
    width = bias.shape[1]

    def kernel(ids, x_ref, po, pt, vo, vt, bias, *refs):
        pieces = refs[: up.n]
        residual, centered, factor_ref, full, active, slope, weight, sems = refs[up.n :]
        copies = up.copies(ids, pieces, weight, sems)
        first = pl.program_id(0) == 0
        pl.when(first)(lambda: start_all(copies))
        res = x_ref[...].astype(F32) + (branch_sum(po, pt) + pair_row(vo, vt, V_OBIAS))
        residual[...] = res[:, :HALF]
        average, factor = row_stats(res)
        cent = (res - average) * factor
        centered[...] = cent.astype(BF)
        factor_ref[...] = factor
        low = (cent * pair_row(vo, vt, V_GAIN2) + pair_row(vo, vt, V_SHIFT2)).astype(BF)
        full[...] = low
        pl.when(first)(lambda: wait_all(copies))
        hidden = dot(low, weight[...]) + bias[...]
        bell = jnp.exp(-0.5 * hidden * hidden) * (1.0 / math.sqrt(2.0 * math.pi))
        phi = 0.5 * (1.0 + lax.erf(hidden * 2.0**-0.5))
        active[...] = (hidden * phi).astype(BF)
        slope[...] = (phi + hidden * bell).astype(BF)

    return call(
        kernel,
        "second_norm_up",
        [(ids, smem()), (x, row_tile(D)), *[(p, row_tile(D)) for p in parts], *[(v, whole(8, HALF)) for v in vecs],
         (bias, whole(1, width))]
        + up.operands,
        [
            (hbm((LEN, HALF), F32), row_tile(HALF)),
            (hbm((LEN, D)), row_tile(D)),
            (hbm((LEN, 1), F32), row_tile(1)),
            (hbm((LEN, D)), row_tile(D)),
            (shape((LEN, width)), row_tile(width)),
            (shape((LEN, width)), row_tile(width)),
        ],
        grid=ROW_GRID,
        scratch=up.scratch,
        after=after,
    )


def hidden_backward(ids, cot, slope, up, down, after):
    width = slope.shape[1]

    def kernel(ids, cot_ref, slope_ref, *refs):
        up_pieces, refs = refs[: up.n], refs[up.n :]
        down_pieces, refs = refs[: down.n], refs[down.n :]
        hidden_grad, partial, bias_grad, up_full, up_sems, down_full, down_sems = refs
        down_copies = down.copies(ids, down_pieces, down_full, down_sems)
        up_copies = up.copies(ids, up_pieces, up_full, up_sems)
        first = pl.program_id(0) == 0

        def begin():
            start_all(down_copies)
            start_all(up_copies)
            bias_grad[...] = jnp.zeros_like(bias_grad)
            wait_all(down_copies)

        pl.when(first)(begin)
        grad = dot(cot_ref[...], down_full[...], NT) * slope_ref[...].astype(F32)
        low = grad.astype(BF)
        hidden_grad[...] = low
        bias_grad[...] += jnp.sum(low.astype(F32), axis=0, keepdims=True)
        pl.when(first)(lambda: wait_all(up_copies))
        partial[...] = dot(low, up_full[...], NT).astype(BF)

    return call(
        kernel,
        "hidden_backward",
        [(ids, smem()), (cot, row_tile(D)), (slope, row_tile(width))] + up.operands + down.operands,
        [(hbm((LEN, width)), row_tile(width)), (shape((LEN, D)), row_tile(D)), (shape((1, width), F32), whole(1, width))],
        grid=ROW_GRID,
        scratch=up.scratch + down.scratch,
        after=after,
    )


def second_norm_backward(ids, cot, parts, centered, factor, vecs, output, after):
    width = output.dims[0]

    def kernel(ids, cot_ref, po, pt, cent_ref, factor_ref, vo, vt, *refs):
        pieces, (branch, res_grad, att_grad, sums_ref, weight, sems) = refs[: output.n], refs[output.n :]
        copies = output.copies(ids, pieces, weight, sems)
        first = pl.program_id(0) == 0

        def begin():
            start_all(copies)
            sums_ref[...] = jnp.zeros_like(sums_ref)

        pl.when(first)(begin)
        grad = branch_sum(po, pt)
        cent = cent_ref[...].astype(F32)
        cot = cot_ref[...].astype(F32)
        total = cot + norm_grad(grad, cent, factor_ref[...], pair_row(vo, vt, V_GAIN2))
        low = total.astype(BF)
        branch[...] = low
        res_grad[...] = total[:, :HALF]
        news = (grad[:, :HALF] * cent[:, :HALF], grad[:, :HALF], low[:, :HALF].astype(F32), cot[:, :HALF])
        for i, value in enumerate(news):
            sums_ref[i : i + 1, :] += jnp.sum(value, axis=0, keepdims=True)
        pl.when(first)(lambda: wait_all(copies))
        att_grad[...] = dot(low, weight[...], NT).astype(BF)

    return call(
        kernel,
        "second_norm_backward",
        [(ids, smem()), (cot, row_tile(D)), *[(p, row_tile(D)) for p in parts], (centered, row_tile(D)),
         (factor, row_tile(1)), *[(v, whole(8, HALF)) for v in vecs]]
        + output.operands,
        [
            (shape((LEN, D)), row_tile(D)),
            (shape((LEN, HALF), F32), row_tile(HALF)),
            (shape((LEN, width)), row_tile(width)),
            (shape((4, HALF), F32), whole(4, HALF)),
        ],
        grid=ROW_GRID,
        scratch=output.scratch,
        after=after,
    )


def attention_backward(prefix, qkv, grads, logs, attended, first_head, heads, after):
    bq = 256

    def kernel(prefix_ref, qkv_ref, grad_ref, log_ref, att_ref, out_ref, sums_ref, key_sum, value_sum):
        prefix_end = prefix_ref[0]
        keys = qkv_ref[:, HDIM : 2 * HDIM]
        values = qkv_ref[:, 2 * HDIM : 3 * HDIM]
        keys_t = keys.T
        query_total = jnp.zeros((1, HDIM), F32)
        for lo in reversed(range(0, LEN, bq)):
            n = max(MAX_PREFIX, lo + bq)
            query = qkv_ref[lo : lo + bq, 0:HDIM]
            grad = grad_ref[lo : lo + bq, :]
            scores = dot(keys[:n], query, NT) * (SCALE * LOG2E)
            weights = jnp.exp2(scores - log_ref[0, :, lo : lo + bq])
            tail = jnp.where(visible_mask(lo, n - lo, bq, prefix_end), weights[lo:], 0.0)
            weights = tail if lo == 0 else jnp.concatenate([weights[:lo], tail], axis=0)
            weight_grad_t = dot(values[:n], grad, NT)
            mixed = grad.astype(F32) * att_ref[lo : lo + bq, :].astype(F32)
            delta = jnp.sum(mixed.T, axis=0, keepdims=True)
            score_grad = (weights * (weight_grad_t - delta)).astype(BF)
            value_part = dot(weights.astype(BF), grad)
            key_part = dot(score_grad, query)
            if lo + bq == LEN:
                value_sum[...] = value_part
                key_sum[...] = key_part
            else:
                value_sum[:n, :] += value_part
                key_sum[:n, :] += key_part
            query_part = (dot(keys_t[:, :n], score_grad).T * SCALE).astype(BF)
            out_ref[lo : lo + bq, 0:HDIM] = query_part
            query_total = query_total + jnp.sum(query_part.astype(F32), axis=0, keepdims=True)
        out_ref[:, HDIM : 2 * HDIM] = (key_sum[...] * SCALE).astype(BF)
        value_low = value_sum[...].astype(BF)
        out_ref[:, 2 * HDIM : 3 * HDIM] = value_low
        sums_ref[0] = both(query_total, jnp.sum(value_low.astype(F32), axis=0, keepdims=True))

    return call(
        kernel,
        "attention_backward",
        [
            (prefix, smem()),
            (qkv, pl.BlockSpec((LEN, 3 * HDIM), lambda h: (0, h + first_head))),
            (grads, pl.BlockSpec((LEN, HDIM), lambda h: (0, h + first_head))),
            (logs, pl.BlockSpec((1, 1, LEN), lambda h: (h, 0, 0))),
            (attended, pl.BlockSpec((LEN, HDIM), lambda h: (0, h))),
        ],
        [
            (shape((LEN, 3 * HDIM * heads)), pl.BlockSpec((LEN, 3 * HDIM), lambda h: (0, h))),
            (shape((heads, 1, 2 * HDIM), F32), pl.BlockSpec((1, 1, 2 * HDIM), lambda h: (h, 0, 0))),
        ],
        grid=(heads,),
        scratch=[pltpu.VMEM((LEN, HDIM), F32), pltpu.VMEM((LEN, HDIM), F32)],
        after=after,
    )


def project_backward(ids, grads, x, vecs, joint, after):
    widths = [g.shape[1] for g in grads]

    def kernel(ids, x_ref, vo, vt, *refs):
        grad_refs, refs = refs[: len(grads)], refs[len(grads) :]
        pieces, (own, other, sums, weight, sems) = refs[: joint.n], refs[joint.n :]
        copies = joint.copies(ids, pieces, weight, sems)
        first = pl.program_id(0) == 0
        pl.when(first)(lambda: start_all(copies))
        values = x_ref[...].astype(F32)
        average, factor = row_stats(values)
        pl.when(first)(lambda: wait_all(copies))
        total, column = 0.0, 0
        for ref, width in zip(grad_refs, widths):
            total = total + dot(ref[...], weight[:, column : column + width], NT)
            column += width
        own[...] = total[:, :HALF].astype(BF)
        other[:, :HALF] = total[:, HALF:].astype(BF)
        scaled = total * pair_row(vo, vt, V_GAIN1)
        lane = lax.broadcasted_iota(jnp.int32, (TILE, HDIM), 1)
        packed = jnp.zeros((TILE, HDIM), F32)
        parts = jnp.zeros((TILE, HDIM), F32)
        for i, value in enumerate((scaled, scaled * ((values - average) * factor))):
            row_sum = jnp.sum(value, axis=1, keepdims=True)
            high = row_sum.astype(BF).astype(F32)
            packed = jnp.where(lane == 2 * i, high, jnp.where(lane == 2 * i + 1, row_sum - high, packed))
            parts = jnp.where(lane == i, row_sum, parts)
        other[:, HALF:] = packed.astype(BF)
        sums[...] = parts

    return call(
        kernel,
        "project_backward",
        [(ids, smem()), (x, row_tile(D)), *[(v, whole(8, HALF)) for v in vecs]]
        + [(g, row_tile(g.shape[1])) for g in grads]
        + joint.operands,
        [
            (shape((LEN, HALF)), row_tile(HALF)),
            (shape((LEN, HALF + HDIM)), row_tile(HALF + HDIM)),
            (shape((LEN, HDIM), F32), row_tile(HDIM)),
        ],
        grid=ROW_GRID,
        scratch=joint.scratch,
        after=after,
    )


def down_project(ids, active, down, after):
    def kernel(ids, a_ref, *refs):
        pieces, (own, other, weight, sems) = refs[: down.n], refs[down.n :]
        copies = down.copies(ids, pieces, weight, sems)

        def begin():
            start_all(copies)
            wait_all(copies)

        pl.when(pl.program_id(0) == 0)(begin)
        value = dot(a_ref[...], weight[...]).astype(BF)
        own[...] = value[:, :HALF]
        other[...] = value[:, HALF:]

    return call(
        kernel,
        "down_project",
        [(ids, smem()), (active, row_tile(active.shape[1]))] + down.operands,
        [(shape((LEN, HALF)), row_tile(HALF))] * 2,
        grid=ROW_GRID,
        scratch=down.scratch,
        after=after,
    )


def first_norm_backward(x, own, other, sums, vecs, res_grad, after):
    def kernel(x_ref, po, pt, so, vo, res_ref, out, sums_ref):
        pl.when(pl.program_id(0) == 0)(lambda: sums_ref.__setitem__(..., jnp.zeros_like(sums_ref)))
        values = x_ref[...].astype(F32)
        average, factor = row_stats(values)
        cent = (values[:, :HALF] - average) * factor
        grad = po[...].astype(F32) + pt[:, :HALF].astype(F32)
        got = pt[:, HALF:].astype(F32)
        first = (so[:, 0:1] + (got[:, 0:1] + got[:, 1:2])) * (1.0 / D)
        second = (so[:, 1:2] + (got[:, 2:3] + got[:, 3:4])) * (1.0 / D)
        back = factor * (grad * vo[V_GAIN1 : V_GAIN1 + 1, :] - first - cent * second)
        out[...] = (res_ref[...] + back).astype(BF)
        for i, value in enumerate((grad * cent, grad)):
            sums_ref[i : i + 1, :] += jnp.sum(value, axis=0, keepdims=True)

    return call(
        kernel,
        "first_norm_backward",
        [(x, row_tile(D)), (own, row_tile(HALF)), (other, row_tile(HALF + HDIM)), (sums, row_tile(HDIM)),
         (vecs[0], whole(8, HALF)), (res_grad, row_tile(HALF))],
        [(shape((LEN, HALF)), row_tile(HALF)), (shape((2, HALF), F32), whole(2, HALF))],
        grid=ROW_GRID,
        after=after,
    )


def layer(lay, tokens_in, cotangent, prefix_length, first_gain, first_shift, joint_weight, joint_bias,
          output_weight, output_bias, second_gain, second_shift, up_weight, up_bias, down_weight, down_bias):
    heads = joint_bias.shape[0] // (2 * HDIM)
    ids = device_ids(lay)

    j_width, o_rows, ff = joint_weight.shape[1], output_weight.shape[0], down_weight.shape[0]
    per = o_rows // lay.s
    jo_piece = own_pieces(
        ids, [(joint_weight, lay.piece, 0), *[(output_weight, per, b * lay.piece) for b in range(per // lay.piece)]], lay.piece
    )
    jo = Gathered(lay, jo_piece, 2, "joint_pieces", True)

    zero_row = jnp.zeros_like(first_gain)
    vec_own = jnp.stack(
        [first_gain, first_shift, second_gain, second_shift, output_bias, zero_row, zero_row, zero_row]
    )
    vecs = (vec_own, swap_cores(vec_own))
    bias_rows = joint_bias.reshape(heads, 2, HDIM)
    joint_row = jnp.stack([bias_rows[:, 0], jnp.zeros_like(bias_rows[:, 0]), bias_rows[:, 1]], axis=1).reshape(1, -1)
    (x, cot), token = pair_up(
        [(tokens_in, swap_cores(tokens_in)), (cotangent, swap_cores(cotangent))], (*vecs, joint_row)
    )

    token = jo.spread((token,))
    up_piece, up_token = extract(lay, ids, up_weight, lay.piece, (token,))
    up = Gathered(lay, up_piece, 2, "up_pieces", False)
    token = up.double((up_token,))
    token = jo.forward((token,))
    down_piece, down_token = extract(lay, ids, down_weight, ff // lay.s, (token, *up.got))
    down = Gathered(lay, down_piece, 1, "down_pieces", False)
    token = up.spread((token, *jo.arrays()))
    joint_w = joint_weight_of(jo, joint_weight)
    output_w = output_weight_of(jo, output_weight, j_width)

    (full_one, qkv), token = first_norm_project(
        ids, x, vecs, joint_row, joint_w, (up.others, down_token)
    )
    pair = heads // 2
    token = down.double((token,))
    (attended_a, logs_a), token = attention_first(prefix_length, qkv, pair, (token,))
    token = up.forward((token,))
    up_w = up_weight_of(up, up_weight)
    (attended_b, logs_b, branch), token = attention_second(
        ids, prefix_length, qkv, pair, attended_a, output_w, (token,)
    )
    token = down.spread((token,))
    (branch,), token = hold([branch], (token, *up.arrays()), "hold_branch")
    (residual, centered, factor, full_two, active, slope), token = second_norm_up(
        ids, x, (branch, swap_cores(branch)), vecs, up_bias.reshape(1, -1), up_w, (token,)
    )
    token = down.forward((token,))
    down_w = down_weight_of(down, down_weight)
    both_orders = [lay.order_a, lay.order_b]
    later_steps = range(len(lay.split_bits) - 1)
    down_parts, token = weight_grad(lay, ids, [(cot, [active])], both_orders, "down_grad", (token,))
    down_parts, token = hold(down_parts, (token, *down.arrays()), "hold_down")
    down_red = Reduction(lay, ids, both_orders, down_parts)

    (hidden_grad, norm_part, up_bias_grad), token = hidden_backward(ids, cot, slope, up_w, down_w, (token,))
    passed, token = weight_grad(lay, ids, [(full_two, [hidden_grad])], both_orders, "up_grad", (token,))
    passed = [norm_part, *passed]
    for _ in later_steps:
        passed, token = down_red.advance((token,), "down_sum", passed)
    norm_part, *up_parts = passed
    up_red = Reduction(lay, ids, both_orders, up_parts)
    norm_parts = (norm_part, swap_cores(norm_part))
    (branch_grad, res_grad, att_grad, sums_two), token = second_norm_backward(
        ids, cot, norm_parts, centered, factor, vecs, output_w, (token,)
    )
    (qkv_grad_a, joint_sums_a), token = attention_backward(
        prefix_length, qkv, att_grad, logs_a, attended_a, 0, pair, (token,)
    )
    (qkv_grad_b, joint_sums_b), token = attention_backward(
        prefix_length, qkv, att_grad, logs_b, attended_b, pair, pair, (token,)
    )
    down_rows, token = first_rows(down_red, (token,), "down_rows")
    parts_a, token = weight_grad(
        lay, ids, [(full_one, [qkv_grad_a]), (branch_grad, [attended_a, attended_b])], [lay.order_a],
        "joint_grad_a", (token,),
    )
    red_a = Reduction(lay, ids, [lay.order_a], parts_a)
    parts_b, token = weight_grad(lay, ids, [(full_one, [qkv_grad_b])], [lay.order_b], "joint_grad_b", (token,))
    red_b = Reduction(lay, ids, [lay.order_b], parts_b)
    for _ in later_steps:
        _, token = up_red.advance((token,), "up_sum")
    down_rows, token = next_rows(lay, ids, down_rows, (token,), "down_rows_2")
    (first_own, first_send, row_sums), token = project_backward(
        ids, [qkv_grad_a, qkv_grad_b], x, vecs, joint_w, (token,)
    )
    (down_total, first_send), token = row_total(lay, down_rows, (token,), "down_total", (), [first_send])
    first_got = swap_cores(first_send)
    (down_own, down_send), token = down_project(ids, active, down_w, (token,))
    up_rows, token = first_rows(up_red, (token,), "up_rows")
    for _ in later_steps:
        _, token = red_b.advance((token,), "joint_sum_b")
    for _ in later_steps:
        _, token = red_a.advance((token,), "joint_sum_a")
    (tokens_grad, sums_one), token = first_norm_backward(
        x, first_own, first_got, row_sums, vecs, res_grad, (token,)
    )
    small = Small(lay, (sums_one, sums_two, joint_sums_a, joint_sums_b, up_bias_grad))
    up_rows, token = next_rows(lay, ids, up_rows, (token,), "up_rows_2")
    rows_b, token = first_rows(red_b, (token,), "joint_rows_b")
    (ffn_total,), token = row_total(lay, up_rows, (token,), "up_total", [down_total])
    ffn_pieces = spread(lay, rest_sum(lay, ffn_total))
    token = small.step((token,))
    rows_a, token = first_rows(red_a, (token,), "joint_rows_a")
    token = small.step((token,))
    rows_b, token = next_rows(lay, ids, rows_b, (token,), "joint_rows_b_2")
    rows_a, token = next_rows(lay, ids, rows_a, (token,), "joint_rows_a_2")

    layer_out = (
        residual + (down_own.astype(F32) + swap_cores(down_send).astype(F32) + down_bias[None, :])
    ).astype(BF)
    token = small.step((token,))
    (total_b,), token = row_total(lay, rows_b, (token,), "joint_total_b")
    (joint_total,), token = row_total(lay, rows_a, (token,), "joint_total_a", [total_b])
    joint_pieces = spread(lay, rest_sum(lay, joint_total))
    token = small.finish((token,))
    small = small.value.reshape(-1)
    (grad_down, grad_up), token = finish(
        lay, ids, ffn_pieces, [([(0, ff)], True), ([(ff, ff)], False)], "finish_ffn", (token,)
    )
    mid = j_width // 2
    (grad_joint, grad_output), token = finish(
        lay,
        ids,
        joint_pieces,
        [([(mid, mid), (0, mid)], False), ([(2 * mid, o_rows)], True)],
        "finish_attention",
        (token,),
    )

    def take(start, n):
        return lax.slice_in_dim(small, start, start + n, axis=0)

    joint_n = joint_bias.shape[0]
    return (
        layer_out,
        tokens_grad,
        take(0, HALF),
        take(HALF, HALF),
        grad_joint,
        take(6 * HALF, joint_n),
        grad_output,
        take(4 * HALF, HALF),
        take(2 * HALF, HALF),
        take(3 * HALF, HALF),
        grad_up,
        take(6 * HALF + joint_n, up_bias.shape[0]),
        grad_down,
        take(5 * HALF, HALF),
    )


def solution(mesh):
    lay = Layout(mesh)
    vec, rows, cols, flat = P("col"), P("row", "col"), P("col", "row"), P(("dp", "row"), "col")

    def shards(*args):
        return layer(lay, *args)

    return jax.shard_map(
        shards,
        mesh=mesh,
        in_specs=(flat, flat, P(("dp", "row")), vec, vec, rows, vec, cols, vec, vec, vec, rows, vec, cols, vec),
        out_specs=(flat, flat, vec, vec, rows, vec, cols, vec, vec, vec, rows, vec, cols, vec),
        check_vma=False,
    )
```

time: 1090 us -> 314 us (0.29)
  waiting for transfers between devices: 736 us -> 123 us
  Pallas kernels: 0 us -> 118 us
  matrix products: 117 us -> 0 us
  blocking collectives: 107 us -> 0 us
  starting transfers between devices: 1.11 us -> 53.1 us
  other arithmetic: 51.7 us -> 2.42 us
  local copies, waits for them, and re-layouts: 52.1 us -> 14.6 us
  between operations: 15.2 us -> 1.91 us
    reduce_scatter x8 -> x0, waiting for transfers between devices: 482 us -> none  [the longest x1 180 us: shards(): lax.psum_scatter(reorder(grad_up_weight, 0), ('dp', 'row'), scatter_dimen...]
    all_gather x10 -> x0, waiting for transfers between devices: 250 us -> none  [the longest x2 141 us: rows_forward(): lax.all_gather(weight, 'row', axis=0, tiled=True)]
    ppermute x0 -> x56, waiting for transfers between devices: none -> 123 us  [the longest x49 121 us: swap(): return lax.ppermute(value, axis, [(i, i ^ bit) for i in range(size)])]
    pallas_call x0 -> x50, Pallas kernels: none -> 118 us  [call(): pl.pallas_call(body, grid=grid, in_specs=[spec for _, spec in ins] + [any...]
    dot_general x26 -> x0, matrix products: 117 us -> none  [the longest x4 21.9 us: contract_rows(): lax.dot_general(left_side, right_side, (((0,), (0,)), ((), ())), preferre...]
    psum x5 -> x0, blocking collectives: 87.9 us -> none  [the longest x1 77.4 us: shards(): lax.psum((grad_first_gain, grad_first_shift, grad_joint_bias, grad_output...]
    ppermute x0 -> x56, starting transfers between devices: none -> 53.1 us  [the longest x49 51.9 us: swap(): return lax.ppermute(value, axis, [(i, i ^ bit) for i in range(size)])]
    convert_element_type x14 -> x1, other arithmetic: 25.5 us -> 1.54 us  [layer(): layer_out = (residual + (down_own.astype(F32) + swap_cores(down_send).ast...]
  transfers between devices with their start and end apart: 18 -> 56, of which waited for: 12 -> 31; matrix products, arithmetic and copies ran while one was open for 17% -> 2% of each run, Pallas kernels for 0% -> 36%
where the time goes in v2:
time: 314 us; the launch traced here: 313 us
  waiting for transfers between devices  123 us (39%)
  Pallas kernels  118 us (38%)
  starting transfers between devices  53.1 us (17%)
  local copies, waits for them, and re-layouts  14.6 us (5%)
    ppermute x49, waiting for transfers between devices, swap(): return lax.ppermute(value, axis, [(i, i ^ bit) for i in range(size)])  121 us
    pallas_call x50, Pallas kernels, call(): pl.pallas_call(body, grid=grid, in_specs=[spec for _, spec in ins] + [any...  118 us
    ppermute x49, starting transfers between devices, swap(): return lax.ppermute(value, axis, [(i, i ^ bit) for i in range(size)])  51.9 us
    unnamed x44, local copies, waits for them, and re-layouts  9.41 us
  transfers between devices with their start and end apart: 56, of which 31 were waited for; matrix products, arithmetic and copies ran while one was open for 2% of the time, Pallas kernels for 36%

profile of v2, /device:TPU:0, one launch (start us, length us, event | category | flops | bytes accessed | tf_op | source)
XLA Modules:
  0.0 313.1 jit_solution(1400705632875034283)
XLA Ops:
  5.0 4.7 %collective-permute-start.5 = (bf16[1,64,2048]{2,1,0:T(8,128)(2,1)}, bf16[1,64,2048]{2,1,0:T(8,128)(2,1)S(1)}, u32[]{:S(2)}, u32[]{:S(2)}) collective-permute-start(bf16[1,64,2048]{2,1,0:T(8,128)(2,1)} %maximum_bitcast_fusion), channel_id=1, source_target_pairs={{0,6},{2,4},{4,2},{6,0},{1,7},{3,5},{5,3},{7,1},{8,14},{10,12},{12... | collective-permute-start | bytes 786440 | tf_op jit(solution)/shard_map/ppermute | solution.py:83
  17.5 15.4 %collective-permute-done.4.refs_1_ = bf16[1,64,2048]{2,1,0:T(8,128)(2,1)} collective-permute-done((bf16[1,64,2048]{2,1,0:T(8,128)(2,1)}, bf16[1,64,2048]{2,1,0:T(8,128)(2,1)}, u32[]{:S(2)}, u32[]{:S(2)}) %collective-permute-start.4) | collective-permute-done | bytes 262176 | tf_op jit(solution)/shard_map/ppermute | solution.py:83
  39.8 13.7 %collective-permute-done.8.refs_1_.refs_3_.refs_0_ = bf16[1,64,2048]{2,1,0:T(8,128)(2,1)S(1)} collective-permute-done((bf16[1,64,2048]{2,1,0:T(8,128)(2,1)S(1)}, bf16[1,64,2048]{2,1,0:T(8,128)(2,1)S(1)}, u32[]{:S(2)}, u32[]{:S(2)}) %collective-permute-start.8) | collective-permute-done | bytes 262176 | tf_op jit(solution)/shard_map/ppermute | solution.py:83
  59.5 7.9 %collective-permute-done.9.refs_4_.refs_1_ = bf16[2,64,2048]{2,1,0:T(8,128)(2,1)S(1)} collective-permute-done((bf16[2,64,2048]{2,1,0:T(8,128)(2,1)S(1)}, bf16[2,64,2048]{2,1,0:T(8,128)(2,1)S(1)}, u32[]{:S(2)}, u32[]{:S(2)}) %collective-permute-start.9) | collective-permute-done | bytes 524320 | tf_op jit(solution)/shard_map/ppermute | solution.py:83
  71.3 7.3 %first_norm_project.1 = (bf16[1024,1024]{1,0:T(8,128)(2,1)}, bf16[1024,1536]{1,0:T(8,128)(2,1)S(1)}, f32[8,128]{1,0:T(8,128)S(1)}) custom-call(s32[3]{0:T(128)S(1)} %pad_add_fusion.refs_0_, bf16[1024,1024]{1,0:T(8,128)(2,1)S(1)} %get-tuple-element.171.refs_1_.refs_0_, f32[8,512]{1,0:T(8,128)S(1)} %stack.46.refs_4_.refs_2_.refs_6_, ...), custom_call_target="tpu_custom_call" | custom-call | flops 1 | bytes 8302500 | tf_op jit(solution)/shard_map/first_norm_project/pallas_call | solution.py:129
  78.6 4.0 %collective-permute-done.10.refs_1_.refs_0_ = bf16[1,512,256]{2,1,0:T(8,128)(2,1)S(1)} collective-permute-done((bf16[1,512,256]{2,1,0:T(8,128)(2,1)S(1)}, bf16[1,512,256]{2,1,0:T(8,128)(2,1)S(1)}, u32[]{:S(2)}, u32[]{:S(2)}) %collective-permute-start.10) | collective-permute-done | bytes 262176 | tf_op jit(solution)/shard_map/ppermute | solution.py:83
  83.4 3.2 %attention_first.1 = (bf16[1024,256]{1,0:T(8,128)(2,1)S(1)}, f32[2,1,1024]{2,1,0:T(1,128)S(1)}, f32[8,128]{1,0:T(8,128)S(1)}) custom-call(s32[1]{0:T(128)S(6)} %copy.57.refs_0_.refs_1_, bf16[1024,1536]{1,0:T(8,128)(2,1)S(1)} %get-tuple-element.187.refs_1_.refs_2_, f32[8,128]{1,0:T(8,128)S(1)} %get-tuple-element.188.refs_2_), custom_call_target="tpu_custom_call" | custom-call | flops 1 | bytes 4612500 | tf_op jit(solution)/shard_map/attention_first/pallas_call | solution.py:129
  89.9 5.4 %attention_second.1 = (bf16[1024,256]{1,0:T(8,128)(2,1)S(1)}, f32[2,1,1024]{2,1,0:T(1,128)S(1)}, bf16[1024,1024]{1,0:T(8,128)(2,1)S(1)}, f32[8,128]{1,0:T(8,128)S(1)}) custom-call(s32[3]{0:T(128)S(1)} %pad_add_fusion.refs_0_, s32[1]{0:T(128)S(6)} %copy.57.refs_0_.refs_1_, bf16[1024,1536]{1,0:T(8,128)(2,1)S(1)} %get-tuple-element.187.refs_1_.refs_2_, ...), custom_call_target="tpu_custom_call" | custom-call | flops 1 | bytes 6457500 | tf_op jit(solution)/shard_map/attention_second/pallas_call | solution.py:129
  103.3 12.3 %second_norm_up.1 = (f32[1024,512]{1,0:T(8,128)}, bf16[1024,1024]{1,0:T(8,128)(2,1)}, f32[1024,1]{1,0:T(8,128)}, bf16[1024,1024]{1,0:T(8,128)(2,1)}, bf16[1024,2...) custom-call(s32[3]{0:T(128)S(1)} %pad_add_fusion.refs_0_, ...), custom_call_target="tpu_custom_call" | custom-call | flops 1 | bytes 13837500 | tf_op jit(solution)/shard_map/second_norm_up/pallas_call | solution.py:129
  115.6 3.5 %collective-permute-done.20.refs_1_.refs_3_.refs_11_.refs_4_ = bf16[3,512,256]{2,1,0:T(8,128)(2,1)S(1)} collective-permute-done((bf16[3,512,256]{2,1,0:T(8,128)(2,1)S(1)}, bf16[3,512,256]{2,1,0:T(8,128)(2,1)S(1)}, u32[]{:S(2)}, u32[]{:S(2)}) %collective-permute-start.20) | collective-permute-done | bytes 786464 | tf_op jit(solution)/shard_map/ppermute | solution.py:83
  122.5 6.7 %down_grad.1 = (bf16[8,64,1024]{2,1,0:T(8,128)(2,1)S(1)}, bf16[8,64,1024]{2,1,0:T(8,128)(2,1)S(1)}, bf16[8,64,1024]{2,1,0:T(8,128)(2,1)S(1)}, bf16[8,64,1024]{2,1,0:T(8,128)(2,1)S(1)}, f32[8,128]{1,0:T(8,128)S(1)}) custom-call(s32[3]{0:T(128)S(1)} %pad_add_fusion.refs_0_, bf16[1024,1024]{1,0:T(8,128)(2,1)S(1)} %copy-done.1, ...), custom_call_target="tpu_custom_call" | custom-call | flops 1 | bytes 8302500 | tf_op jit(solution)/shard_map/down_grad/pallas_call | solution.py:129
  133.1 13.0 %hidden_backward.1 = (bf16[1024,2048]{1,0:T(8,128)(2,1)}, bf16[1024,1024]{1,0:T(8,128)(2,1)S(1)}, f32[1,2048]{1,0:T(1,128)S(1)}, f32[8,128]{1,0:T(8,128)S(1)}) custom-call(s32[3]{0:T(128)S(1)} %pad_add_fusion.refs_0_, bf16[1024,1024]{1,0:T(8,128)(2,1)S(1)} %copy-done.1, bf16[1024,2048]{1,0:T(8,128)(2,1)S(1)} %get-tuple-element.217.refs_2_, ...), custom_call_target="tpu_custom_call" | custom-call | flops 1 | bytes 15682500 | tf_op jit(solution)/shard_map/hidden_backward/pallas_call | solution.py:129
  148.4 6.7 %up_grad.1 = (bf16[8,64,1024]{2,1,0:T(8,128)(2,1)S(1)}, bf16[8,64,1024]{2,1,0:T(8,128)(2,1)S(1)}, bf16[8,64,1024]{2,1,0:T(8,128)(2,1)S(1)}, bf16[8,64,1024]{2,1,0:T(8,128)(2,1)S(1)}, f32[8,128]{1,0:T(8,128)S(1)}) custom-call(s32[3]{0:T(128)S(1)} %pad_add_fusion.refs_0_, bf16[1024,1024]{1,0:T(8,128)(2,1)S(1)} %copy-done.9, bf16[1024,2048]{1,0:T(8,128)(2,1)S(1)} %copy-done.6, ...), custom_call_target="tpu_custom_call" | custom-call | flops 1 | bytes 8302500 | tf_op jit(solution)/shard_map/up_grad/pallas_call | solution.py:129
  160.8 6.4 %second_norm_backward.1 = (bf16[1024,1024]{1,0:T(8,128)(2,1)S(1)}, f32[1024,512]{1,0:T(8,128)S(1)}, bf16[1024,512]{1,0:T(8,128)(2,1)S(1)}, f32[4,512]{1,0:T(4,128)S(1)}, f32[8,128]{1,0:T(8,128)S(1)}) custom-call(s32[3]{0:T(128)S(1)} %pad_add_fusion.refs_0_, bf16[1024,1024]{1,0:T(8,128)(2,1)S(1)} %copy-done.1, ...), custom_call_target="tpu_custom_call" | custom-call | flops 1 | bytes 8302500 | tf_op jit(solution)/shard_map/second_norm_backward/pallas_call | solution.py:129
  167.3 4.9 %attention_backward.2 = (bf16[1024,768]{1,0:T(8,128)(2,1)S(1)}, f32[2,1,256]{2,1,0:T(1,128)S(1)}, f32[8,128]{1,0:T(8,128)S(1)}) custom-call(s32[1]{0:T(128)S(6)} %copy.57.refs_0_.refs_1_, bf16[1024,1536]{1,0:T(8,128)(2,1)S(1)} %get-tuple-element.187.refs_1_.refs_2_, bf16[1024,512]{1,0:T(8,128)(2,1)S(1)} %get-tuple-element.235.refs_2_, ...), custom_call_target="tpu_custom_call" | custom-call | flops 1 | bytes 5535000 | tf_op jit(solution)/shard_map/attention_backward/pallas_call | solution.py:129
  172.2 4.7 %attention_backward.3 = (bf16[1024,768]{1,0:T(8,128)(2,1)S(1)}, f32[2,1,256]{2,1,0:T(1,128)S(1)}, f32[8,128]{1,0:T(8,128)S(1)}) custom-call(s32[1]{0:T(128)S(6)} %copy.57.refs_0_.refs_1_, bf16[1024,1536]{1,0:T(8,128)(2,1)S(1)} %get-tuple-element.187.refs_1_.refs_2_, bf16[1024,512]{1,0:T(8,128)(2,1)S(1)} %get-tuple-element.235.refs_2_, ...), custom_call_target="tpu_custom_call" | custom-call | flops 1 | bytes 5535000 | tf_op jit(solution)/shard_map/attention_backward/pallas_call | solution.py:129
  179.5 5.0 %joint_grad_a.1 = (bf16[8,64,1280]{2,1,0:T(8,128)(2,1)S(1)}, bf16[8,64,1280]{2,1,0:T(8,128)(2,1)S(1)}, f32[8,128]{1,0:T(8,128)S(1)}) custom-call(s32[3]{0:T(128)S(1)} %pad_add_fusion.refs_0_, bf16[1024,1024]{1,0:T(8,128)(2,1)S(1)} %copy-done.5, bf16[1024,768]{1,0:T(8,128)(2,1)S(1)} %get-tuple-element.250.refs_2_.refs_4_, ...), custom_call_target="tpu_custom_call" | custom-call | flops 1 | bytes 7380000 | tf_op jit(solution)/shard_map/joint_grad_a/pallas_call | solution.py:129
  184.6 3.6 %joint_grad_b.1 = (bf16[8,64,768]{2,1,0:T(8,128)(2,1)S(1)}, bf16[8,64,768]{2,1,0:T(8,128)(2,1)S(1)}, f32[8,128]{1,0:T(8,128)S(1)}) custom-call(s32[3]{0:T(128)S(1)} %pad_add_fusion.refs_0_, bf16[1024,1024]{1,0:T(8,128)(2,1)S(1)} %copy-done.5, bf16[1024,768]{1,0:T(8,128)(2,1)S(1)} %get-tuple-element.249.refs_2_.refs_5_, f32[8,128]{1,0:T(8,128)S(1)} %get-tuple-element.253.refs_3_), custom_call_target="tpu_custom_call" | custom-call | flops 1 | bytes 5535000 | tf_op jit(solution)/shard_map/joint_grad_b/pallas_call | solution.py:129
  188.2 6.2 %collective-permute-done.29 = bf16[8,64,1024]{2,1,0:T(8,128)(2,1)S(1)} collective-permute-done((bf16[8,64,1024]{2,1,0:T(8,128)(2,1)S(1)}, bf16[8,64,1024]{2,1,0:T(8,128)(2,1)S(1)}, u32[]{:S(2)}, u32[]{:S(2)}) %collective-permute-start.29) | collective-permute-done | bytes 1048608 | tf_op jit(solution)/shard_map/ppermute | solution.py:83
  198.5 7.5 %project_backward.1 = (bf16[1024,512]{1,0:T(8,128)(2,1)S(1)}, bf16[1024,640]{1,0:T(8,128)(2,1)S(1)}, f32[1024,128]{1,0:T(8,128)S(1)}, f32[8,128]{1,0:T(8,128)S(1)}) custom-call(s32[3]{0:T(128)S(1)} %pad_add_fusion.refs_0_, bf16[1024,1024]{1,0:T(8,128)(2,1)S(1)} %get-tuple-element.171.refs_1_.refs_0_, f32[8,512]{1,0:T(8,128)S(1)} %stack.46.refs_4_.refs_2_.refs_6_, ...), custom_call_target="tpu_custom_call" | custom-call | flops 1 | bytes 7380000 | tf_op jit(solution)/shard_map/project_backward/pallas_call | solution.py:129
  206.0 4.4 %collective-permute-done.31 = bf16[1,64,2048]{2,1,0:T(8,128)(2,1)S(1)} collective-permute-done((bf16[1,64,2048]{2,1,0:T(8,128)(2,1)S(1)}, bf16[1,64,2048]{2,1,0:T(8,128)(2,1)S(1)}, u32[]{:S(2)}, u32[]{:S(2)}) %collective-permute-start.31) | collective-permute-done | bytes 262176 | tf_op jit(solution)/shard_map/ppermute | solution.py:83
  213.1 6.4 %down_project.1 = (bf16[1024,512]{1,0:T(8,128)(2,1)S(1)}, bf16[1024,512]{1,0:T(8,128)(2,1)S(1)}, f32[8,128]{1,0:T(8,128)S(1)}) custom-call(s32[3]{0:T(128)S(1)} %pad_add_fusion.refs_0_, bf16[1024,2048]{1,0:T(8,128)(2,1)S(1)} %get-tuple-element.200.refs_2_.refs_1_, bf16[3,512,256]{2,1,0:T(8,128)(2,1)S(1)} %get-tuple-element.201.refs_1_.refs_9_.refs_2_, ...), custom_call_target="tpu_custom_call" | custom-call | flops 1 | bytes 8302500 | tf_op jit(solution)/shard_map/down_project/pallas_call | solution.py:129
  219.5 5.7 %collective-permute-done.36 = bf16[4,64,1024]{2,1,0:T(8,128)(2,1)S(1)} collective-permute-done((bf16[4,64,1024]{2,1,0:T(8,128)(2,1)S(1)}, bf16[4,64,1024]{2,1,0:T(8,128)(2,1)S(1)}, u32[]{:S(2)}, u32[]{:S(2)}) %collective-permute-start.36) | collective-permute-done | bytes 524320 | tf_op jit(solution)/shard_map/ppermute | solution.py:83
  225.3 13.6 %collective-permute-done.37 = bf16[4,64,1024]{2,1,0:T(8,128)(2,1)S(1)} collective-permute-done((bf16[4,64,1024]{2,1,0:T(8,128)(2,1)S(1)}, bf16[4,64,1024]{2,1,0:T(8,128)(2,1)S(1)}, u32[]{:S(2)}, u32[]{:S(2)}) %collective-permute-start.37) | collective-permute-done | bytes 524320 | tf_op jit(solution)/shard_map/ppermute | solution.py:83
  245.0 3.0 first_norm_backward.1
  248.0 3.8 %collective-permute-done.39 = bf16[2,64,2048]{2,1,0:T(8,128)(2,1)S(1)} collective-permute-done((bf16[2,64,2048]{2,1,0:T(8,128)(2,1)S(1)}, bf16[2,64,2048]{2,1,0:T(8,128)(2,1)S(1)}, u32[]{:S(2)}, u32[]{:S(2)}) %collective-permute-start.39) | collective-permute-done | bytes 524320 | tf_op jit(solution)/shard_map/ppermute | solution.py:83
  255.8 8.6 %collective-permute-done.40 = bf16[1,64,2048]{2,1,0:T(8,128)(2,1)S(1)} collective-permute-done((bf16[1,64,2048]{2,1,0:T(8,128)(2,1)S(1)}, bf16[1,64,2048]{2,1,0:T(8,128)(2,1)S(1)}, u32[]{:S(2)}, u32[]{:S(2)}) %collective-permute-start.40) | collective-permute-done | bytes 262176 | tf_op jit(solution)/shard_map/ppermute | solution.py:83
  268.5 2.9 collective-permute-done.42.refs_1_
  272.5 6.3 %collective-permute-done.46 = bf16[2,64,768]{2,1,0:T(8,128)(2,1)S(1)} collective-permute-done((bf16[2,64,768]{2,1,0:T(8,128)(2,1)S(1)}, bf16[2,64,768]{2,1,0:T(8,128)(2,1)S(1)}, u32[]{:S(2)}, u32[]{:S(2)}) %collective-permute-start.46) | collective-permute-done | bytes 196640 | tf_op jit(solution)/shard_map/ppermute | solution.py:83
  286.5 4.1 %collective-permute-done.48 = bf16[1,64,768]{2,1,0:T(8,128)(2,1)S(1)} collective-permute-done((bf16[1,64,768]{2,1,0:T(8,128)(2,1)S(1)}, bf16[1,64,768]{2,1,0:T(8,128)(2,1)S(1)}, u32[]{:S(2)}, u32[]{:S(2)}) %collective-permute-start.48) | collective-permute-done | bytes 98336 | tf_op jit(solution)/shard_map/ppermute | solution.py:83
  299.9 4.5 %collective-permute-done.53.refs_2_ = bf16[64,4096]{1,0:T(8,128)(2,1)S(1)} collective-permute-done((bf16[64,4096]{1,0:T(8,128)(2,1)S(1)}, bf16[64,4096]{1,0:T(8,128)(2,1)S(1)}, u32[]{:S(2)}, u32[]{:S(2)}) %collective-permute-start.53) | collective-permute-done | bytes 524320 | tf_op jit(solution)/shard_map/ppermute | solution.py:83
  304.4 3.4 %finish_ffn.1 = (f32[2048,256]{1,0:T(8,128)}, f32[256,2048]{1,0:T(8,128)}, f32[8,128]{1,0:T(8,128)S(1)}) custom-call(s32[3]{0:T(128)S(1)} %pad_add_fusion.refs_0_, bf16[64,4096]{1,0:T(8,128)(2,1)S(1)} %get-tuple-element.321.refs_1_, bf16[64,4096]{1,0:T(8,128)(2,1)S(1)} %collective-permute-done.53.refs_2_, ...), custom_call_target="tpu_custom_call" | custom-call | flops 1 | bytes 1845000 | tf_op jit(solution)/shard_map/finish_ffn/pallas_call | solution.py:129
  (190 shorter events, 102.5 us)
Async XLA Ops:
  9.6 23.2 %collective-permute-start.4 = (bf16[1,64,2048]{2,1,0:T(8,128)(2,1)}, bf16[1,64,2048]{2,1,0:T(8,128)(2,1)}, u32[]{:S(2)}, u32[]{:S(2)}) collective-permute-start(bf16[1,64,2048]{2,1,0:T(8,128)(2,1)} %maximum_bitcast_fusion), channel_id=1, source_target_pairs={{0,4},{2,6},{4,0},{6,2},{1,5},{3,7},{5,1},{7,3},{8,12},{10,14},{12... | collective-permute-start | bytes 786440 | tf_op jit(solution)/shard_map/ppermute | solution.py:83
  9.6 23.2 %collective-permute-start.3 = (bf16[1,64,2048]{2,1,0:T(8,128)(2,1)}, bf16[1,64,2048]{2,1,0:T(8,128)(2,1)}, u32[]{:S(2)}, u32[]{:S(2)}) collective-permute-start(bf16[1,64,2048]{2,1,0:T(8,128)(2,1)} %maximum_bitcast_fusion), channel_id=1, source_target_pairs={{0,2},{2,0},{4,6},{6,4},{1,3},{3,1},{5,7},{7,5},{8,10},{10,8},{12,... | collective-permute-start | bytes 786440 | tf_op jit(solution)/shard_map/ppermute | solution.py:83
  34.8 19.3 %collective-permute-start.7 = (bf16[3,64,2048]{2,1,0:T(8,128)(2,1)}, bf16[3,64,2048]{2,1,0:T(8,128)(2,1)S(1)}, u32[]{:S(2)}, u32[]{:S(2)}) collective-permute-start(bf16[3,64,2048]{2,1,0:T(8,128)(2,1)} %get-tuple-element.173.refs_3_.refs_5_.refs_4_.refs_8_.refs_6_), channel_id=1, source_target_pairs={{0,16},{8,24},{16,0},{24,8},{1,17},{9,25},{17,1},{25,9},{2,18},{10... | collective-permute-start | bytes 2359304 | tf_op jit(solution)/shard_map/ppermute | solution.py:83
  36.4 19.1 %collective-permute-start.6 = (bf16[3,64,2048]{2,1,0:T(8,128)(2,1)}, bf16[3,64,2048]{2,1,0:T(8,128)(2,1)}, u32[]{:S(2)}, u32[]{:S(2)}) collective-permute-start(bf16[3,64,2048]{2,1,0:T(8,128)(2,1)} %get-tuple-element.173.refs_3_.refs_5_.refs_4_.refs_8_.refs_6_), channel_id=1, source_target_pairs={{0,8},{8,0},{16,24},{24,16},{1,9},{9,1},{17,25},{25,17},{2,10},{10... | collective-permute-start | bytes 2359304 | tf_op jit(solution)/shard_map/ppermute | solution.py:83
  39.7 13.7 %collective-permute-start.8 = (bf16[1,64,2048]{2,1,0:T(8,128)(2,1)S(1)}, bf16[1,64,2048]{2,1,0:T(8,128)(2,1)S(1)}, u32[]{:S(2)}, u32[]{:S(2)}) collective-permute-start(bf16[1,64,2048]{2,1,0:T(8,128)(2,1)S(1)} %bitcast.115), channel_id=1, source_target_pairs={{0,4},{2,6},{4,0},{6,2},{1,5},{3,7},{5,1},{7,3},{8,12},{10,14},{12... | collective-permute-start | bytes 786440 | tf_op jit(solution)/shard_map/ppermute | solution.py:83
  53.5 13.9 %collective-permute-start.9 = (bf16[2,64,2048]{2,1,0:T(8,128)(2,1)S(1)}, bf16[2,64,2048]{2,1,0:T(8,128)(2,1)S(1)}, u32[]{:S(2)}, u32[]{:S(2)}) collective-permute-start(bf16[2,64,2048]{2,1,0:T(8,128)(2,1)S(1)} %get-tuple-element.179), channel_id=1, source_target_pairs={{0,2},{2,0},{4,6},{6,4},{1,3},{3,1},{5,7},{7,5},{8,10},{10,8},{12,... | collective-permute-start | bytes 1572872 | tf_op jit(solution)/shard_map/ppermute | solution.py:83
  67.5 19.1 %collective-permute-start.15 = (bf16[3,64,2048]{2,1,0:T(8,128)(2,1)S(1)}, bf16[3,64,2048]{2,1,0:T(8,128)(2,1)S(1)}, u32[]{:S(2)}, u32[]{:S(2)}) collective-permute-start(bf16[3,64,2048]{2,1,0:T(8,128)(2,1)S(1)} %get-tuple-element.183.refs_11_.refs_1_.refs_7_.refs_3_), channel_id=1, source_target_pairs={{0,16},{8,24},{16,0},{24,8},{1,17},{9,25},{17,1},{25,9},{2,18},{10... | collective-permute-start | bytes 2359304 | tf_op jit(solution)/shard_map/ppermute | solution.py:83
  68.8 17.8 %collective-permute-start.14 = (bf16[3,64,2048]{2,1,0:T(8,128)(2,1)S(1)}, bf16[3,64,2048]{2,1,0:T(8,128)(2,1)S(1)}, u32[]{:S(2)}, u32[]{:S(2)}) collective-permute-start(bf16[3,64,2048]{2,1,0:T(8,128)(2,1)S(1)} %get-tuple-element.183.refs_11_.refs_1_.refs_7_.refs_3_), channel_id=1, source_target_pairs={{0,8},{8,0},{16,24},{24,16},{1,9},{9,1},{17,25},{25,17},{2,10},{10... | collective-permute-start | bytes 2359304 | tf_op jit(solution)/shard_map/ppermute | solution.py:83
  99.1 20.0 %collective-permute-start.20 = (bf16[3,512,256]{2,1,0:T(8,128)(2,1)S(1)}, bf16[3,512,256]{2,1,0:T(8,128)(2,1)S(1)}, u32[]{:S(2)}, u32[]{:S(2)}) collective-permute-start(bf16[3,512,256]{2,1,0:T(8,128)(2,1)S(1)} %get-tuple-element.201.refs_1_.refs_9_.refs_2_), channel_id=1, source_target_pairs={{0,16},{8,24},{16,0},{24,8},{1,17},{9,25},{17,1},{25,9},{2,18},{10... | collective-permute-start | bytes 2359304 | tf_op jit(solution)/shard_map/ppermute | solution.py:83
  99.5 19.6 %collective-permute-start.19 = (bf16[3,512,256]{2,1,0:T(8,128)(2,1)S(1)}, bf16[3,512,256]{2,1,0:T(8,128)(2,1)S(1)}, u32[]{:S(2)}, u32[]{:S(2)}) collective-permute-start(bf16[3,512,256]{2,1,0:T(8,128)(2,1)S(1)} %get-tuple-element.201.refs_1_.refs_9_.refs_2_), channel_id=1, source_target_pairs={{0,8},{8,0},{16,24},{24,16},{1,9},{9,1},{17,25},{25,17},{2,10},{10... | collective-permute-start | bytes 2359304 | tf_op jit(solution)/shard_map/ppermute | solution.py:83
  131.0 24.1 %collective-permute-start.23 = (bf16[8,64,1024]{2,1,0:T(8,128)(2,1)S(1)}, bf16[8,64,1024]{2,1,0:T(8,128)(2,1)S(1)}, u32[]{:S(2)}, u32[]{:S(2)}) collective-permute-start(bf16[8,64,1024]{2,1,0:T(8,128)(2,1)S(1)} %get-tuple-element.213), channel_id=1, source_target_pairs={{0,8},{8,0},{16,24},{24,16},{1,9},{9,1},{17,25},{25,17},{2,10},{10... | collective-permute-start | bytes 3145736 | tf_op jit(solution)/shard_map/ppermute | solution.py:83
  132.5 22.9 %collective-permute-start.24 = (bf16[8,64,1024]{2,1,0:T(8,128)(2,1)S(1)}, bf16[8,64,1024]{2,1,0:T(8,128)(2,1)S(1)}, u32[]{:S(2)}, u32[]{:S(2)}) collective-permute-start(bf16[8,64,1024]{2,1,0:T(8,128)(2,1)S(1)} %get-tuple-element.215), channel_id=1, source_target_pairs={{0,16},{8,24},{16,0},{24,8},{1,17},{9,25},{17,1},{25,9},{2,18},{10... | collective-permute-start | bytes 3145736 | tf_op jit(solution)/shard_map/ppermute | solution.py:83
  156.7 20.2 %collective-permute-start.25 = (bf16[4,64,1024]{2,1,0:T(8,128)(2,1)S(1)}, bf16[4,64,1024]{2,1,0:T(8,128)(2,1)S(1)}, u32[]{:S(2)}, u32[]{:S(2)}) collective-permute-start(bf16[4,64,1024]{2,1,0:T(8,128)(2,1)S(1)} %get-tuple-element.228), channel_id=1, source_target_pairs={{0,16},{8,24},{16,0},{24,8},{1,17},{9,25},{17,1},{25,9},{2,18},{10... | collective-permute-start | bytes 1572872 | tf_op jit(solution)/shard_map/ppermute | solution.py:83
  157.9 19.0 %collective-permute-start.26 = (bf16[4,64,1024]{2,1,0:T(8,128)(2,1)S(1)}, bf16[4,64,1024]{2,1,0:T(8,128)(2,1)S(1)}, u32[]{:S(2)}, u32[]{:S(2)}) collective-permute-start(bf16[4,64,1024]{2,1,0:T(8,128)(2,1)S(1)} %get-tuple-element.230), channel_id=1, source_target_pairs={{0,8},{8,0},{16,24},{24,16},{1,9},{9,1},{17,25},{25,17},{2,10},{10... | collective-permute-start | bytes 1572872 | tf_op jit(solution)/shard_map/ppermute | solution.py:83
  158.4 35.9 %collective-permute-start.29 = (bf16[8,64,1024]{2,1,0:T(8,128)(2,1)S(1)}, bf16[8,64,1024]{2,1,0:T(8,128)(2,1)S(1)}, u32[]{:S(2)}, u32[]{:S(2)}) collective-permute-start(bf16[8,64,1024]{2,1,0:T(8,128)(2,1)S(1)} %get-tuple-element.245), channel_id=1, source_target_pairs={{0,8},{8,0},{16,24},{24,16},{1,9},{9,1},{17,25},{25,17},{2,10},{10... | collective-permute-start | bytes 3145736 | tf_op jit(solution)/shard_map/ppermute | solution.py:83
  159.9 34.4 %collective-permute-start.30 = (bf16[8,64,1024]{2,1,0:T(8,128)(2,1)S(1)}, bf16[8,64,1024]{2,1,0:T(8,128)(2,1)S(1)}, u32[]{:S(2)}, u32[]{:S(2)}) collective-permute-start(bf16[8,64,1024]{2,1,0:T(8,128)(2,1)S(1)} %get-tuple-element.247), channel_id=1, source_target_pairs={{0,16},{8,24},{16,0},{24,8},{1,17},{9,25},{17,1},{25,9},{2,18},{10... | collective-permute-start | bytes 3145736 | tf_op jit(solution)/shard_map/ppermute | solution.py:83
  177.7 17.8 %collective-permute-start.28 = (bf16[2,64,2048]{2,1,0:T(8,128)(2,1)S(1)}, bf16[2,64,2048]{2,1,0:T(8,128)(2,1)S(1)}, u32[]{:S(2)}, u32[]{:S(2)}) collective-permute-start(bf16[2,64,2048]{2,1,0:T(8,128)(2,1)S(1)} %get-tuple-element.243), channel_id=1, source_target_pairs={{0,2},{2,0},{4,6},{6,4},{1,3},{3,1},{5,7},{7,5},{8,10},{10,8},{12,... | collective-permute-start | bytes 1572872 | tf_op jit(solution)/shard_map/ppermute | solution.py:83
  196.2 14.1 %collective-permute-start.31 = (bf16[1,64,2048]{2,1,0:T(8,128)(2,1)S(1)}, bf16[1,64,2048]{2,1,0:T(8,128)(2,1)S(1)}, u32[]{:S(2)}, u32[]{:S(2)}) collective-permute-start(bf16[1,64,2048]{2,1,0:T(8,128)(2,1)S(1)} %get-tuple-element.257), channel_id=1, source_target_pairs={{0,4},{2,6},{4,0},{6,2},{1,5},{3,7},{5,1},{7,3},{8,12},{10,14},{12... | collective-permute-start | bytes 786440 | tf_op jit(solution)/shard_map/ppermute | solution.py:83
  197.9 44.6 %collective-permute-start.34 = (bf16[8,64,1280]{2,1,0:T(8,128)(2,1)S(1)}, bf16[8,64,1280]{2,1,0:T(8,128)(2,1)S(1)}, u32[]{:S(2)}, u32[]{:S(2)}) collective-permute-start(bf16[8,64,1280]{2,1,0:T(8,128)(2,1)S(1)} %get-tuple-element.269), channel_id=1, source_target_pairs={{0,8},{8,0},{16,24},{24,16},{1,9},{9,1},{17,25},{25,17},{2,10},{10... | collective-permute-start | bytes 3932168 | tf_op jit(solution)/shard_map/ppermute | solution.py:83
  210.4 34.6 %collective-permute-start.33 = (bf16[1024,640]{1,0:T(8,128)(2,1)S(1)}, bf16[1024,640]{1,0:T(8,128)(2,1)S(1)}, u32[]{:S(2)}, u32[]{:S(2)}) collective-permute-start(bf16[1024,640]{1,0:T(8,128)(2,1)S(1)} %get-tuple-element.265), channel_id=1, source_target_pairs={{0,1},{1,0},{2,3},{3,2},{4,5},{5,4},{6,7},{7,6},{8,9},{9,8},{10,11... | collective-permute-start | bytes 3932168 | tf_op jit(solution)/shard_map/ppermute | solution.py:87
  210.5 14.8 %collective-permute-start.36 = (bf16[4,64,1024]{2,1,0:T(8,128)(2,1)S(1)}, bf16[4,64,1024]{2,1,0:T(8,128)(2,1)S(1)}, u32[]{:S(2)}, u32[]{:S(2)}) collective-permute-start(bf16[4,64,1024]{2,1,0:T(8,128)(2,1)S(1)} %get-tuple-element.273), channel_id=1, source_target_pairs={{0,16},{8,24},{16,0},{24,8},{1,17},{9,25},{17,1},{25,9},{2,18},{10... | collective-permute-start | bytes 1572872 | tf_op jit(solution)/shard_map/ppermute | solution.py:83
  211.4 27.4 %collective-permute-start.37 = (bf16[4,64,1024]{2,1,0:T(8,128)(2,1)S(1)}, bf16[4,64,1024]{2,1,0:T(8,128)(2,1)S(1)}, u32[]{:S(2)}, u32[]{:S(2)}) collective-permute-start(bf16[4,64,1024]{2,1,0:T(8,128)(2,1)S(1)} %get-tuple-element.275), channel_id=1, source_target_pairs={{0,8},{8,0},{16,24},{24,16},{1,9},{9,1},{17,25},{25,17},{2,10},{10... | collective-permute-start | bytes 1572872 | tf_op jit(solution)/shard_map/ppermute | solution.py:83
  212.0 29.7 %collective-permute-start.35 = (bf16[8,64,768]{2,1,0:T(8,128)(2,1)S(1)}, bf16[8,64,768]{2,1,0:T(8,128)(2,1)S(1)}, u32[]{:S(2)}, u32[]{:S(2)}) collective-permute-start(bf16[8,64,768]{2,1,0:T(8,128)(2,1)S(1)} %get-tuple-element.271), channel_id=1, source_target_pairs={{0,16},{8,24},{16,0},{24,8},{1,17},{9,25},{17,1},{25,9},{2,18},{10... | collective-permute-start | bytes 2359304 | tf_op jit(solution)/shard_map/ppermute | solution.py:83
  240.2 43.8 %collective-permute-start.32 = (bf16[1024,512]{1,0:T(8,128)(2,1)S(1)}, bf16[1024,512]{1,0:T(8,128)(2,1)S(1)}, u32[]{:S(2)}, u32[]{:S(2)}) collective-permute-start(bf16[1024,512]{1,0:T(8,128)(2,1)S(1)} %get-tuple-element.263), channel_id=1, source_target_pairs={{0,1},{1,0},{2,3},{3,2},{4,5},{5,4},{6,7},{7,6},{8,9},{9,8},{10,11... | collective-permute-start | bytes 3145736 | tf_op jit(solution)/shard_map/ppermute | solution.py:87
  243.5 21.0 %collective-permute-start.43 = (bf16[4,64,1280]{2,1,0:T(8,128)(2,1)S(1)}, bf16[4,64,1280]{2,1,0:T(8,128)(2,1)S(1)}, u32[]{:S(2)}, u32[]{:S(2)}) collective-permute-start(bf16[4,64,1280]{2,1,0:T(8,128)(2,1)S(1)} %get-tuple-element.299), channel_id=1, source_target_pairs={{0,16},{8,24},{16,0},{24,8},{1,17},{9,25},{17,1},{25,9},{2,18},{10... | collective-permute-start | bytes 1966088 | tf_op jit(solution)/shard_map/ppermute | solution.py:83
  265.6 14.9 %collective-permute-start.45 = (bf16[2,64,1280]{2,1,0:T(8,128)(2,1)S(1)}, bf16[2,64,1280]{2,1,0:T(8,128)(2,1)S(1)}, u32[]{:S(2)}, u32[]{:S(2)}) collective-permute-start(bf16[2,64,1280]{2,1,0:T(8,128)(2,1)S(1)} %get-tuple-element.304), channel_id=1, source_target_pairs={{0,2},{2,0},{4,6},{6,4},{1,3},{3,1},{5,7},{7,5},{8,10},{10,8},{12,... | collective-permute-start | bytes 983048 | tf_op jit(solution)/shard_map/ppermute | solution.py:83
  271.6 24.6 %collective-permute-start.55 = (bf16[64,4096]{1,0:T(8,128)(2,1)S(1)}, bf16[64,4096]{1,0:T(8,128)(2,1)S(1)}, u32[]{:S(2)}, u32[]{:S(2)}) collective-permute-start(bf16[64,4096]{1,0:T(8,128)(2,1)S(1)} %get-tuple-element.321.refs_1_), channel_id=1, source_target_pairs={{0,24},{8,16},{16,8},{24,0},{1,25},{9,17},{17,9},{25,1},{2,26},{10... | collective-permute-start | bytes 1572872 | tf_op jit(solution)/shard_map/ppermute | solution.py:83
  285.6 14.2 %collective-permute-start.54 = (bf16[64,4096]{1,0:T(8,128)(2,1)S(1)}, bf16[64,4096]{1,0:T(8,128)(2,1)S(1)}, u32[]{:S(2)}, u32[]{:S(2)}) collective-permute-start(bf16[64,4096]{1,0:T(8,128)(2,1)S(1)} %get-tuple-element.321.refs_1_), channel_id=1, source_target_pairs={{0,16},{8,24},{16,0},{24,8},{1,17},{9,25},{17,1},{25,9},{2,18},{10... | collective-permute-start | bytes 1572872 | tf_op jit(solution)/shard_map/ppermute | solution.py:83
  290.6 13.8 %collective-permute-start.53 = (bf16[64,4096]{1,0:T(8,128)(2,1)S(1)}, bf16[64,4096]{1,0:T(8,128)(2,1)S(1)}, u32[]{:S(2)}, u32[]{:S(2)}) collective-permute-start(bf16[64,4096]{1,0:T(8,128)(2,1)S(1)} %get-tuple-element.321.refs_1_), channel_id=1, source_target_pairs={{0,8},{8,0},{16,24},{24,16},{1,9},{9,1},{17,25},{25,17},{2,10},{10... | collective-permute-start | bytes 1572872 | tf_op jit(solution)/shard_map/ppermute | solution.py:83
  293.4 15.1 %collective-permute-start.52 = (bf16[64,2048]{1,0:T(8,128)(2,1)S(1)}, bf16[64,2048]{1,0:T(8,128)(2,1)S(1)}, u32[]{:S(2)}, u32[]{:S(2)}) collective-permute-start(bf16[64,2048]{1,0:T(8,128)(2,1)S(1)} %get-tuple-element.320.refs_1_), channel_id=1, source_target_pairs={{0,24},{8,16},{16,8},{24,0},{1,25},{9,17},{17,9},{25,1},{2,26},{10... | collective-permute-start | bytes 786440 | tf_op jit(solution)/shard_map/ppermute | solution.py:83
  294.4 14.1 %collective-permute-start.51 = (bf16[64,2048]{1,0:T(8,128)(2,1)S(1)}, bf16[64,2048]{1,0:T(8,128)(2,1)S(1)}, u32[]{:S(2)}, u32[]{:S(2)}) collective-permute-start(bf16[64,2048]{1,0:T(8,128)(2,1)S(1)} %get-tuple-element.320.refs_1_), channel_id=1, source_target_pairs={{0,16},{8,24},{16,0},{24,8},{1,17},{9,25},{17,1},{25,9},{2,18},{10... | collective-permute-start | bytes 786440 | tf_op jit(solution)/shard_map/ppermute | solution.py:83
  296.2 14.9 %collective-permute-start.50 = (bf16[64,2048]{1,0:T(8,128)(2,1)S(1)}, bf16[64,2048]{1,0:T(8,128)(2,1)S(1)}, u32[]{:S(2)}, u32[]{:S(2)}) collective-permute-start(bf16[64,2048]{1,0:T(8,128)(2,1)S(1)} %get-tuple-element.320.refs_1_), channel_id=1, source_target_pairs={{0,8},{8,0},{16,24},{24,16},{1,9},{9,1},{17,25},{25,17},{2,10},{10... | collective-permute-start | bytes 786440 | tf_op jit(solution)/shard_map/ppermute | solution.py:83
  (43 other events, 389.1 us)

commit v3 on v2

--- a/solution.py
+++ b/solution.py
@@ -105,14 +105,11 @@
     "up_grad": 9,
     "second_norm_backward": 9,
     "attention_backward": 6,
-    "joint_grad_a": 8,
-    "joint_grad_b": 6,
+    "joint_grad": 10,
     "project_backward": 8,
     "first_norm_backward": 6,
     "down_project": 9,
-    "joint_sum_a": 32,
-    "joint_sum_b": 40,
-    "up_rows": 40,
+    "joint_sum": 32,
 }
 COST_SCALE = 0.25 * 3.69e6
 
@@ -380,74 +377,115 @@
     return Weight(gathered, block, (rows, D), pairs)
 
 
-def weight_grad(lay, ids, sides, orders, name, after=()):
-    columns = sum(r.shape[1] for _, rights in sides for r in rights)
-    width = columns // len(orders)
-    ins = [(ids, smem())]
-    for left, rights in sides:
-        ins.append((left, pl.BlockSpec((LEN, lay.block), lambda z: (0, z))))
-        ins.extend((r, whole(*r.shape)) for r in rights)
-    counts = [len(rights) for _, rights in sides]
+def store_piece(ids, keep, send, bit, q, value):
+    spot = ((q >> (bit + 1)) << bit) + (q & ((1 << bit) - 1))
+    mine = ((ids[1] >> bit) & 1) == ((q >> bit) & 1)
+    pl.when(mine)(lambda: keep.__setitem__(spot, value))
+    pl.when(jnp.logical_not(mine))(lambda: send.__setitem__(spot, value))
+
+
+def small_chunks(refs):
+    two, joint_a, joint_b, up, first = refs
+    for row in range(4):
+        yield from (two[row : row + 1, i : i + HDIM] for i in range(0, HALF, HDIM))
+    for ref in (joint_a, joint_b):
+        for head in range(ref.shape[0]):
+            yield from (ref[head, :, i : i + HDIM] for i in range(0, ref.shape[2], HDIM))
+    yield from (up[:, i : i + HDIM] for i in range(0, up.shape[1], HDIM))
+    for begin in (0, HALF):
+        for row in range(2):
+            yield from (first[row : row + 1, i : i + HDIM] for i in range(begin, begin + HALF, HDIM))
+
+
+def weight_grad(lay, ids, parts, orders, name, smalls, after=()):
+    ins, widths = [(ids, smem())], []
+    for sides in parts:
+        for left, right in sides:
+            ins.append((left, pl.BlockSpec((LEN, lay.block), lambda z: (0, z))))
+            ins.append((right, whole(*right.shape)))
+        widths.append(sum(right.shape[1] for _, right in sides))
+    widths[0] += HDIM
+    ins.extend((v, whole(*v.shape)) for v in smalls)
     n_out = 2 * len(orders)
+
+    def kernel(ids, *refs):
+        ins, outs, rows_ref = list(refs[: -n_out - 1]), refs[-n_out - 1 : -1], refs[-1]
+        small_refs = ins[-len(smalls) :]
+
+        def fill():
+            rows_ref[...] = jnp.zeros_like(rows_ref)
+            for i, chunk in enumerate(small_chunks(small_refs)):
+                rows_ref[i : i + 1, :] = chunk
+
+        pl.when(pl.program_id(0) == 0)(fill)
+        for i, order in enumerate(orders):
+            values = []
+            for _ in parts[i]:
+                left, right = ins.pop(0), ins.pop(0)
+                values.append(dot(left[...], right[...], TN).astype(BF))
+            if i == 0:
+                values.append(rows_ref[...].astype(BF))
+            block = jnp.concatenate(values, axis=1)
+            for q in range(lay.s):
+                part = block[q * lay.piece : (q + 1) * lay.piece]
+                store_piece(ids, outs[2 * i], outs[2 * i + 1], order[0], q, part)
+
+    outs = []
+    for width in widths:
+        out = pl.BlockSpec((lay.s // 2, lay.piece, width), lambda z: (z, 0, 0))
+        outs += [(shape((lay.R * lay.s // 2, lay.piece, width)), out)] * 2
+    return call(
+        kernel, name, ins, outs, grid=(lay.R,), scratch=[pltpu.VMEM((lay.block, HDIM), F32)], after=after
+    )
+
+
+def output_grad(lay, ids, left, rights, orders, name, after):
+    width = rights[0].shape[1]
+    n_out = 2 * len(orders)
+    if len(rights) != len(orders):
+        return halves_grad(lay, ids, left, jnp.concatenate(rights, axis=1), orders, name, after)
+
+    def kernel(ids, left_ref, *refs):
+        for i, order in enumerate(orders):
+            block = dot(left_ref[...], refs[i][...], TN).astype(BF)
+            keep, send = refs[len(rights) + 2 * i : len(rights) + 2 * i + 2]
+            for q in range(lay.s):
+                store_piece(ids, keep, send, order[0], q, block[q * lay.piece : (q + 1) * lay.piece])
+
     out = pl.BlockSpec((lay.s // 2, lay.piece, width), lambda z: (z, 0, 0))
-
-    def kernel(ids, *refs):
-        ins, outs = refs[:-n_out], refs[-n_out:]
-        parts, at = [], 0
-        for n in counts:
-            left = ins[at][...]
-            parts.extend(dot(left, ins[at + 1 + i][...], TN).astype(BF) for i in range(n))
-            at += n + 1
-        block = parts[0] if len(parts) == 1 else jnp.concatenate(parts, axis=1)
-        for q in range(lay.s):
-            rows = block[q * lay.piece : (q + 1) * lay.piece]
-            for i, order in enumerate(orders):
+    return call(
+        kernel,
+        name,
+        [(ids, smem()), (left, pl.BlockSpec((LEN, lay.block), lambda z: (0, z)))]
+        + [(r, whole(*r.shape)) for r in rights],
+        [(shape((lay.R * lay.s // 2, lay.piece, width)), out)] * n_out,
+        grid=(lay.R,),
+        after=after,
+        mib=18,
+    )
+
+
+def halves_grad(lay, ids, left, right, orders, name, after):
+    width = right.shape[1] // len(orders)
+    n_out = 2 * len(orders)
+
+    def kernel(ids, left_ref, right_ref, *outs):
+        block = dot(left_ref[...], right_ref[...], TN).astype(BF)
+        for i, order in enumerate(orders):
+            for q in range(lay.s):
                 keep, send, bit = outs[2 * i], outs[2 * i + 1], order[0]
-                part = rows[:, i * width : (i + 1) * width]
-                mine = ((ids[1] >> bit) & 1) == ((q >> bit) & 1)
-                spot = ((q >> (bit + 1)) << bit) + (q & ((1 << bit) - 1))
-
-                def to_keep(keep=keep, spot=spot, part=part):
-                    keep[spot] = part
-
-                def to_send(send=send, spot=spot, part=part):
-                    send[spot] = part
-
-                pl.when(mine)(to_keep)
-                pl.when(jnp.logical_not(mine))(to_send)
-
-    kind = shape((lay.R * lay.s // 2, lay.piece, width))
-    return call(kernel, name, ins, [(kind, out)] * n_out, grid=(lay.R,), after=after)
-
-
-class Small:
-    def __init__(self, lay, arrays):
-        self.lay = lay
-        self.bits = [("dp", lay.Q, bit) for bit in lay.split_bits + lay.rest_bits]
-        self.bits += [("row", lay.R, bit) for bit in lay.row_bits]
-        self.value = jnp.concatenate([a.reshape(-1) for a in arrays]).reshape(-1, HDIM)
-        self.send()
-
-    def send(self):
-        self.got = swap(self.value, *self.bits.pop(0))
-
-    def add(self, after):
-        def kernel(a, b, out):
-            out[...] = a[...] + b[...]
-
-        ins = [(self.value, vmem()), (self.got, vmem())]
-        (self.value,), token = call(kernel, "small_sum", ins, [(shape(self.value.shape, F32), vmem())], after=after)
-        return token
-
-    def step(self, after):
-        token = self.add(after)
-        self.send()
-        return token
-
-    def finish(self, after):
-        while self.bits:
-            after = (self.step(after),)
-        return self.add(after)
+                part = block[q * lay.piece : (q + 1) * lay.piece, i * width : (i + 1) * width]
+                store_piece(ids, keep, send, bit, q, part)
+
+    out = pl.BlockSpec((lay.s // 2, lay.piece, width), lambda z: (z, 0, 0))
+    return call(
+        kernel,
+        name,
+        [(ids, smem()), (left, pl.BlockSpec((LEN, lay.block), lambda z: (0, z))), (right, whole(*right.shape))],
+        [(shape((lay.R * lay.s // 2, lay.piece, width)), out)] * n_out,
+        grid=(lay.R,),
+        after=after,
+    )
 
 
 class Reduction:
@@ -463,27 +501,33 @@
             self.got.append(swap(part, "dp", self.lay.Q, self.lay.split_bits[order[self.step]]))
         self.step += 1
 
-    def advance(self, after, name, passing=()):
+    def advance(self, after, name, passing=(), joined=()):
         lay, n = self.lay, len(self.orders)
         bits = [order[self.step] for order in self.orders]
         ins, outs = [(self.ids, smem())], []
+        reds = [self, *joined]
         for i, bit in enumerate(bits):
             groups = lay.R * 2 ** self.left[i].index(bit)
             rows = 2 ** (len(self.left[i]) - 1 - self.left[i].index(bit)) * lay.piece
-            width = self.keep[i].shape[-1]
-            for value in (self.keep[i], self.got[i]):
+            width = sum(r.keep[i].shape[-1] for r in reds)
+            for value in [v for r in reds for v in (r.keep[i], r.got[i])]:
+                columns = value.shape[-1]
                 ins.append(
-                    (value.reshape(groups, 2, rows, width), pl.BlockSpec((1, 2, rows, width), lambda g: (g, 0, 0, 0)))
+                    (value.reshape(groups, 2, rows, columns), pl.BlockSpec((1, 2, rows, columns), lambda g: (g, 0, 0, 0)))
                 )
             outs += [(shape((groups, rows, width)), pl.BlockSpec((1, rows, width), lambda g: (g, 0, 0)))] * 2
 
         def kernel(ids, *refs):
-            ins, outs = refs[: 2 * n], refs[2 * n :]
+            ins, outs = list(refs[: 2 * n * len(reds)]), refs[2 * n * len(reds) :]
             for i, bit in enumerate(bits):
                 mine = (ids[1] >> bit) & 1
-                a, b = ins[2 * i], ins[2 * i + 1]
-                for target, which in ((outs[2 * i], mine), (outs[2 * i + 1], 1 - mine)):
-                    target[0] = (a[0, which].astype(F32) + b[0, which].astype(F32)).astype(BF)
+                first = 0
+                for _ in reds:
+                    a, b = ins.pop(0), ins.pop(0)
+                    last = first + a.shape[3]
+                    for target, which in ((outs[2 * i], mine), (outs[2 * i + 1], 1 - mine)):
+                        target[0, :, first:last] = (a[0, which].astype(F32) + b[0, which].astype(F32)).astype(BF)
+                    first = last
 
         parts, token = call(kernel, name, ins, outs, grid=(groups,), after=after, passing=passing)
         self.left = [[b for b in left if b != bit] for left, bit in zip(self.left, bits)]
@@ -491,15 +535,17 @@
         return parts[2 * n :], token
 
 
-def first_rows(reduction, after, name):
+def first_rows(reduction, after, name, passing=()):
     lay, ids, n = reduction.lay, reduction.ids, len(reduction.orders)
     ins = [(ids, smem())]
-    width = reduction.keep[0].shape[-1]
-    for i in range(n):
+    widths = [keep.shape[-1] for keep in reduction.keep]
+    starts = [sum(widths[:i]) for i in range(n)]
+    columns = sum(widths)
+    for i, width in enumerate(widths):
         for value in (reduction.keep[i], reduction.got[i]):
             value = value.reshape(lay.R // 2, 2, lay.piece, width)
             ins.append((value, pl.BlockSpec((1, 2, lay.piece, width), lambda g: (g, 0, 0, 0))))
-    out = pl.BlockSpec((1, lay.piece, n * width), lambda g: (g, 0, 0))
+    out = pl.BlockSpec((1, lay.piece, columns), lambda g: (g, 0, 0))
 
     def kernel(ids, *refs):
         ins, (keep, send) = refs[:-2], refs[-2:]
@@ -507,11 +553,14 @@
         for target, bit in ((keep, mine), (send, 1 - mine)):
             for i in range(n):
                 a, b = ins[2 * i], ins[2 * i + 1]
-                target[0, :, i * width : (i + 1) * width] = (a[0, bit].astype(F32) + b[0, bit].astype(F32)).astype(BF)
-
-    kind = shape((lay.R // 2, lay.piece, n * width))
-    (keep, send), token = call(kernel, name, ins, [(kind, out)] * 2, grid=(lay.R // 2,), after=after)
-    return (keep, swap(send, "row", lay.R, 1)), token
+                total = (a[0, bit].astype(F32) + b[0, bit].astype(F32)).astype(BF)
+                target[0, :, starts[i] : starts[i] + widths[i]] = total
+
+    kind = shape((lay.R // 2, lay.piece, columns))
+    (keep, send, *passed), token = call(
+        kernel, name, ins, [(kind, out)] * 2, grid=(lay.R // 2,), after=after, passing=passing
+    )
+    return ((keep, swap(send, "row", lay.R, 1)), *passed), token
 
 
 def next_rows(lay, ids, pair, after, name):
@@ -574,21 +623,53 @@
     return got
 
 
+class Spread:
+    def __init__(self, lay, total):
+        self.lay = lay
+        self.pieces = {0: total}
+        for i in range(min(2, len(lay.split_bits))):
+            self.pieces[1 << i] = swap(total, "dp", lay.Q, lay.split_bits[i])
+
+    def forward(self, after, name):
+        lay, token = self.lay, after[0]
+        if len(lay.split_bits) >= 2:
+            (left, right), token = cut(lay, [self.pieces[1][None], self.pieces[2][None]], 2, after, name)
+            self.pieces[3] = (
+                swap(left[0], "dp", lay.Q, lay.split_bits[1]),
+                swap(right[0], "dp", lay.Q, lay.split_bits[0]),
+            )
+        for i, bit in list(enumerate(lay.split_bits))[2:]:
+            for q, piece in list(self.pieces.items()):
+                self.pieces[q | 1 << i] = jax.tree.map(lambda v: swap(v, "dp", lay.Q, bit), piece)
+        return token
+
+    def all(self):
+        return [self.pieces[q] for q in range(self.lay.s)]
+
+
 def finish(lay, ids, pieces, plan, name, after=()):
     outs = []
     for spans, transposed in plan:
         n = sum(c for _, c in spans)
         outs.append((shape((n, lay.block) if transposed else (lay.block, n), F32), vmem()))
+    arrays = jax.tree.leaves(pieces)
+    n_in = len(arrays)
     widest = max([HDIM] + [sum(c for _, c in spans) for spans, t in plan if t])
 
     def kernel(ids, *refs):
-        ins, results, scratch = refs[: lay.s], refs[lay.s : -1], refs[-1]
+        ins, results, scratch = list(refs[:n_in]), refs[n_in:-1], refs[-1]
+        values = []
+        for piece in pieces:
+            if isinstance(piece, tuple):
+                values.append(jnp.concatenate([ins.pop(0)[...], ins.pop(0)[...]], axis=1))
+            else:
+                values.append(ins.pop(0))
         for (spans, transposed), result in zip(plan, results):
             column = 0
             for first, n in spans:
                 for offset in range(lay.s):
                     rows = pl.ds(aligned(ids[1] ^ offset, lay.piece), lay.piece)
-                    value = ins[offset][:, first : first + n].astype(F32)
+                    value = values[offset][:, first : first + n].astype(F32)
                     if transposed:
                         scratch[rows, column : column + n] = value
                     else:
@@ -600,7 +681,7 @@
     return call(
         kernel,
         name,
-        [(ids, smem())] + [(p, vmem()) for p in pieces],
+        [(ids, smem())] + [(p, vmem()) for p in arrays],
         outs,
         scratch=[pltpu.VMEM((lay.block, widest), F32)],
         after=after,
@@ -938,10 +1019,15 @@
 
     def kernel(ids, x_ref, vo, vt, *refs):
         grad_refs, refs = refs[: len(grads)], refs[len(grads) :]
-        pieces, (own, other, sums, weight, sems) = refs[: joint.n], refs[joint.n :]
+        pieces, (own, other, sums, columns, weight, sems) = refs[: joint.n], refs[joint.n :]
         copies = joint.copies(ids, pieces, weight, sems)
         first = pl.program_id(0) == 0
-        pl.when(first)(lambda: start_all(copies))
+
+        def begin():
+            start_all(copies)
+            columns[...] = jnp.zeros_like(columns)
+
+        pl.when(first)(begin)
         values = x_ref[...].astype(F32)
         average, factor = row_stats(values)
         pl.when(first)(lambda: wait_all(copies))
@@ -951,11 +1037,14 @@
             column += width
         own[...] = total[:, :HALF].astype(BF)
         other[:, :HALF] = total[:, HALF:].astype(BF)
-        scaled = total * pair_row(vo, vt, V_GAIN1)
+        gain = pair_row(vo, vt, V_GAIN1)
+        product = total * ((values - average) * factor)
+        columns[0:1, :] += jnp.sum(product, axis=0, keepdims=True)
+        columns[1:2, :] += jnp.sum(total, axis=0, keepdims=True)
         lane = lax.broadcasted_iota(jnp.int32, (TILE, HDIM), 1)
         packed = jnp.zeros((TILE, HDIM), F32)
         parts = jnp.zeros((TILE, HDIM), F32)
-        for i, value in enumerate((scaled, scaled * ((values - average) * factor))):
+        for i, value in enumerate((total * gain, product * gain)):
             row_sum = jnp.sum(value, axis=1, keepdims=True)
             high = row_sum.astype(BF).astype(F32)
             packed = jnp.where(lane == 2 * i, high, jnp.where(lane == 2 * i + 1, row_sum - high, packed))
@@ -973,6 +1062,7 @@
             (shape((LEN, HALF)), row_tile(HALF)),
             (shape((LEN, HALF + HDIM)), row_tile(HALF + HDIM)),
             (shape((LEN, HDIM), F32), row_tile(HDIM)),
+            (shape((8, D), F32), whole(8, D)),
         ],
         grid=ROW_GRID,
         scratch=joint.scratch,
@@ -980,9 +1070,23 @@
     )
 
 
+MOST = LEN // 2
+
+
+def most_tiles(width):
+    return [
+        pl.BlockSpec((TILE, width), lambda i: (jnp.minimum(i, MOST // TILE - 1), 0)),
+        pl.BlockSpec((TILE, width), lambda i: (jnp.maximum(i - MOST // TILE, 0), 0)),
+    ]
+
+
+def in_most():
+    return pl.program_id(0) < MOST // TILE
+
+
 def down_project(ids, active, down, after):
     def kernel(ids, a_ref, *refs):
-        pieces, (own, other, weight, sems) = refs[: down.n], refs[down.n :]
+        pieces, (own, other, rest, weight, sems) = refs[: down.n], refs[down.n :]
         copies = down.copies(ids, pieces, weight, sems)
 
         def begin():
@@ -992,22 +1096,38 @@
         pl.when(pl.program_id(0) == 0)(begin)
         value = dot(a_ref[...], weight[...]).astype(BF)
         own[...] = value[:, :HALF]
-        other[...] = value[:, HALF:]
+        pl.when(in_most())(lambda: other.__setitem__(..., value[:, HALF:]))
+        pl.when(jnp.logical_not(in_most()))(lambda: rest.__setitem__(..., value[:, HALF:]))
 
     return call(
         kernel,
         "down_project",
         [(ids, smem()), (active, row_tile(active.shape[1]))] + down.operands,
-        [(shape((LEN, HALF)), row_tile(HALF))] * 2,
+        [(shape((LEN, HALF)), row_tile(HALF))]
+        + [(shape((n, HALF)), spec) for n, spec in zip((MOST, LEN - MOST), most_tiles(HALF))],
         grid=ROW_GRID,
         scratch=down.scratch,
         after=after,
     )
 
 
+def add_output(residual, own, got, bias, after):
+    def kernel(res, a, most, rest, bias, out):
+        b = jnp.where(in_most(), most[...], rest[...])
+        out[...] = (res[...] + (a[...].astype(F32) + b.astype(F32) + bias[...])).astype(BF)
+
+    return call(
+        kernel,
+        "add_output",
+        [(residual, row_tile(HALF)), (own, row_tile(HALF)), *zip(got, most_tiles(HALF)), (bias, whole(1, HALF))],
+        [(shape((LEN, HALF)), row_tile(HALF))],
+        grid=ROW_GRID,
+        after=after,
+    )
+
+
 def first_norm_backward(x, own, other, sums, vecs, res_grad, after):
-    def kernel(x_ref, po, pt, so, vo, res_ref, out, sums_ref):
-        pl.when(pl.program_id(0) == 0)(lambda: sums_ref.__setitem__(..., jnp.zeros_like(sums_ref)))
+    def kernel(x_ref, po, pt, so, vo, res_ref, out):
         values = x_ref[...].astype(F32)
         average, factor = row_stats(values)
         cent = (values[:, :HALF] - average) * factor
@@ -1017,15 +1137,13 @@
         second = (so[:, 1:2] + (got[:, 2:3] + got[:, 3:4])) * (1.0 / D)
         back = factor * (grad * vo[V_GAIN1 : V_GAIN1 + 1, :] - first - cent * second)
         out[...] = (res_ref[...] + back).astype(BF)
-        for i, value in enumerate((grad * cent, grad)):
-            sums_ref[i : i + 1, :] += jnp.sum(value, axis=0, keepdims=True)
 
     return call(
         kernel,
         "first_norm_backward",
         [(x, row_tile(D)), (own, row_tile(HALF)), (other, row_tile(HALF + HDIM)), (sums, row_tile(HDIM)),
          (vecs[0], whole(8, HALF)), (res_grad, row_tile(HALF))],
-        [(shape((LEN, HALF)), row_tile(HALF)), (shape((2, HALF), F32), whole(2, HALF))],
+        [(shape((LEN, HALF)), row_tile(HALF))],
         grid=ROW_GRID,
         after=after,
     )
@@ -1085,12 +1203,12 @@
     down_w = down_weight_of(down, down_weight)
     both_orders = [lay.order_a, lay.order_b]
     later_steps = range(len(lay.split_bits) - 1)
-    down_parts, token = weight_grad(lay, ids, [(cot, [active])], both_orders, "down_grad", (token,))
+    down_parts, token = halves_grad(lay, ids, cot, active, both_orders, "down_grad", (token,))
     down_parts, token = hold(down_parts, (token, *down.arrays()), "hold_down")
     down_red = Reduction(lay, ids, both_orders, down_parts)
 
     (hidden_grad, norm_part, up_bias_grad), token = hidden_backward(ids, cot, slope, up_w, down_w, (token,))
-    passed, token = weight_grad(lay, ids, [(full_two, [hidden_grad])], both_orders, "up_grad", (token,))
+    passed, token = halves_grad(lay, ids, full_two, hidden_grad, both_orders, "up_grad", (token,))
     passed = [norm_part, *passed]
     for _ in later_steps:
         passed, token = down_red.advance((token,), "down_sum", passed)
@@ -1106,83 +1224,91 @@
     (qkv_grad_b, joint_sums_b), token = attention_backward(
         prefix_length, qkv, att_grad, logs_b, attended_b, pair, pair, (token,)
     )
-    down_rows, token = first_rows(down_red, (token,), "down_rows")
-    parts_a, token = weight_grad(
-        lay, ids, [(full_one, [qkv_grad_a]), (branch_grad, [attended_a, attended_b])], [lay.order_a],
-        "joint_grad_a", (token,),
-    )
-    red_a = Reduction(lay, ids, [lay.order_a], parts_a)
-    parts_b, token = weight_grad(lay, ids, [(full_one, [qkv_grad_b])], [lay.order_b], "joint_grad_b", (token,))
-    red_b = Reduction(lay, ids, [lay.order_b], parts_b)
+    (down_rows,), token = first_rows(down_red, (token,), "down_rows")
+    output_parts, token = output_grad(lay, ids, branch_grad, (attended_a, attended_b), both_orders, "output_grad", (token,))
+    output_red = Reduction(lay, ids, both_orders, output_parts)
+    (first_own, first_send, row_sums, first_sums), token = project_backward(
+        ids, [qkv_grad_a, qkv_grad_b], x, vecs, joint_w, (token,)
+    )
+    down_rows, token = next_rows(lay, ids, down_rows, (token,), "down_rows_2")
+    for i in later_steps:
+        _, token = up_red.advance((token,), "up_sum", (), (output_red,) if i == 0 else ())
+    joint_parts, token = weight_grad(
+        lay,
+        ids,
+        [[(full_one, qkv_grad_a)], [(full_one, qkv_grad_b)]],
+        both_orders,
+        "joint_grad",
+        (sums_two, joint_sums_a, joint_sums_b, up_bias_grad, first_sums),
+        (token,),
+    )
+    joint_red = Reduction(lay, ids, both_orders, joint_parts)
+    (down_own, *down_send), token = down_project(ids, active, down_w, (token,))
+    (down_total,), token = row_total(lay, down_rows, (token,), "down_total")
+    (up_rows, *down_send), token = first_rows(up_red, (token,), "up_rows", down_send)
+    (layer_out,), token = add_output(
+        residual, down_own, [swap_cores(p) for p in down_send], down_bias.reshape(1, -1), (token,)
+    )
+    up_rows, token = next_rows(lay, ids, up_rows, (token,), "up_rows_2")
+    passed = [first_send]
     for _ in later_steps:
-        _, token = up_red.advance((token,), "up_sum")
-    down_rows, token = next_rows(lay, ids, down_rows, (token,), "down_rows_2")
-    (first_own, first_send, row_sums), token = project_backward(
-        ids, [qkv_grad_a, qkv_grad_b], x, vecs, joint_w, (token,)
-    )
-    (down_total, first_send), token = row_total(lay, down_rows, (token,), "down_total", (), [first_send])
-    first_got = swap_cores(first_send)
-    (down_own, down_send), token = down_project(ids, active, down_w, (token,))
-    up_rows, token = first_rows(up_red, (token,), "up_rows")
-    for _ in later_steps:
-        _, token = red_b.advance((token,), "joint_sum_b")
-    for _ in later_steps:
-        _, token = red_a.advance((token,), "joint_sum_a")
-    (tokens_grad, sums_one), token = first_norm_backward(
-        x, first_own, first_got, row_sums, vecs, res_grad, (token,)
-    )
-    small = Small(lay, (sums_one, sums_two, joint_sums_a, joint_sums_b, up_bias_grad))
-    up_rows, token = next_rows(lay, ids, up_rows, (token,), "up_rows_2")
-    rows_b, token = first_rows(red_b, (token,), "joint_rows_b")
+        passed, token = joint_red.advance((token,), "joint_sum", passed)
+    (tokens_grad,), token = first_norm_backward(
+        x, first_own, swap_cores(passed[0]), row_sums, vecs, res_grad, (token,)
+    )
     (ffn_total,), token = row_total(lay, up_rows, (token,), "up_total", [down_total])
-    ffn_pieces = spread(lay, rest_sum(lay, ffn_total))
-    token = small.step((token,))
-    rows_a, token = first_rows(red_a, (token,), "joint_rows_a")
-    token = small.step((token,))
-    rows_b, token = next_rows(lay, ids, rows_b, (token,), "joint_rows_b_2")
-    rows_a, token = next_rows(lay, ids, rows_a, (token,), "joint_rows_a_2")
-
-    layer_out = (
-        residual + (down_own.astype(F32) + swap_cores(down_send).astype(F32) + down_bias[None, :])
-    ).astype(BF)
-    token = small.step((token,))
-    (total_b,), token = row_total(lay, rows_b, (token,), "joint_total_b")
-    (joint_total,), token = row_total(lay, rows_a, (token,), "joint_total_a", [total_b])
+    ffn = Spread(lay, rest_sum(lay, ffn_total))
+    (joint_rows,), token = first_rows(joint_red, (token,), "joint_rows")
+    joint_rows, token = next_rows(lay, ids, joint_rows, (token,), "joint_rows_2")
+    token = ffn.forward((token,), "ffn_pieces")
+    (joint_total,), token = row_total(lay, joint_rows, (token,), "joint_total")
     joint_pieces = spread(lay, rest_sum(lay, joint_total))
-    token = small.finish((token,))
-    small = small.value.reshape(-1)
-    (grad_down, grad_up), token = finish(
-        lay, ids, ffn_pieces, [([(0, ff)], True), ([(ff, ff)], False)], "finish_ffn", (token,)
+    up_mid, o_mid = ff // 2, o_rows // 2
+    up_half = up_mid + o_mid
+    (grad_down, grad_up, grad_output), token = finish(
+        lay,
+        ids,
+        ffn.all(),
+        [
+            ([(0, ff)], True),
+            ([(ff, up_mid), (ff + up_half, up_mid)], False),
+            ([(ff + up_mid, o_mid), (ff + up_half + up_mid, o_mid)], True),
+        ],
+        "finish_ffn",
+        (token,),
     )
     mid = j_width // 2
-    (grad_joint, grad_output), token = finish(
+    (grad_joint, small), token = finish(
         lay,
         ids,
         joint_pieces,
-        [([(mid, mid), (0, mid)], False), ([(2 * mid, o_rows)], True)],
+        [([(0, mid), (mid + HDIM, mid)], False), ([(mid, HDIM)], False)],
         "finish_attention",
         (token,),
     )
+    small = small.reshape(-1)
+    joint_n, up_n = joint_bias.shape[0], up_bias.shape[0]
+    first_at = 4 * HALF + joint_n + up_n
+    sums_one = small[first_at : first_at + 2 * HALF] + swap_cores(small[first_at + 2 * HALF : first_at + 4 * HALF])
 
     def take(start, n):
         return lax.slice_in_dim(small, start, start + n, axis=0)
 
-    joint_n = joint_bias.shape[0]
     return (
         layer_out,
         tokens_grad,
+        sums_one[:HALF],
+        sums_one[HALF:],
+        grad_joint,
+        take(4 * HALF, joint_n),
+        grad_output,
+        take(2 * HALF, HALF),
         take(0, HALF),
         take(HALF, HALF),
-        grad_joint,
-        take(6 * HALF, joint_n),
-        grad_output,
-        take(4 * HALF, HALF),
-        take(2 * HALF, HALF),
+        grad_up,
+        take(4 * HALF + joint_n, up_n),
+        grad_down,
         take(3 * HALF, HALF),
-        grad_up,
-        take(6 * HALF + joint_n, up_bias.shape[0]),
-        grad_down,
-        take(5 * HALF, HALF),
     )
 
 

time: 314 us -> 300 us (0.955)
  waiting for transfers between devices: 123 us -> 107 us
  Pallas kernels: 118 us -> 122 us
    ppermute x49 -> x46, waiting for transfers between devices: 121 us -> 102 us  [swap(): return lax.ppermute(value, axis, [(i, i ^ bit) for i in range(size)])]
    pallas_call x50 -> x44, Pallas kernels: 118 us -> 122 us  [call(): pl.pallas_call(body, grid=grid, in_specs=[spec for _, spec in ins] + [any...]
    ppermute x49 -> x46, starting transfers between devices: 51.9 us -> 50.9 us  [swap(): return lax.ppermute(value, axis, [(i, i ^ bit) for i in range(size)])]
    unnamed x44 -> x38, local copies, waits for them, and re-layouts: 9.41 us -> 9.39 us
  transfers between devices with their start and end apart: 56 -> 55, of which waited for: 31 -> 26; matrix products, arithmetic and copies ran while one was open for 2% -> 2% of each run, Pallas kernels for 36% -> 38%
where the time goes in v3:
time: 300 us; the launch traced here: 299 us
  Pallas kernels  122 us (41%)
  waiting for transfers between devices  107 us (36%)
  starting transfers between devices  52.6 us (18%)
  local copies, waits for them, and re-layouts  15.1 us (5%)
    pallas_call x44, Pallas kernels, call(): pl.pallas_call(body, grid=grid, in_specs=[spec for _, spec in ins] + [any...  122 us
    ppermute x46, waiting for transfers between devices, swap(): return lax.ppermute(value, axis, [(i, i ^ bit) for i in range(size)])  102 us
    ppermute x46, starting transfers between devices, swap(): return lax.ppermute(value, axis, [(i, i ^ bit) for i in range(size)])  50.9 us
    unnamed x38, local copies, waits for them, and re-layouts  9.39 us
  transfers between devices with their start and end apart: 55, of which 26 were waited for; matrix products, arithmetic and copies ran while one was open for 2% of the time, Pallas kernels for 38%

profile of v3, /device:TPU:0, one launch (start us, length us, event | category | flops | bytes accessed | tf_op | source)
XLA Modules:
  0.0 299.1 jit_solution(18032202949190191015)
XLA Ops:
  5.0 4.7 %collective-permute-start.5 = (bf16[1,64,2048]{2,1,0:T(8,128)(2,1)}, bf16[1,64,2048]{2,1,0:T(8,128)(2,1)S(1)}, u32[]{:S(2)}, u32[]{:S(2)}) collective-permute-start(bf16[1,64,2048]{2,1,0:T(8,128)(2,1)} %maximum_bitcast_fusion), channel_id=1, source_target_pairs={{0,6},{2,4},{4,2},{6,0},{1,7},{3,5},{5,3},{7,1},{8,14},{10,12},{12... | collective-permute-start | bytes 786440 | tf_op jit(solution)/shard_map/ppermute | solution.py:83
  17.5 15.4 %collective-permute-done.4.refs_1_ = bf16[1,64,2048]{2,1,0:T(8,128)(2,1)} collective-permute-done((bf16[1,64,2048]{2,1,0:T(8,128)(2,1)}, bf16[1,64,2048]{2,1,0:T(8,128)(2,1)}, u32[]{:S(2)}, u32[]{:S(2)}) %collective-permute-start.4) | collective-permute-done | bytes 262176 | tf_op jit(solution)/shard_map/ppermute | solution.py:83
  32.9 2.0 joint_pieces_join.1
  39.8 13.7 %collective-permute-done.8.refs_1_.refs_3_.refs_0_ = bf16[1,64,2048]{2,1,0:T(8,128)(2,1)S(1)} collective-permute-done((bf16[1,64,2048]{2,1,0:T(8,128)(2,1)S(1)}, bf16[1,64,2048]{2,1,0:T(8,128)(2,1)S(1)}, u32[]{:S(2)}, u32[]{:S(2)}) %collective-permute-start.8) | collective-permute-done | bytes 262176 | tf_op jit(solution)/shard_map/ppermute | solution.py:83
  59.5 7.9 %collective-permute-done.9.refs_4_.refs_1_ = bf16[2,64,2048]{2,1,0:T(8,128)(2,1)S(1)} collective-permute-done((bf16[2,64,2048]{2,1,0:T(8,128)(2,1)S(1)}, bf16[2,64,2048]{2,1,0:T(8,128)(2,1)S(1)}, u32[]{:S(2)}, u32[]{:S(2)}) %collective-permute-start.9) | collective-permute-done | bytes 524320 | tf_op jit(solution)/shard_map/ppermute | solution.py:83
  71.3 7.3 %first_norm_project.1 = (bf16[1024,1024]{1,0:T(8,128)(2,1)}, bf16[1024,1536]{1,0:T(8,128)(2,1)S(1)}, f32[8,128]{1,0:T(8,128)S(1)}) custom-call(s32[3]{0:T(128)S(1)} %pad_add_fusion.refs_0_, bf16[1024,1024]{1,0:T(8,128)(2,1)S(1)} %get-tuple-element.167.refs_1_.refs_0_, f32[8,512]{1,0:T(8,128)S(1)} %stack.46.refs_4_.refs_2_.refs_6_, ...), custom_call_target="tpu_custom_call" | custom-call | flops 1 | bytes 8302500 | tf_op jit(solution)/shard_map/first_norm_project/pallas_call | solution.py:126
  78.6 4.0 %collective-permute-done.10.refs_1_.refs_0_ = bf16[1,512,256]{2,1,0:T(8,128)(2,1)S(1)} collective-permute-done((bf16[1,512,256]{2,1,0:T(8,128)(2,1)S(1)}, bf16[1,512,256]{2,1,0:T(8,128)(2,1)S(1)}, u32[]{:S(2)}, u32[]{:S(2)}) %collective-permute-start.10) | collective-permute-done | bytes 262176 | tf_op jit(solution)/shard_map/ppermute | solution.py:83
  83.4 3.2 %attention_first.1 = (bf16[1024,256]{1,0:T(8,128)(2,1)S(1)}, f32[2,1,1024]{2,1,0:T(1,128)S(1)}, f32[8,128]{1,0:T(8,128)S(1)}) custom-call(s32[1]{0:T(128)S(6)} %copy.55.refs_0_.refs_1_, bf16[1024,1536]{1,0:T(8,128)(2,1)S(1)} %get-tuple-element.183.refs_1_.refs_2_, f32[8,128]{1,0:T(8,128)S(1)} %get-tuple-element.184.refs_2_), custom_call_target="tpu_custom_call" | custom-call | flops 1 | bytes 4612500 | tf_op jit(solution)/shard_map/attention_first/pallas_call | solution.py:126
  89.9 5.3 %attention_second.1 = (bf16[1024,256]{1,0:T(8,128)(2,1)S(1)}, f32[2,1,1024]{2,1,0:T(1,128)S(1)}, bf16[1024,1024]{1,0:T(8,128)(2,1)S(1)}, f32[8,128]{1,0:T(8,128)S(1)}) custom-call(s32[3]{0:T(128)S(1)} %pad_add_fusion.refs_0_, s32[1]{0:T(128)S(6)} %copy.55.refs_0_.refs_1_, bf16[1024,1536]{1,0:T(8,128)(2,1)S(1)} %get-tuple-element.183.refs_1_.refs_2_, ...), custom_call_target="tpu_custom_call" | custom-call | flops 1 | bytes 6457500 | tf_op jit(solution)/shard_map/attention_second/pallas_call | solution.py:126
  95.5 2.1 collective-permute-done.16.refs_4_.refs_10_.refs_6_
  101.0 2.2 collective-permute-done.18.refs_3_
  103.3 12.3 %second_norm_up.1 = (f32[1024,512]{1,0:T(8,128)}, bf16[1024,1024]{1,0:T(8,128)(2,1)}, f32[1024,1]{1,0:T(8,128)}, bf16[1024,1024]{1,0:T(8,128)(2,1)}, bf16[1024,2...) custom-call(s32[3]{0:T(128)S(1)} %pad_add_fusion.refs_0_, ...), custom_call_target="tpu_custom_call" | custom-call | flops 1 | bytes 13837500 | tf_op jit(solution)/shard_map/second_norm_up/pallas_call | solution.py:126
  115.6 3.5 %collective-permute-done.20.refs_1_.refs_3_.refs_11_.refs_4_ = bf16[3,512,256]{2,1,0:T(8,128)(2,1)S(1)} collective-permute-done((bf16[3,512,256]{2,1,0:T(8,128)(2,1)S(1)}, bf16[3,512,256]{2,1,0:T(8,128)(2,1)S(1)}, u32[]{:S(2)}, u32[]{:S(2)}) %collective-permute-start.20) | collective-permute-done | bytes 786464 | tf_op jit(solution)/shard_map/ppermute | solution.py:83
  122.5 6.7 %down_grad.1 = (bf16[8,64,1024]{2,1,0:T(8,128)(2,1)S(1)}, bf16[8,64,1024]{2,1,0:T(8,128)(2,1)S(1)}, bf16[8,64,1024]{2,1,0:T(8,128)(2,1)S(1)}, bf16[8,64,1024]{2,1,0:T(8,128)(2,1)S(1)}, f32[8,128]{1,0:T(8,128)S(1)}) custom-call(s32[3]{0:T(128)S(1)} %pad_add_fusion.refs_0_, bf16[1024,1024]{1,0:T(8,128)(2,1)S(1)} %copy-done.1, ...), custom_call_target="tpu_custom_call" | custom-call | flops 1 | bytes 8302500 | tf_op jit(solution)/shard_map/down_grad/pallas_call | solution.py:126
  133.1 13.0 %hidden_backward.1 = (bf16[1024,2048]{1,0:T(8,128)(2,1)}, bf16[1024,1024]{1,0:T(8,128)(2,1)S(1)}, f32[1,2048]{1,0:T(1,128)S(1)}, f32[8,128]{1,0:T(8,128)S(1)}) custom-call(s32[3]{0:T(128)S(1)} %pad_add_fusion.refs_0_, bf16[1024,1024]{1,0:T(8,128)(2,1)S(1)} %copy-done.1, bf16[1024,2048]{1,0:T(8,128)(2,1)S(1)} %get-tuple-element.214.refs_2_, ...), custom_call_target="tpu_custom_call" | custom-call | flops 1 | bytes 15682500 | tf_op jit(solution)/shard_map/hidden_backward/pallas_call | solution.py:126
  146.2 2.2 copy-done.6
  148.4 6.7 %up_grad.1 = (bf16[8,64,1024]{2,1,0:T(8,128)(2,1)S(1)}, bf16[8,64,1024]{2,1,0:T(8,128)(2,1)S(1)}, bf16[8,64,1024]{2,1,0:T(8,128)(2,1)S(1)}, bf16[8,64,1024]{2,1,0:T(8,128)(2,1)S(1)}, f32[8,128]{1,0:T(8,128)S(1)}) custom-call(s32[3]{0:T(128)S(1)} %pad_add_fusion.refs_0_, bf16[1024,1024]{1,0:T(8,128)(2,1)S(1)} %copy-done.10, bf16[1024,2048]{1,0:T(8,128)(2,1)S(1)} %copy-done.6, ...), custom_call_target="tpu_custom_call" | custom-call | flops 1 | bytes 8302500 | tf_op jit(solution)/shard_map/up_grad/pallas_call | solution.py:126
  160.8 6.4 %second_norm_backward.1 = (bf16[1024,1024]{1,0:T(8,128)(2,1)S(1)}, f32[1024,512]{1,0:T(8,128)S(1)}, bf16[1024,512]{1,0:T(8,128)(2,1)S(1)}, f32[4,512]{1,0:T(4,128)S(1)}, f32[8,128]{1,0:T(8,128)S(1)}) custom-call(s32[3]{0:T(128)S(1)} %pad_add_fusion.refs_0_, bf16[1024,1024]{1,0:T(8,128)(2,1)S(1)} %copy-done.1, ...), custom_call_target="tpu_custom_call" | custom-call | flops 1 | bytes 8302500 | tf_op jit(solution)/shard_map/second_norm_backward/pallas_call | solution.py:126
  167.2 4.9 %attention_backward.2 = (bf16[1024,768]{1,0:T(8,128)(2,1)S(1)}, f32[2,1,256]{2,1,0:T(1,128)S(1)}, f32[8,128]{1,0:T(8,128)S(1)}) custom-call(s32[1]{0:T(128)S(6)} %copy.55.refs_0_.refs_1_, bf16[1024,1536]{1,0:T(8,128)(2,1)S(1)} %get-tuple-element.183.refs_1_.refs_2_, bf16[1024,512]{1,0:T(8,128)(2,1)S(1)} %get-tuple-element.228.refs_2_, ...), custom_call_target="tpu_custom_call" | custom-call | flops 1 | bytes 5535000 | tf_op jit(solution)/shard_map/attention_backward/pallas_call | solution.py:126
  172.1 4.7 %attention_backward.3 = (bf16[1024,768]{1,0:T(8,128)(2,1)S(1)}, f32[2,1,256]{2,1,0:T(1,128)S(1)}, f32[8,128]{1,0:T(8,128)S(1)}) custom-call(s32[1]{0:T(128)S(6)} %copy.55.refs_0_.refs_1_, bf16[1024,1536]{1,0:T(8,128)(2,1)S(1)} %get-tuple-element.183.refs_1_.refs_2_, bf16[1024,512]{1,0:T(8,128)(2,1)S(1)} %get-tuple-element.228.refs_2_, ...), custom_call_target="tpu_custom_call" | custom-call | flops 1 | bytes 5535000 | tf_op jit(solution)/shard_map/attention_backward/pallas_call | solution.py:126
  179.5 4.7 %output_grad.1 = (bf16[8,64,256]{2,1,0:T(8,128)(2,1)S(1)}, bf16[8,64,256]{2,1,0:T(8,128)(2,1)S(1)}, bf16[8,64,256]{2,1,0:T(8,128)(2,1)S(1)}, bf16[8,64,256]{2,1,0:T(8,128)(2,1)S(1)}, f32[8,128]{1,0:T(8,128)S(1)}) custom-call(s32[3]{0:T(128)S(1)} %pad_add_fusion.refs_0_, bf16[1024,1024]{1,0:T(8,128)(2,1)S(1)} %get-tuple-element.240.refs_1_, ...), custom_call_target="tpu_custom_call" | custom-call | flops 1 | bytes 1845000 | tf_op jit(solution)/shard_map/output_grad/pallas_call | solution.py:126
  185.9 7.8 %project_backward.1 = (bf16[1024,512]{1,0:T(8,128)(2,1)S(1)}, bf16[1024,640]{1,0:T(8,128)(2,1)S(1)}, f32[1024,128]{1,0:T(8,128)S(1)}, f32[8,1024]{1,0:T(8,128)S(1)}, f32[8,128]{1,0:T(8,128)S(1)}) custom-call(s32[3]{0:T(128)S(1)} %pad_add_fusion.refs_0_, bf16[1024,1024]{1,0:T(8,128)(2,1)S(1)} %get-tuple-element.167.refs_1_.refs_0_, ...), custom_call_target="tpu_custom_call" | custom-call | flops 1 | bytes 7380000 | tf_op jit(solution)/shard_map/project_backward/pallas_call | solution.py:126
  195.1 4.8 %collective-permute-done.29 = bf16[8,64,256]{2,1,0:T(8,128)(2,1)S(1)} collective-permute-done((bf16[8,64,256]{2,1,0:T(8,128)(2,1)S(1)}, bf16[8,64,256]{2,1,0:T(8,128)(2,1)S(1)}, u32[]{:S(2)}, u32[]{:S(2)}) %collective-permute-start.29) | collective-permute-done | bytes 262176 | tf_op jit(solution)/shard_map/ppermute | solution.py:83
  204.4 7.6 %joint_grad.1 = (bf16[8,64,896]{2,1,0:T(8,128)(2,1)S(1)}, bf16[8,64,896]{2,1,0:T(8,128)(2,1)S(1)}, bf16[8,64,768]{2,1,0:T(8,128)(2,1)S(1)}, bf16[8,64,768]{2,1,0:T(8,128)(2,1)S(1)}, f32[8,128]{1,0:T(8,128)S(1)}) custom-call(s32[3]{0:T(128)S(1)} %pad_add_fusion.refs_0_, bf16[1024,1024]{1,0:T(8,128)(2,1)S(1)} %copy-done.5, ...), custom_call_target="tpu_custom_call" | custom-call | flops 1 | bytes 9225000 | tf_op jit(solution)/shard_map/joint_grad/pallas_call | solution.py:126
  214.6 6.5 %down_project.1 = (bf16[1024,512]{1,0:T(8,128)(2,1)S(1)}, bf16[512,512]{1,0:T(8,128)(2,1)S(1)}, bf16[512,512]{1,0:T(8,128)(2,1)S(1)}, f32[8,128]{1,0:T(8,128)S(1)}) custom-call(s32[3]{0:T(128)S(1)} %pad_add_fusion.refs_0_, bf16[1024,2048]{1,0:T(8,128)(2,1)S(1)} %get-tuple-element.196.refs_2_.refs_1_, ...), custom_call_target="tpu_custom_call" | custom-call | flops 1 | bytes 8302500 | tf_op jit(solution)/shard_map/down_project/pallas_call | solution.py:126
  227.0 9.8 %collective-permute-done.40 = bf16[2,64,2560]{2,1,0:T(8,128)(2,1)S(1)} collective-permute-done((bf16[2,64,2560]{2,1,0:T(8,128)(2,1)S(1)}, bf16[2,64,2560]{2,1,0:T(8,128)(2,1)S(1)}, u32[]{:S(2)}, u32[]{:S(2)}) %collective-permute-start.40) | collective-permute-done | bytes 655392 | tf_op jit(solution)/shard_map/ppermute | solution.py:83
  242.1 3.0 %first_norm_backward.1 = (bf16[1024,512]{1,0:T(8,128)(2,1)}, f32[8,128]{1,0:T(8,128)S(1)}) custom-call(bf16[1024,1024]{1,0:T(8,128)(2,1)S(1)} %get-tuple-element.167.refs_1_.refs_0_, bf16[1024,512]{1,0:T(8,128)(2,1)S(1)} %get-tuple-element.278.refs_1_, bf16[1024,640]{1,0:T(8,128)(2,1)S(1)} %collective-permute-done.41.refs_2_, ...), custom_call_target="tpu_custom_call" | custom-call | flops 1 | bytes 5535000 | tf_op jit(solution)/shard_map/first_norm_backward/pallas_call | solution.py:126
  245.1 12.7 %collective-permute-done.44 = bf16[1,64,2560]{2,1,0:T(8,128)(2,1)S(1)} collective-permute-done((bf16[1,64,2560]{2,1,0:T(8,128)(2,1)S(1)}, bf16[1,64,2560]{2,1,0:T(8,128)(2,1)S(1)}, u32[]{:S(2)}, u32[]{:S(2)}) %collective-permute-start.44) | collective-permute-done | bytes 327712 | tf_op jit(solution)/shard_map/ppermute | solution.py:83
  261.4 10.2 %collective-permute-done.45 = bf16[2,64,1664]{2,1,0:T(8,128)(2,1)S(1)} collective-permute-done((bf16[2,64,1664]{2,1,0:T(8,128)(2,1)S(1)}, bf16[2,64,1664]{2,1,0:T(8,128)(2,1)S(1)}, u32[]{:S(2)}, u32[]{:S(2)}) %collective-permute-start.45) | collective-permute-done | bytes 426016 | tf_op jit(solution)/shard_map/ppermute | solution.py:83
  272.2 2.3 collective-permute-start.46
  275.8 7.5 %collective-permute-done.46 = bf16[1,64,1664]{2,1,0:T(8,128)(2,1)S(1)} collective-permute-done((bf16[1,64,1664]{2,1,0:T(8,128)(2,1)S(1)}, bf16[1,64,1664]{2,1,0:T(8,128)(2,1)S(1)}, u32[]{:S(2)}, u32[]{:S(2)}) %collective-permute-start.46) | collective-permute-done | bytes 213024 | tf_op jit(solution)/shard_map/ppermute | solution.py:83
  287.0 3.6 %finish_ffn.1 = (f32[2048,256]{1,0:T(8,128)}, f32[256,2048]{1,0:T(8,128)}, f32[512,256]{1,0:T(8,128)}, f32[8,128]{1,0:T(8,128)S(1)}) custom-call(s32[3]{0:T(128)S(1)} %pad_add_fusion.refs_0_, bf16[64,4608]{1,0:T(8,128)(2,1)S(1)} %get-tuple-element.307.refs_1_, bf16[64,4608]{1,0:T(8,128)(2,1)S(1)} %collective-permute-done.47.refs_2_, ...), custom_call_target="tpu_custom_call" | custom-call | flops 1 | bytes 1845000 | tf_op jit(solution)/shard_map/finish_ffn/pallas_call | solution.py:126
  (176 shorter events, 88.4 us)
Async XLA Ops:
  5.0 12.5 %collective-permute-start.5 = (bf16[1,64,2048]{2,1,0:T(8,128)(2,1)}, bf16[1,64,2048]{2,1,0:T(8,128)(2,1)S(1)}, u32[]{:S(2)}, u32[]{:S(2)}) collective-permute-start(bf16[1,64,2048]{2,1,0:T(8,128)(2,1)} %maximum_bitcast_fusion), channel_id=1, source_target_pairs={{0,6},{2,4},{4,2},{6,0},{1,7},{3,5},{5,3},{7,1},{8,14},{10,12},{12... | collective-permute-start | bytes 786440 | tf_op jit(solution)/shard_map/ppermute | solution.py:83
  9.6 23.2 %collective-permute-start.4 = (bf16[1,64,2048]{2,1,0:T(8,128)(2,1)}, bf16[1,64,2048]{2,1,0:T(8,128)(2,1)}, u32[]{:S(2)}, u32[]{:S(2)}) collective-permute-start(bf16[1,64,2048]{2,1,0:T(8,128)(2,1)} %maximum_bitcast_fusion), channel_id=1, source_target_pairs={{0,4},{2,6},{4,0},{6,2},{1,5},{3,7},{5,1},{7,3},{8,12},{10,14},{12... | collective-permute-start | bytes 786440 | tf_op jit(solution)/shard_map/ppermute | solution.py:83
  9.6 23.2 %collective-permute-start.3 = (bf16[1,64,2048]{2,1,0:T(8,128)(2,1)}, bf16[1,64,2048]{2,1,0:T(8,128)(2,1)}, u32[]{:S(2)}, u32[]{:S(2)}) collective-permute-start(bf16[1,64,2048]{2,1,0:T(8,128)(2,1)} %maximum_bitcast_fusion), channel_id=1, source_target_pairs={{0,2},{2,0},{4,6},{6,4},{1,3},{3,1},{5,7},{7,5},{8,10},{10,8},{12,... | collective-permute-start | bytes 786440 | tf_op jit(solution)/shard_map/ppermute | solution.py:83
  34.8 19.3 %collective-permute-start.7 = (bf16[3,64,2048]{2,1,0:T(8,128)(2,1)}, bf16[3,64,2048]{2,1,0:T(8,128)(2,1)S(1)}, u32[]{:S(2)}, u32[]{:S(2)}) collective-permute-start(bf16[3,64,2048]{2,1,0:T(8,128)(2,1)} %get-tuple-element.169.refs_3_.refs_5_.refs_4_.refs_8_.refs_6_), channel_id=1, source_target_pairs={{0,16},{8,24},{16,0},{24,8},{1,17},{9,25},{17,1},{25,9},{2,18},{10... | collective-permute-start | bytes 2359304 | tf_op jit(solution)/shard_map/ppermute | solution.py:83
  36.4 19.1 %collective-permute-start.6 = (bf16[3,64,2048]{2,1,0:T(8,128)(2,1)}, bf16[3,64,2048]{2,1,0:T(8,128)(2,1)}, u32[]{:S(2)}, u32[]{:S(2)}) collective-permute-start(bf16[3,64,2048]{2,1,0:T(8,128)(2,1)} %get-tuple-element.169.refs_3_.refs_5_.refs_4_.refs_8_.refs_6_), channel_id=1, source_target_pairs={{0,8},{8,0},{16,24},{24,16},{1,9},{9,1},{17,25},{25,17},{2,10},{10... | collective-permute-start | bytes 2359304 | tf_op jit(solution)/shard_map/ppermute | solution.py:83
  39.7 13.7 %collective-permute-start.8 = (bf16[1,64,2048]{2,1,0:T(8,128)(2,1)S(1)}, bf16[1,64,2048]{2,1,0:T(8,128)(2,1)S(1)}, u32[]{:S(2)}, u32[]{:S(2)}) collective-permute-start(bf16[1,64,2048]{2,1,0:T(8,128)(2,1)S(1)} %bitcast.118), channel_id=1, source_target_pairs={{0,4},{2,6},{4,0},{6,2},{1,5},{3,7},{5,1},{7,3},{8,12},{10,14},{12... | collective-permute-start | bytes 786440 | tf_op jit(solution)/shard_map/ppermute | solution.py:83
  53.5 13.9 %collective-permute-start.9 = (bf16[2,64,2048]{2,1,0:T(8,128)(2,1)S(1)}, bf16[2,64,2048]{2,1,0:T(8,128)(2,1)S(1)}, u32[]{:S(2)}, u32[]{:S(2)}) collective-permute-start(bf16[2,64,2048]{2,1,0:T(8,128)(2,1)S(1)} %get-tuple-element.175), channel_id=1, source_target_pairs={{0,2},{2,0},{4,6},{6,4},{1,3},{3,1},{5,7},{7,5},{8,10},{10,8},{12,... | collective-permute-start | bytes 1572872 | tf_op jit(solution)/shard_map/ppermute | solution.py:83
  67.5 19.1 %collective-permute-start.15 = (bf16[3,64,2048]{2,1,0:T(8,128)(2,1)S(1)}, bf16[3,64,2048]{2,1,0:T(8,128)(2,1)S(1)}, u32[]{:S(2)}, u32[]{:S(2)}) collective-permute-start(bf16[3,64,2048]{2,1,0:T(8,128)(2,1)S(1)} %get-tuple-element.179.refs_11_.refs_1_.refs_7_.refs_3_), channel_id=1, source_target_pairs={{0,16},{8,24},{16,0},{24,8},{1,17},{9,25},{17,1},{25,9},{2,18},{10... | collective-permute-start | bytes 2359304 | tf_op jit(solution)/shard_map/ppermute | solution.py:83
  68.8 17.8 %collective-permute-start.14 = (bf16[3,64,2048]{2,1,0:T(8,128)(2,1)S(1)}, bf16[3,64,2048]{2,1,0:T(8,128)(2,1)S(1)}, u32[]{:S(2)}, u32[]{:S(2)}) collective-permute-start(bf16[3,64,2048]{2,1,0:T(8,128)(2,1)S(1)} %get-tuple-element.179.refs_11_.refs_1_.refs_7_.refs_3_), channel_id=1, source_target_pairs={{0,8},{8,0},{16,24},{24,16},{1,9},{9,1},{17,25},{25,17},{2,10},{10... | collective-permute-start | bytes 2359304 | tf_op jit(solution)/shard_map/ppermute | solution.py:83
  82.6 12.8 %collective-permute-start.13 = (bf16[2,512,256]{2,1,0:T(8,128)(2,1)S(1)}, bf16[2,512,256]{2,1,0:T(8,128)(2,1)S(1)}, u32[]{:S(2)}, u32[]{:S(2)}) collective-permute-start(bf16[2,512,256]{2,1,0:T(8,128)(2,1)S(1)} %get-tuple-element.182), channel_id=1, source_target_pairs={{0,2},{2,0},{4,6},{6,4},{1,3},{3,1},{5,7},{7,5},{8,10},{10,8},{12,... | collective-permute-start | bytes 1572872 | tf_op jit(solution)/shard_map/ppermute | solution.py:83
  99.1 20.0 %collective-permute-start.20 = (bf16[3,512,256]{2,1,0:T(8,128)(2,1)S(1)}, bf16[3,512,256]{2,1,0:T(8,128)(2,1)S(1)}, u32[]{:S(2)}, u32[]{:S(2)}) collective-permute-start(bf16[3,512,256]{2,1,0:T(8,128)(2,1)S(1)} %get-tuple-element.197.refs_1_.refs_9_.refs_2_), channel_id=1, source_target_pairs={{0,16},{8,24},{16,0},{24,8},{1,17},{9,25},{17,1},{25,9},{2,18},{10... | collective-permute-start | bytes 2359304 | tf_op jit(solution)/shard_map/ppermute | solution.py:83
  99.5 19.6 %collective-permute-start.19 = (bf16[3,512,256]{2,1,0:T(8,128)(2,1)S(1)}, bf16[3,512,256]{2,1,0:T(8,128)(2,1)S(1)}, u32[]{:S(2)}, u32[]{:S(2)}) collective-permute-start(bf16[3,512,256]{2,1,0:T(8,128)(2,1)S(1)} %get-tuple-element.197.refs_1_.refs_9_.refs_2_), channel_id=1, source_target_pairs={{0,8},{8,0},{16,24},{24,16},{1,9},{9,1},{17,25},{25,17},{2,10},{10... | collective-permute-start | bytes 2359304 | tf_op jit(solution)/shard_map/ppermute | solution.py:83
  131.0 24.1 %collective-permute-start.23 = (bf16[8,64,1024]{2,1,0:T(8,128)(2,1)S(1)}, bf16[8,64,1024]{2,1,0:T(8,128)(2,1)S(1)}, u32[]{:S(2)}, u32[]{:S(2)}) collective-permute-start(bf16[8,64,1024]{2,1,0:T(8,128)(2,1)S(1)} %get-tuple-element.210), channel_id=1, source_target_pairs={{0,8},{8,0},{16,24},{24,16},{1,9},{9,1},{17,25},{25,17},{2,10},{10... | collective-permute-start | bytes 3145736 | tf_op jit(solution)/shard_map/ppermute | solution.py:83
  132.5 22.9 %collective-permute-start.24 = (bf16[8,64,1024]{2,1,0:T(8,128)(2,1)S(1)}, bf16[8,64,1024]{2,1,0:T(8,128)(2,1)S(1)}, u32[]{:S(2)}, u32[]{:S(2)}) collective-permute-start(bf16[8,64,1024]{2,1,0:T(8,128)(2,1)S(1)} %get-tuple-element.212), channel_id=1, source_target_pairs={{0,16},{8,24},{16,0},{24,8},{1,17},{9,25},{17,1},{25,9},{2,18},{10... | collective-permute-start | bytes 3145736 | tf_op jit(solution)/shard_map/ppermute | solution.py:83
  156.7 20.2 %collective-permute-start.26 = (bf16[4,64,1024]{2,1,0:T(8,128)(2,1)S(1)}, bf16[4,64,1024]{2,1,0:T(8,128)(2,1)S(1)}, u32[]{:S(2)}, u32[]{:S(2)}) collective-permute-start(bf16[4,64,1024]{2,1,0:T(8,128)(2,1)S(1)} %get-tuple-element.242), channel_id=1, source_target_pairs={{0,16},{8,24},{16,0},{24,8},{1,17},{9,25},{17,1},{25,9},{2,18},{10... | collective-permute-start | bytes 1572872 | tf_op jit(solution)/shard_map/ppermute | solution.py:83
  157.9 19.0 %collective-permute-start.27 = (bf16[4,64,1024]{2,1,0:T(8,128)(2,1)S(1)}, bf16[4,64,1024]{2,1,0:T(8,128)(2,1)S(1)}, u32[]{:S(2)}, u32[]{:S(2)}) collective-permute-start(bf16[4,64,1024]{2,1,0:T(8,128)(2,1)S(1)} %get-tuple-element.244), channel_id=1, source_target_pairs={{0,8},{8,0},{16,24},{24,16},{1,9},{9,1},{17,25},{25,17},{2,10},{10... | collective-permute-start | bytes 1572872 | tf_op jit(solution)/shard_map/ppermute | solution.py:83
  158.4 36.7 %collective-permute-start.28 = (bf16[8,64,1024]{2,1,0:T(8,128)(2,1)S(1)}, bf16[8,64,1024]{2,1,0:T(8,128)(2,1)S(1)}, u32[]{:S(2)}, u32[]{:S(2)}) collective-permute-start(bf16[8,64,1024]{2,1,0:T(8,128)(2,1)S(1)} %get-tuple-element.250), channel_id=1, source_target_pairs={{0,8},{8,0},{16,24},{24,16},{1,9},{9,1},{17,25},{25,17},{2,10},{10... | collective-permute-start | bytes 3145736 | tf_op jit(solution)/shard_map/ppermute | solution.py:83
  159.9 35.2 %collective-permute-start.30 = (bf16[8,64,1024]{2,1,0:T(8,128)(2,1)S(1)}, bf16[8,64,1024]{2,1,0:T(8,128)(2,1)S(1)}, u32[]{:S(2)}, u32[]{:S(2)}) collective-permute-start(bf16[8,64,1024]{2,1,0:T(8,128)(2,1)S(1)} %get-tuple-element.254), channel_id=1, source_target_pairs={{0,16},{8,24},{16,0},{24,8},{1,17},{9,25},{17,1},{25,9},{2,18},{10... | collective-permute-start | bytes 3145736 | tf_op jit(solution)/shard_map/ppermute | solution.py:83
  177.7 16.0 %collective-permute-start.32 = (bf16[2,64,2048]{2,1,0:T(8,128)(2,1)S(1)}, bf16[2,64,2048]{2,1,0:T(8,128)(2,1)S(1)}, u32[]{:S(2)}, u32[]{:S(2)}) collective-permute-start(bf16[2,64,2048]{2,1,0:T(8,128)(2,1)S(1)} %get-tuple-element.258), channel_id=1, source_target_pairs={{0,2},{2,0},{4,6},{6,4},{1,3},{3,1},{5,7},{7,5},{8,10},{10,8},{12,... | collective-permute-start | bytes 1572872 | tf_op jit(solution)/shard_map/ppermute | solution.py:83
  184.2 15.8 %collective-permute-start.29 = (bf16[8,64,256]{2,1,0:T(8,128)(2,1)S(1)}, bf16[8,64,256]{2,1,0:T(8,128)(2,1)S(1)}, u32[]{:S(2)}, u32[]{:S(2)}) collective-permute-start(bf16[8,64,256]{2,1,0:T(8,128)(2,1)S(1)} %get-tuple-element.252), channel_id=1, source_target_pairs={{0,8},{8,0},{16,24},{24,16},{1,9},{9,1},{17,25},{25,17},{2,10},{10... | collective-permute-start | bytes 786440 | tf_op jit(solution)/shard_map/ppermute | solution.py:83
  184.8 15.2 %collective-permute-start.31 = (bf16[8,64,256]{2,1,0:T(8,128)(2,1)S(1)}, bf16[8,64,256]{2,1,0:T(8,128)(2,1)S(1)}, u32[]{:S(2)}, u32[]{:S(2)}) collective-permute-start(bf16[8,64,256]{2,1,0:T(8,128)(2,1)S(1)} %get-tuple-element.256), channel_id=1, source_target_pairs={{0,16},{8,24},{16,0},{24,8},{1,17},{9,25},{17,1},{25,9},{2,18},{10... | collective-permute-start | bytes 786440 | tf_op jit(solution)/shard_map/ppermute | solution.py:83
  201.2 20.0 %collective-permute-start.33 = (bf16[4,64,1280]{2,1,0:T(8,128)(2,1)S(1)}, bf16[4,64,1280]{2,1,0:T(8,128)(2,1)S(1)}, u32[]{:S(2)}, u32[]{:S(2)}) collective-permute-start(bf16[4,64,1280]{2,1,0:T(8,128)(2,1)S(1)} %get-tuple-element.265), channel_id=1, source_target_pairs={{0,16},{8,24},{16,0},{24,8},{1,17},{9,25},{17,1},{25,9},{2,18},{10... | collective-permute-start | bytes 1966088 | tf_op jit(solution)/shard_map/ppermute | solution.py:83
  202.2 19.1 %collective-permute-start.34 = (bf16[4,64,1280]{2,1,0:T(8,128)(2,1)S(1)}, bf16[4,64,1280]{2,1,0:T(8,128)(2,1)S(1)}, u32[]{:S(2)}, u32[]{:S(2)}) collective-permute-start(bf16[4,64,1280]{2,1,0:T(8,128)(2,1)S(1)} %get-tuple-element.267), channel_id=1, source_target_pairs={{0,8},{8,0},{16,24},{24,16},{1,9},{9,1},{17,25},{25,17},{2,10},{10... | collective-permute-start | bytes 1966088 | tf_op jit(solution)/shard_map/ppermute | solution.py:83
  202.7 18.5 %collective-permute-start.35 = (bf16[1,64,2048]{2,1,0:T(8,128)(2,1)S(1)}, bf16[1,64,2048]{2,1,0:T(8,128)(2,1)S(1)}, u32[]{:S(2)}, u32[]{:S(2)}) collective-permute-start(bf16[1,64,2048]{2,1,0:T(8,128)(2,1)S(1)} %get-tuple-element.269), channel_id=1, source_target_pairs={{0,4},{2,6},{4,0},{6,2},{1,5},{3,7},{5,1},{7,3},{8,12},{10,14},{12... | collective-permute-start | bytes 786440 | tf_op jit(solution)/shard_map/ppermute | solution.py:83
  212.0 25.6 %collective-permute-start.38 = (bf16[8,64,896]{2,1,0:T(8,128)(2,1)S(1)}, bf16[8,64,896]{2,1,0:T(8,128)(2,1)S(1)}, u32[]{:S(2)}, u32[]{:S(2)}) collective-permute-start(bf16[8,64,896]{2,1,0:T(8,128)(2,1)S(1)} %get-tuple-element.280), channel_id=1, source_target_pairs={{0,8},{8,0},{16,24},{24,16},{1,9},{9,1},{17,25},{25,17},{2,10},{10... | collective-permute-start | bytes 2752520 | tf_op jit(solution)/shard_map/ppermute | solution.py:83
  213.5 24.1 %collective-permute-start.39 = (bf16[8,64,768]{2,1,0:T(8,128)(2,1)S(1)}, bf16[8,64,768]{2,1,0:T(8,128)(2,1)S(1)}, u32[]{:S(2)}, u32[]{:S(2)}) collective-permute-start(bf16[8,64,768]{2,1,0:T(8,128)(2,1)S(1)} %get-tuple-element.282), channel_id=1, source_target_pairs={{0,16},{8,24},{16,0},{24,8},{1,17},{9,25},{17,1},{25,9},{2,18},{10... | collective-permute-start | bytes 2359304 | tf_op jit(solution)/shard_map/ppermute | solution.py:83
  222.2 14.6 %collective-permute-start.40 = (bf16[2,64,2560]{2,1,0:T(8,128)(2,1)S(1)}, bf16[2,64,2560]{2,1,0:T(8,128)(2,1)S(1)}, u32[]{:S(2)}, u32[]{:S(2)}) collective-permute-start(bf16[2,64,2560]{2,1,0:T(8,128)(2,1)S(1)} %get-tuple-element.284), channel_id=1, source_target_pairs={{0,2},{2,0},{4,6},{6,4},{1,3},{3,1},{5,7},{7,5},{8,10},{10,8},{12,... | collective-permute-start | bytes 1966088 | tf_op jit(solution)/shard_map/ppermute | solution.py:83
  238.8 21.7 %collective-permute-start.42 = (bf16[4,64,896]{2,1,0:T(8,128)(2,1)S(1)}, bf16[4,64,896]{2,1,0:T(8,128)(2,1)S(1)}, u32[]{:S(2)}, u32[]{:S(2)}) collective-permute-start(bf16[4,64,896]{2,1,0:T(8,128)(2,1)S(1)} %get-tuple-element.294), channel_id=1, source_target_pairs={{0,16},{8,24},{16,0},{24,8},{1,17},{9,25},{17,1},{25,9},{2,18},{10... | collective-permute-start | bytes 1376264 | tf_op jit(solution)/shard_map/ppermute | solution.py:83
  239.9 20.6 %collective-permute-start.43 = (bf16[4,64,768]{2,1,0:T(8,128)(2,1)S(1)}, bf16[4,64,768]{2,1,0:T(8,128)(2,1)S(1)}, u32[]{:S(2)}, u32[]{:S(2)}) collective-permute-start(bf16[4,64,768]{2,1,0:T(8,128)(2,1)S(1)} %get-tuple-element.296), channel_id=1, source_target_pairs={{0,8},{8,0},{16,24},{24,16},{1,9},{9,1},{17,25},{25,17},{2,10},{10... | collective-permute-start | bytes 1179656 | tf_op jit(solution)/shard_map/ppermute | solution.py:83
  240.4 17.4 %collective-permute-start.44 = (bf16[1,64,2560]{2,1,0:T(8,128)(2,1)S(1)}, bf16[1,64,2560]{2,1,0:T(8,128)(2,1)S(1)}, u32[]{:S(2)}, u32[]{:S(2)}) collective-permute-start(bf16[1,64,2560]{2,1,0:T(8,128)(2,1)S(1)} %get-tuple-element.299), channel_id=1, source_target_pairs={{0,4},{2,6},{4,0},{6,2},{1,5},{3,7},{5,1},{7,3},{8,12},{10,14},{12... | collective-permute-start | bytes 983048 | tf_op jit(solution)/shard_map/ppermute | solution.py:83
  257.9 16.6 %collective-permute-start.48 = (bf16[64,4608]{1,0:T(8,128)(2,1)S(1)}, bf16[64,4608]{1,0:T(8,128)(2,1)S(1)}, u32[]{:S(2)}, u32[]{:S(2)}) collective-permute-start(bf16[64,4608]{1,0:T(8,128)(2,1)S(1)} %get-tuple-element.307.refs_1_), channel_id=1, source_target_pairs={{0,16},{8,24},{16,0},{24,8},{1,17},{9,25},{17,1},{25,9},{2,18},{10... | collective-permute-start | bytes 1769480 | tf_op jit(solution)/shard_map/ppermute | solution.py:83
  259.1 15.4 %collective-permute-start.47 = (bf16[64,4608]{1,0:T(8,128)(2,1)S(1)}, bf16[64,4608]{1,0:T(8,128)(2,1)S(1)}, u32[]{:S(2)}, u32[]{:S(2)}) collective-permute-start(bf16[64,4608]{1,0:T(8,128)(2,1)S(1)} %get-tuple-element.307.refs_1_), channel_id=1, source_target_pairs={{0,8},{8,0},{16,24},{24,16},{1,9},{9,1},{17,25},{25,17},{2,10},{10... | collective-permute-start | bytes 1769480 | tf_op jit(solution)/shard_map/ppermute | solution.py:83
  (42 other events, 289.6 us)

commit v4 on v3

--- a/solution.py
+++ b/solution.py
@@ -111,6 +111,7 @@
     "down_project": 9,
     "joint_sum": 32,
 }
+WIDE = {"second_norm_up": 18, "hidden_backward": 18, "attention_second": 18}
 COST_SCALE = 0.25 * 3.69e6
 
 
@@ -132,7 +133,7 @@
         + [shape(a.shape, a.dtype) for a in passing]
         + [shape((8, HDIM), F32)],
         scratch_shapes=list(scratch),
-        compiler_params=params(mib or (8 if "sum" in name or "rows" in name else 18 if name in COST else 8)),
+        compiler_params=params(mib or (WIDE.get(name, 12) if name in COST else 8)),
         input_output_aliases={n_in + n_after + i: n_out + i for i in range(n_pass)},
         cost_estimate=pl.CostEstimate(
             flops=1, bytes_accessed=int(COST_SCALE * COST.get(name, 2)), transcendentals=0
@@ -461,7 +462,7 @@
         [(shape((lay.R * lay.s // 2, lay.piece, width)), out)] * n_out,
         grid=(lay.R,),
         after=after,
-        mib=18,
+        mib=12,
     )
 
 
@@ -647,11 +648,13 @@
         return [self.pieces[q] for q in range(self.lay.s)]
 
 
-def finish(lay, ids, pieces, plan, name, after=()):
+def finish(lay, ids, pieces, plan, name, after=(), small=None):
     outs = []
     for spans, transposed in plan:
         n = sum(c for _, c in spans)
         outs.append((shape((n, lay.block) if transposed else (lay.block, n), F32), vmem()))
+    if small:
+        outs += [(shape((rows, HDIM), F32), vmem()) for rows in small[1]]
     arrays = jax.tree.leaves(pieces)
     n_in = len(arrays)
     widest = max([HDIM] + [sum(c for _, c in spans) for spans, t in plan if t])
@@ -677,6 +680,14 @@
                 column += n
             if transposed:
                 result[...] = scratch[:, :column].T
+        if small:
+            for offset in range(lay.s):
+                rows = pl.ds(aligned(ids[1] ^ offset, lay.piece), lay.piece)
+                scratch[rows, :HDIM] = values[offset][:, small[0] : small[0] + HDIM].astype(F32)
+            row = 0
+            for count, result in zip(small[1], results[len(plan) :]):
+                result[...] = scratch[row : row + count, :HDIM]
+                row += count
 
     return call(
         kernel,
@@ -685,7 +696,7 @@
         outs,
         scratch=[pltpu.VMEM((lay.block, widest), F32)],
         after=after,
-        mib=18,
+        mib=12,
     )
 
 
@@ -1278,37 +1289,35 @@
         (token,),
     )
     mid = j_width // 2
-    (grad_joint, small), token = finish(
+    counts = [HALF] * 4 + [joint_bias.shape[0], up_bias.shape[0], 2 * HALF, 2 * HALF]
+    (grad_joint, *small), token = finish(
         lay,
         ids,
         joint_pieces,
-        [([(0, mid), (mid + HDIM, mid)], False), ([(mid, HDIM)], False)],
+        [([(0, mid), (mid + HDIM, mid)], False)],
         "finish_attention",
         (token,),
-    )
-    small = small.reshape(-1)
-    joint_n, up_n = joint_bias.shape[0], up_bias.shape[0]
-    first_at = 4 * HALF + joint_n + up_n
-    sums_one = small[first_at : first_at + 2 * HALF] + swap_cores(small[first_at + 2 * HALF : first_at + 4 * HALF])
-
-    def take(start, n):
-        return lax.slice_in_dim(small, start, start + n, axis=0)
-
+        (mid, [n // HDIM for n in counts]),
+    )
+    sums_one = (small[6] + swap_cores(small[7])).reshape(-1)
+    second_gain_grad, second_shift_grad, output_bias_grad, down_bias_grad, joint_bias_grad, up_bias_grad = [
+        v.reshape(-1) for v in small[:6]
+    ]
     return (
         layer_out,
         tokens_grad,
         sums_one[:HALF],
         sums_one[HALF:],
         grad_joint,
-        take(4 * HALF, joint_n),
+        joint_bias_grad,
         grad_output,
-        take(2 * HALF, HALF),
-        take(0, HALF),
-        take(HALF, HALF),
+        output_bias_grad,
+        second_gain_grad,
+        second_shift_grad,
         grad_up,
-        take(4 * HALF + joint_n, up_n),
+        up_bias_grad,
         grad_down,
-        take(3 * HALF, HALF),
+        down_bias_grad,
     )
 
 

time: 300 us -> 298 us (level)
  transfers between devices with their start and end apart: 55 -> 55, of which waited for: 26 -> 26; matrix products, arithmetic and copies ran while one was open for 2% -> 1% of each run, Pallas kernels for 38% -> 38%
where the time goes in v4:
time: 298 us
  Pallas kernels  121 us (41%)
  waiting for transfers between devices  108 us (36%)
  starting transfers between devices  52.6 us (18%)
  local copies, waits for them, and re-layouts  13.3 us (4%)
    pallas_call x44, Pallas kernels, call(): pl.pallas_call(body, grid=grid, in_specs=[spec for _, spec in ins] + [any...  121 us
    ppermute x46, waiting for transfers between devices, swap(): return lax.ppermute(value, axis, [(i, i ^ bit) for i in range(size)])  102 us
    ppermute x46, starting transfers between devices, swap(): return lax.ppermute(value, axis, [(i, i ^ bit) for i in range(size)])  50.9 us
    unnamed x38, local copies, waits for them, and re-layouts  9.4 us
  transfers between devices with their start and end apart: 55, of which 26 were waited for; matrix products, arithmetic and copies ran while one was open for 1% of the time, Pallas kernels for 38%

profile of v4, /device:TPU:0, one launch (start us, length us, event | category | flops | bytes accessed | tf_op | source)
XLA Modules:
  0.0 297.9 jit_solution(15213077921546895374)
XLA Ops:
  5.0 4.7 %collective-permute-start.5 = (bf16[1,64,2048]{2,1,0:T(8,128)(2,1)}, bf16[1,64,2048]{2,1,0:T(8,128)(2,1)S(1)}, u32[]{:S(2)}, u32[]{:S(2)}) collective-permute-start(bf16[1,64,2048]{2,1,0:T(8,128)(2,1)} %maximum_bitcast_fusion), channel_id=1, source_target_pairs={{0,6},{2,4},{4,2},{6,0},{1,7},{3,5},{5,3},{7,1},{8,14},{10,12},{12... | collective-permute-start | bytes 786440 | tf_op jit(solution)/shard_map/ppermute | solution.py:83
  17.5 15.4 %collective-permute-done.4.refs_1_ = bf16[1,64,2048]{2,1,0:T(8,128)(2,1)} collective-permute-done((bf16[1,64,2048]{2,1,0:T(8,128)(2,1)}, bf16[1,64,2048]{2,1,0:T(8,128)(2,1)}, u32[]{:S(2)}, u32[]{:S(2)}) %collective-permute-start.4) | collective-permute-done | bytes 262176 | tf_op jit(solution)/shard_map/ppermute | solution.py:83
  32.9 2.0 joint_pieces_join.1
  39.8 13.7 %collective-permute-done.8.refs_1_.refs_3_.refs_0_ = bf16[1,64,2048]{2,1,0:T(8,128)(2,1)S(1)} collective-permute-done((bf16[1,64,2048]{2,1,0:T(8,128)(2,1)S(1)}, bf16[1,64,2048]{2,1,0:T(8,128)(2,1)S(1)}, u32[]{:S(2)}, u32[]{:S(2)}) %collective-permute-start.8) | collective-permute-done | bytes 262176 | tf_op jit(solution)/shard_map/ppermute | solution.py:83
  59.5 7.9 %collective-permute-done.9.refs_4_.refs_1_ = bf16[2,64,2048]{2,1,0:T(8,128)(2,1)S(1)} collective-permute-done((bf16[2,64,2048]{2,1,0:T(8,128)(2,1)S(1)}, bf16[2,64,2048]{2,1,0:T(8,128)(2,1)S(1)}, u32[]{:S(2)}, u32[]{:S(2)}) %collective-permute-start.9) | collective-permute-done | bytes 524320 | tf_op jit(solution)/shard_map/ppermute | solution.py:83
  71.3 7.3 %first_norm_project.1 = (bf16[1024,1024]{1,0:T(8,128)(2,1)}, bf16[1024,1536]{1,0:T(8,128)(2,1)S(1)}, f32[8,128]{1,0:T(8,128)S(1)}) custom-call(s32[3]{0:T(128)S(1)} %pad_add_fusion.refs_0_, bf16[1024,1024]{1,0:T(8,128)(2,1)S(1)} %get-tuple-element.174.refs_1_.refs_0_, f32[8,512]{1,0:T(8,128)S(1)} %stack.46.refs_4_.refs_2_.refs_6_, ...), custom_call_target="tpu_custom_call" | custom-call | flops 1 | bytes 8302500 | tf_op jit(solution)/shard_map/first_norm_project/pallas_call | solution.py:127
  78.6 4.0 %collective-permute-done.10.refs_1_.refs_0_ = bf16[1,512,256]{2,1,0:T(8,128)(2,1)S(1)} collective-permute-done((bf16[1,512,256]{2,1,0:T(8,128)(2,1)S(1)}, bf16[1,512,256]{2,1,0:T(8,128)(2,1)S(1)}, u32[]{:S(2)}, u32[]{:S(2)}) %collective-permute-start.10) | collective-permute-done | bytes 262176 | tf_op jit(solution)/shard_map/ppermute | solution.py:83
  83.4 3.2 %attention_first.1 = (bf16[1024,256]{1,0:T(8,128)(2,1)S(1)}, f32[2,1,1024]{2,1,0:T(1,128)S(1)}, f32[8,128]{1,0:T(8,128)S(1)}) custom-call(s32[1]{0:T(128)S(6)} %copy.55.refs_0_.refs_1_, bf16[1024,1536]{1,0:T(8,128)(2,1)S(1)} %get-tuple-element.190.refs_1_.refs_2_, f32[8,128]{1,0:T(8,128)S(1)} %get-tuple-element.191.refs_2_), custom_call_target="tpu_custom_call" | custom-call | flops 1 | bytes 4612500 | tf_op jit(solution)/shard_map/attention_first/pallas_call | solution.py:127
  89.9 5.4 %attention_second.1 = (bf16[1024,256]{1,0:T(8,128)(2,1)S(1)}, f32[2,1,1024]{2,1,0:T(1,128)S(1)}, bf16[1024,1024]{1,0:T(8,128)(2,1)S(1)}, f32[8,128]{1,0:T(8,128)S(1)}) custom-call(s32[3]{0:T(128)S(1)} %pad_add_fusion.refs_0_, s32[1]{0:T(128)S(6)} %copy.55.refs_0_.refs_1_, bf16[1024,1536]{1,0:T(8,128)(2,1)S(1)} %get-tuple-element.190.refs_1_.refs_2_, ...), custom_call_target="tpu_custom_call" | custom-call | flops 1 | bytes 6457500 | tf_op jit(solution)/shard_map/attention_second/pallas_call | solution.py:127
  95.5 2.1 collective-permute-done.16.refs_4_.refs_10_.refs_6_
  101.0 2.2 collective-permute-done.18.refs_3_
  103.3 12.3 %second_norm_up.1 = (f32[1024,512]{1,0:T(8,128)}, bf16[1024,1024]{1,0:T(8,128)(2,1)}, f32[1024,1]{1,0:T(8,128)}, bf16[1024,1024]{1,0:T(8,128)(2,1)}, bf16[1024,2...) custom-call(s32[3]{0:T(128)S(1)} %pad_add_fusion.refs_0_, ...), custom_call_target="tpu_custom_call" | custom-call | flops 1 | bytes 13837500 | tf_op jit(solution)/shard_map/second_norm_up/pallas_call | solution.py:127
  115.5 3.5 %collective-permute-done.20.refs_1_.refs_3_.refs_11_.refs_4_ = bf16[3,512,256]{2,1,0:T(8,128)(2,1)S(1)} collective-permute-done((bf16[3,512,256]{2,1,0:T(8,128)(2,1)S(1)}, bf16[3,512,256]{2,1,0:T(8,128)(2,1)S(1)}, u32[]{:S(2)}, u32[]{:S(2)}) %collective-permute-start.20) | collective-permute-done | bytes 786464 | tf_op jit(solution)/shard_map/ppermute | solution.py:83
  122.5 6.7 %down_grad.1 = (bf16[8,64,1024]{2,1,0:T(8,128)(2,1)S(1)}, bf16[8,64,1024]{2,1,0:T(8,128)(2,1)S(1)}, bf16[8,64,1024]{2,1,0:T(8,128)(2,1)S(1)}, bf16[8,64,1024]{2,1,0:T(8,128)(2,1)S(1)}, f32[8,128]{1,0:T(8,128)S(1)}) custom-call(s32[3]{0:T(128)S(1)} %pad_add_fusion.refs_0_, bf16[1024,1024]{1,0:T(8,128)(2,1)S(1)} %copy-done.1, ...), custom_call_target="tpu_custom_call" | custom-call | flops 1 | bytes 8302500 | tf_op jit(solution)/shard_map/down_grad/pallas_call | solution.py:127
  133.1 13.0 %hidden_backward.1 = (bf16[1024,2048]{1,0:T(8,128)(2,1)}, bf16[1024,1024]{1,0:T(8,128)(2,1)S(1)}, f32[1,2048]{1,0:T(1,128)S(1)}, f32[8,128]{1,0:T(8,128)S(1)}) custom-call(s32[3]{0:T(128)S(1)} %pad_add_fusion.refs_0_, bf16[1024,1024]{1,0:T(8,128)(2,1)S(1)} %copy-done.1, bf16[1024,2048]{1,0:T(8,128)(2,1)S(1)} %get-tuple-element.221.refs_2_, ...), custom_call_target="tpu_custom_call" | custom-call | flops 1 | bytes 15682500 | tf_op jit(solution)/shard_map/hidden_backward/pallas_call | solution.py:127
  146.2 2.2 copy-done.6
  148.4 6.7 %up_grad.1 = (bf16[8,64,1024]{2,1,0:T(8,128)(2,1)S(1)}, bf16[8,64,1024]{2,1,0:T(8,128)(2,1)S(1)}, bf16[8,64,1024]{2,1,0:T(8,128)(2,1)S(1)}, bf16[8,64,1024]{2,1,0:T(8,128)(2,1)S(1)}, f32[8,128]{1,0:T(8,128)S(1)}) custom-call(s32[3]{0:T(128)S(1)} %pad_add_fusion.refs_0_, bf16[1024,1024]{1,0:T(8,128)(2,1)S(1)} %copy-done.10, bf16[1024,2048]{1,0:T(8,128)(2,1)S(1)} %copy-done.6, ...), custom_call_target="tpu_custom_call" | custom-call | flops 1 | bytes 8302500 | tf_op jit(solution)/shard_map/up_grad/pallas_call | solution.py:127
  160.8 6.4 %second_norm_backward.1 = (bf16[1024,1024]{1,0:T(8,128)(2,1)S(1)}, f32[1024,512]{1,0:T(8,128)S(1)}, bf16[1024,512]{1,0:T(8,128)(2,1)S(1)}, f32[4,512]{1,0:T(4,128)S(1)}, f32[8,128]{1,0:T(8,128)S(1)}) custom-call(s32[3]{0:T(128)S(1)} %pad_add_fusion.refs_0_, bf16[1024,1024]{1,0:T(8,128)(2,1)S(1)} %copy-done.1, ...), custom_call_target="tpu_custom_call" | custom-call | flops 1 | bytes 8302500 | tf_op jit(solution)/shard_map/second_norm_backward/pallas_call | solution.py:127
  167.2 4.9 %attention_backward.2 = (bf16[1024,768]{1,0:T(8,128)(2,1)S(1)}, f32[2,1,256]{2,1,0:T(1,128)S(1)}, f32[8,128]{1,0:T(8,128)S(1)}) custom-call(s32[1]{0:T(128)S(6)} %copy.55.refs_0_.refs_1_, bf16[1024,1536]{1,0:T(8,128)(2,1)S(1)} %get-tuple-element.190.refs_1_.refs_2_, bf16[1024,512]{1,0:T(8,128)(2,1)S(1)} %get-tuple-element.235.refs_2_, ...), custom_call_target="tpu_custom_call" | custom-call | flops 1 | bytes 5535000 | tf_op jit(solution)/shard_map/attention_backward/pallas_call | solution.py:127
  172.1 4.7 %attention_backward.3 = (bf16[1024,768]{1,0:T(8,128)(2,1)S(1)}, f32[2,1,256]{2,1,0:T(1,128)S(1)}, f32[8,128]{1,0:T(8,128)S(1)}) custom-call(s32[1]{0:T(128)S(6)} %copy.55.refs_0_.refs_1_, bf16[1024,1536]{1,0:T(8,128)(2,1)S(1)} %get-tuple-element.190.refs_1_.refs_2_, bf16[1024,512]{1,0:T(8,128)(2,1)S(1)} %get-tuple-element.235.refs_2_, ...), custom_call_target="tpu_custom_call" | custom-call | flops 1 | bytes 5535000 | tf_op jit(solution)/shard_map/attention_backward/pallas_call | solution.py:127
  179.5 4.7 %output_grad.1 = (bf16[8,64,256]{2,1,0:T(8,128)(2,1)S(1)}, bf16[8,64,256]{2,1,0:T(8,128)(2,1)S(1)}, bf16[8,64,256]{2,1,0:T(8,128)(2,1)S(1)}, bf16[8,64,256]{2,1,0:T(8,128)(2,1)S(1)}, f32[8,128]{1,0:T(8,128)S(1)}) custom-call(s32[3]{0:T(128)S(1)} %pad_add_fusion.refs_0_, bf16[1024,1024]{1,0:T(8,128)(2,1)S(1)} %get-tuple-element.247.refs_1_, ...), custom_call_target="tpu_custom_call" | custom-call | flops 1 | bytes 1845000 | tf_op jit(solution)/shard_map/output_grad/pallas_call | solution.py:127
  185.9 7.8 %project_backward.1 = (bf16[1024,512]{1,0:T(8,128)(2,1)S(1)}, bf16[1024,640]{1,0:T(8,128)(2,1)S(1)}, f32[1024,128]{1,0:T(8,128)S(1)}, f32[8,1024]{1,0:T(8,128)S(1)}, f32[8,128]{1,0:T(8,128)S(1)}) custom-call(s32[3]{0:T(128)S(1)} %pad_add_fusion.refs_0_, bf16[1024,1024]{1,0:T(8,128)(2,1)S(1)} %get-tuple-element.174.refs_1_.refs_0_, ...), custom_call_target="tpu_custom_call" | custom-call | flops 1 | bytes 7380000 | tf_op jit(solution)/shard_map/project_backward/pallas_call | solution.py:127
  195.1 4.8 %collective-permute-done.29 = bf16[8,64,256]{2,1,0:T(8,128)(2,1)S(1)} collective-permute-done((bf16[8,64,256]{2,1,0:T(8,128)(2,1)S(1)}, bf16[8,64,256]{2,1,0:T(8,128)(2,1)S(1)}, u32[]{:S(2)}, u32[]{:S(2)}) %collective-permute-start.29) | collective-permute-done | bytes 262176 | tf_op jit(solution)/shard_map/ppermute | solution.py:83
  204.4 7.6 %joint_grad.1 = (bf16[8,64,896]{2,1,0:T(8,128)(2,1)S(1)}, bf16[8,64,896]{2,1,0:T(8,128)(2,1)S(1)}, bf16[8,64,768]{2,1,0:T(8,128)(2,1)S(1)}, bf16[8,64,768]{2,1,0:T(8,128)(2,1)S(1)}, f32[8,128]{1,0:T(8,128)S(1)}) custom-call(s32[3]{0:T(128)S(1)} %pad_add_fusion.refs_0_, bf16[1024,1024]{1,0:T(8,128)(2,1)S(1)} %copy-done.5, ...), custom_call_target="tpu_custom_call" | custom-call | flops 1 | bytes 9225000 | tf_op jit(solution)/shard_map/joint_grad/pallas_call | solution.py:127
  214.6 6.5 %down_project.1 = (bf16[1024,512]{1,0:T(8,128)(2,1)S(1)}, bf16[512,512]{1,0:T(8,128)(2,1)S(1)}, bf16[512,512]{1,0:T(8,128)(2,1)S(1)}, f32[8,128]{1,0:T(8,128)S(1)}) custom-call(s32[3]{0:T(128)S(1)} %pad_add_fusion.refs_0_, bf16[1024,2048]{1,0:T(8,128)(2,1)S(1)} %get-tuple-element.203.refs_2_.refs_1_, ...), custom_call_target="tpu_custom_call" | custom-call | flops 1 | bytes 8302500 | tf_op jit(solution)/shard_map/down_project/pallas_call | solution.py:127
  227.0 9.8 %collective-permute-done.40 = bf16[2,64,2560]{2,1,0:T(8,128)(2,1)S(1)} collective-permute-done((bf16[2,64,2560]{2,1,0:T(8,128)(2,1)S(1)}, bf16[2,64,2560]{2,1,0:T(8,128)(2,1)S(1)}, u32[]{:S(2)}, u32[]{:S(2)}) %collective-permute-start.40) | collective-permute-done | bytes 655392 | tf_op jit(solution)/shard_map/ppermute | solution.py:83
  242.1 3.0 %first_norm_backward.1 = (bf16[1024,512]{1,0:T(8,128)(2,1)}, f32[8,128]{1,0:T(8,128)S(1)}) custom-call(bf16[1024,1024]{1,0:T(8,128)(2,1)S(1)} %get-tuple-element.174.refs_1_.refs_0_, bf16[1024,512]{1,0:T(8,128)(2,1)S(1)} %get-tuple-element.285.refs_1_, bf16[1024,640]{1,0:T(8,128)(2,1)S(1)} %collective-permute-done.41.refs_2_, ...), custom_call_target="tpu_custom_call" | custom-call | flops 1 | bytes 5535000 | tf_op jit(solution)/shard_map/first_norm_backward/pallas_call | solution.py:127
  245.1 12.7 %collective-permute-done.44 = bf16[1,64,2560]{2,1,0:T(8,128)(2,1)S(1)} collective-permute-done((bf16[1,64,2560]{2,1,0:T(8,128)(2,1)S(1)}, bf16[1,64,2560]{2,1,0:T(8,128)(2,1)S(1)}, u32[]{:S(2)}, u32[]{:S(2)}) %collective-permute-start.44) | collective-permute-done | bytes 327712 | tf_op jit(solution)/shard_map/ppermute | solution.py:83
  261.3 10.2 %collective-permute-done.45 = bf16[2,64,1664]{2,1,0:T(8,128)(2,1)S(1)} collective-permute-done((bf16[2,64,1664]{2,1,0:T(8,128)(2,1)S(1)}, bf16[2,64,1664]{2,1,0:T(8,128)(2,1)S(1)}, u32[]{:S(2)}, u32[]{:S(2)}) %collective-permute-start.45) | collective-permute-done | bytes 426016 | tf_op jit(solution)/shard_map/ppermute | solution.py:83
  272.1 2.3 collective-permute-start.46
  275.7 7.6 %collective-permute-done.46 = bf16[1,64,1664]{2,1,0:T(8,128)(2,1)S(1)} collective-permute-done((bf16[1,64,1664]{2,1,0:T(8,128)(2,1)S(1)}, bf16[1,64,1664]{2,1,0:T(8,128)(2,1)S(1)}, u32[]{:S(2)}, u32[]{:S(2)}) %collective-permute-start.46) | collective-permute-done | bytes 213024 | tf_op jit(solution)/shard_map/ppermute | solution.py:83
  286.9 3.6 %finish_ffn.1 = (f32[2048,256]{1,0:T(8,128)}, f32[256,2048]{1,0:T(8,128)}, f32[512,256]{1,0:T(8,128)}, f32[8,128]{1,0:T(8,128)S(1)}) custom-call(s32[3]{0:T(128)S(1)} %pad_add_fusion.refs_0_, bf16[64,4608]{1,0:T(8,128)(2,1)S(1)} %get-tuple-element.314.refs_1_, bf16[64,4608]{1,0:T(8,128)(2,1)S(1)} %collective-permute-done.47.refs_2_, ...), custom_call_target="tpu_custom_call" | custom-call | flops 1 | bytes 1845000 | tf_op jit(solution)/shard_map/finish_ffn/pallas_call | solution.py:127
  (173 shorter events, 87.0 us)
Async XLA Ops:
  5.0 12.5 %collective-permute-start.5 = (bf16[1,64,2048]{2,1,0:T(8,128)(2,1)}, bf16[1,64,2048]{2,1,0:T(8,128)(2,1)S(1)}, u32[]{:S(2)}, u32[]{:S(2)}) collective-permute-start(bf16[1,64,2048]{2,1,0:T(8,128)(2,1)} %maximum_bitcast_fusion), channel_id=1, source_target_pairs={{0,6},{2,4},{4,2},{6,0},{1,7},{3,5},{5,3},{7,1},{8,14},{10,12},{12... | collective-permute-start | bytes 786440 | tf_op jit(solution)/shard_map/ppermute | solution.py:83
  9.6 23.2 %collective-permute-start.4 = (bf16[1,64,2048]{2,1,0:T(8,128)(2,1)}, bf16[1,64,2048]{2,1,0:T(8,128)(2,1)}, u32[]{:S(2)}, u32[]{:S(2)}) collective-permute-start(bf16[1,64,2048]{2,1,0:T(8,128)(2,1)} %maximum_bitcast_fusion), channel_id=1, source_target_pairs={{0,4},{2,6},{4,0},{6,2},{1,5},{3,7},{5,1},{7,3},{8,12},{10,14},{12... | collective-permute-start | bytes 786440 | tf_op jit(solution)/shard_map/ppermute | solution.py:83
  9.6 23.2 %collective-permute-start.3 = (bf16[1,64,2048]{2,1,0:T(8,128)(2,1)}, bf16[1,64,2048]{2,1,0:T(8,128)(2,1)}, u32[]{:S(2)}, u32[]{:S(2)}) collective-permute-start(bf16[1,64,2048]{2,1,0:T(8,128)(2,1)} %maximum_bitcast_fusion), channel_id=1, source_target_pairs={{0,2},{2,0},{4,6},{6,4},{1,3},{3,1},{5,7},{7,5},{8,10},{10,8},{12,... | collective-permute-start | bytes 786440 | tf_op jit(solution)/shard_map/ppermute | solution.py:83
  34.8 19.3 %collective-permute-start.7 = (bf16[3,64,2048]{2,1,0:T(8,128)(2,1)}, bf16[3,64,2048]{2,1,0:T(8,128)(2,1)S(1)}, u32[]{:S(2)}, u32[]{:S(2)}) collective-permute-start(bf16[3,64,2048]{2,1,0:T(8,128)(2,1)} %get-tuple-element.176.refs_3_.refs_5_.refs_4_.refs_8_.refs_6_), channel_id=1, source_target_pairs={{0,16},{8,24},{16,0},{24,8},{1,17},{9,25},{17,1},{25,9},{2,18},{10... | collective-permute-start | bytes 2359304 | tf_op jit(solution)/shard_map/ppermute | solution.py:83
  36.4 19.1 %collective-permute-start.6 = (bf16[3,64,2048]{2,1,0:T(8,128)(2,1)}, bf16[3,64,2048]{2,1,0:T(8,128)(2,1)}, u32[]{:S(2)}, u32[]{:S(2)}) collective-permute-start(bf16[3,64,2048]{2,1,0:T(8,128)(2,1)} %get-tuple-element.176.refs_3_.refs_5_.refs_4_.refs_8_.refs_6_), channel_id=1, source_target_pairs={{0,8},{8,0},{16,24},{24,16},{1,9},{9,1},{17,25},{25,17},{2,10},{10... | collective-permute-start | bytes 2359304 | tf_op jit(solution)/shard_map/ppermute | solution.py:83
  39.7 13.7 %collective-permute-start.8 = (bf16[1,64,2048]{2,1,0:T(8,128)(2,1)S(1)}, bf16[1,64,2048]{2,1,0:T(8,128)(2,1)S(1)}, u32[]{:S(2)}, u32[]{:S(2)}) collective-permute-start(bf16[1,64,2048]{2,1,0:T(8,128)(2,1)S(1)} %bitcast.112), channel_id=1, source_target_pairs={{0,4},{2,6},{4,0},{6,2},{1,5},{3,7},{5,1},{7,3},{8,12},{10,14},{12... | collective-permute-start | bytes 786440 | tf_op jit(solution)/shard_map/ppermute | solution.py:83
  53.5 13.9 %collective-permute-start.9 = (bf16[2,64,2048]{2,1,0:T(8,128)(2,1)S(1)}, bf16[2,64,2048]{2,1,0:T(8,128)(2,1)S(1)}, u32[]{:S(2)}, u32[]{:S(2)}) collective-permute-start(bf16[2,64,2048]{2,1,0:T(8,128)(2,1)S(1)} %get-tuple-element.182), channel_id=1, source_target_pairs={{0,2},{2,0},{4,6},{6,4},{1,3},{3,1},{5,7},{7,5},{8,10},{10,8},{12,... | collective-permute-start | bytes 1572872 | tf_op jit(solution)/shard_map/ppermute | solution.py:83
  67.5 19.1 %collective-permute-start.15 = (bf16[3,64,2048]{2,1,0:T(8,128)(2,1)S(1)}, bf16[3,64,2048]{2,1,0:T(8,128)(2,1)S(1)}, u32[]{:S(2)}, u32[]{:S(2)}) collective-permute-start(bf16[3,64,2048]{2,1,0:T(8,128)(2,1)S(1)} %get-tuple-element.186.refs_11_.refs_1_.refs_7_.refs_3_), channel_id=1, source_target_pairs={{0,16},{8,24},{16,0},{24,8},{1,17},{9,25},{17,1},{25,9},{2,18},{10... | collective-permute-start | bytes 2359304 | tf_op jit(solution)/shard_map/ppermute | solution.py:83
  68.8 17.8 %collective-permute-start.14 = (bf16[3,64,2048]{2,1,0:T(8,128)(2,1)S(1)}, bf16[3,64,2048]{2,1,0:T(8,128)(2,1)S(1)}, u32[]{:S(2)}, u32[]{:S(2)}) collective-permute-start(bf16[3,64,2048]{2,1,0:T(8,128)(2,1)S(1)} %get-tuple-element.186.refs_11_.refs_1_.refs_7_.refs_3_), channel_id=1, source_target_pairs={{0,8},{8,0},{16,24},{24,16},{1,9},{9,1},{17,25},{25,17},{2,10},{10... | collective-permute-start | bytes 2359304 | tf_op jit(solution)/shard_map/ppermute | solution.py:83
  82.6 12.8 %collective-permute-start.13 = (bf16[2,512,256]{2,1,0:T(8,128)(2,1)S(1)}, bf16[2,512,256]{2,1,0:T(8,128)(2,1)S(1)}, u32[]{:S(2)}, u32[]{:S(2)}) collective-permute-start(bf16[2,512,256]{2,1,0:T(8,128)(2,1)S(1)} %get-tuple-element.189), channel_id=1, source_target_pairs={{0,2},{2,0},{4,6},{6,4},{1,3},{3,1},{5,7},{7,5},{8,10},{10,8},{12,... | collective-permute-start | bytes 1572872 | tf_op jit(solution)/shard_map/ppermute | solution.py:83
  99.1 20.0 %collective-permute-start.20 = (bf16[3,512,256]{2,1,0:T(8,128)(2,1)S(1)}, bf16[3,512,256]{2,1,0:T(8,128)(2,1)S(1)}, u32[]{:S(2)}, u32[]{:S(2)}) collective-permute-start(bf16[3,512,256]{2,1,0:T(8,128)(2,1)S(1)} %get-tuple-element.204.refs_1_.refs_9_.refs_2_), channel_id=1, source_target_pairs={{0,16},{8,24},{16,0},{24,8},{1,17},{9,25},{17,1},{25,9},{2,18},{10... | collective-permute-start | bytes 2359304 | tf_op jit(solution)/shard_map/ppermute | solution.py:83
  99.5 19.6 %collective-permute-start.19 = (bf16[3,512,256]{2,1,0:T(8,128)(2,1)S(1)}, bf16[3,512,256]{2,1,0:T(8,128)(2,1)S(1)}, u32[]{:S(2)}, u32[]{:S(2)}) collective-permute-start(bf16[3,512,256]{2,1,0:T(8,128)(2,1)S(1)} %get-tuple-element.204.refs_1_.refs_9_.refs_2_), channel_id=1, source_target_pairs={{0,8},{8,0},{16,24},{24,16},{1,9},{9,1},{17,25},{25,17},{2,10},{10... | collective-permute-start | bytes 2359304 | tf_op jit(solution)/shard_map/ppermute | solution.py:83
  131.0 24.1 %collective-permute-start.23 = (bf16[8,64,1024]{2,1,0:T(8,128)(2,1)S(1)}, bf16[8,64,1024]{2,1,0:T(8,128)(2,1)S(1)}, u32[]{:S(2)}, u32[]{:S(2)}) collective-permute-start(bf16[8,64,1024]{2,1,0:T(8,128)(2,1)S(1)} %get-tuple-element.217), channel_id=1, source_target_pairs={{0,8},{8,0},{16,24},{24,16},{1,9},{9,1},{17,25},{25,17},{2,10},{10... | collective-permute-start | bytes 3145736 | tf_op jit(solution)/shard_map/ppermute | solution.py:83
  132.5 22.9 %collective-permute-start.24 = (bf16[8,64,1024]{2,1,0:T(8,128)(2,1)S(1)}, bf16[8,64,1024]{2,1,0:T(8,128)(2,1)S(1)}, u32[]{:S(2)}, u32[]{:S(2)}) collective-permute-start(bf16[8,64,1024]{2,1,0:T(8,128)(2,1)S(1)} %get-tuple-element.219), channel_id=1, source_target_pairs={{0,16},{8,24},{16,0},{24,8},{1,17},{9,25},{17,1},{25,9},{2,18},{10... | collective-permute-start | bytes 3145736 | tf_op jit(solution)/shard_map/ppermute | solution.py:83
  156.7 20.2 %collective-permute-start.26 = (bf16[4,64,1024]{2,1,0:T(8,128)(2,1)S(1)}, bf16[4,64,1024]{2,1,0:T(8,128)(2,1)S(1)}, u32[]{:S(2)}, u32[]{:S(2)}) collective-permute-start(bf16[4,64,1024]{2,1,0:T(8,128)(2,1)S(1)} %get-tuple-element.249), channel_id=1, source_target_pairs={{0,16},{8,24},{16,0},{24,8},{1,17},{9,25},{17,1},{25,9},{2,18},{10... | collective-permute-start | bytes 1572872 | tf_op jit(solution)/shard_map/ppermute | solution.py:83
  157.9 19.0 %collective-permute-start.27 = (bf16[4,64,1024]{2,1,0:T(8,128)(2,1)S(1)}, bf16[4,64,1024]{2,1,0:T(8,128)(2,1)S(1)}, u32[]{:S(2)}, u32[]{:S(2)}) collective-permute-start(bf16[4,64,1024]{2,1,0:T(8,128)(2,1)S(1)} %get-tuple-element.251), channel_id=1, source_target_pairs={{0,8},{8,0},{16,24},{24,16},{1,9},{9,1},{17,25},{25,17},{2,10},{10... | collective-permute-start | bytes 1572872 | tf_op jit(solution)/shard_map/ppermute | solution.py:83
  158.4 36.7 %collective-permute-start.28 = (bf16[8,64,1024]{2,1,0:T(8,128)(2,1)S(1)}, bf16[8,64,1024]{2,1,0:T(8,128)(2,1)S(1)}, u32[]{:S(2)}, u32[]{:S(2)}) collective-permute-start(bf16[8,64,1024]{2,1,0:T(8,128)(2,1)S(1)} %get-tuple-element.257), channel_id=1, source_target_pairs={{0,8},{8,0},{16,24},{24,16},{1,9},{9,1},{17,25},{25,17},{2,10},{10... | collective-permute-start | bytes 3145736 | tf_op jit(solution)/shard_map/ppermute | solution.py:83
  159.9 35.2 %collective-permute-start.30 = (bf16[8,64,1024]{2,1,0:T(8,128)(2,1)S(1)}, bf16[8,64,1024]{2,1,0:T(8,128)(2,1)S(1)}, u32[]{:S(2)}, u32[]{:S(2)}) collective-permute-start(bf16[8,64,1024]{2,1,0:T(8,128)(2,1)S(1)} %get-tuple-element.261), channel_id=1, source_target_pairs={{0,16},{8,24},{16,0},{24,8},{1,17},{9,25},{17,1},{25,9},{2,18},{10... | collective-permute-start | bytes 3145736 | tf_op jit(solution)/shard_map/ppermute | solution.py:83
  177.7 16.0 %collective-permute-start.32 = (bf16[2,64,2048]{2,1,0:T(8,128)(2,1)S(1)}, bf16[2,64,2048]{2,1,0:T(8,128)(2,1)S(1)}, u32[]{:S(2)}, u32[]{:S(2)}) collective-permute-start(bf16[2,64,2048]{2,1,0:T(8,128)(2,1)S(1)} %get-tuple-element.265), channel_id=1, source_target_pairs={{0,2},{2,0},{4,6},{6,4},{1,3},{3,1},{5,7},{7,5},{8,10},{10,8},{12,... | collective-permute-start | bytes 1572872 | tf_op jit(solution)/shard_map/ppermute | solution.py:83
  184.2 15.7 %collective-permute-start.29 = (bf16[8,64,256]{2,1,0:T(8,128)(2,1)S(1)}, bf16[8,64,256]{2,1,0:T(8,128)(2,1)S(1)}, u32[]{:S(2)}, u32[]{:S(2)}) collective-permute-start(bf16[8,64,256]{2,1,0:T(8,128)(2,1)S(1)} %get-tuple-element.259), channel_id=1, source_target_pairs={{0,8},{8,0},{16,24},{24,16},{1,9},{9,1},{17,25},{25,17},{2,10},{10... | collective-permute-start | bytes 786440 | tf_op jit(solution)/shard_map/ppermute | solution.py:83
  184.8 15.1 %collective-permute-start.31 = (bf16[8,64,256]{2,1,0:T(8,128)(2,1)S(1)}, bf16[8,64,256]{2,1,0:T(8,128)(2,1)S(1)}, u32[]{:S(2)}, u32[]{:S(2)}) collective-permute-start(bf16[8,64,256]{2,1,0:T(8,128)(2,1)S(1)} %get-tuple-element.263), channel_id=1, source_target_pairs={{0,16},{8,24},{16,0},{24,8},{1,17},{9,25},{17,1},{25,9},{2,18},{10... | collective-permute-start | bytes 786440 | tf_op jit(solution)/shard_map/ppermute | solution.py:83
  201.2 20.1 %collective-permute-start.33 = (bf16[4,64,1280]{2,1,0:T(8,128)(2,1)S(1)}, bf16[4,64,1280]{2,1,0:T(8,128)(2,1)S(1)}, u32[]{:S(2)}, u32[]{:S(2)}) collective-permute-start(bf16[4,64,1280]{2,1,0:T(8,128)(2,1)S(1)} %get-tuple-element.272), channel_id=1, source_target_pairs={{0,16},{8,24},{16,0},{24,8},{1,17},{9,25},{17,1},{25,9},{2,18},{10... | collective-permute-start | bytes 1966088 | tf_op jit(solution)/shard_map/ppermute | solution.py:83
  202.2 19.1 %collective-permute-start.34 = (bf16[4,64,1280]{2,1,0:T(8,128)(2,1)S(1)}, bf16[4,64,1280]{2,1,0:T(8,128)(2,1)S(1)}, u32[]{:S(2)}, u32[]{:S(2)}) collective-permute-start(bf16[4,64,1280]{2,1,0:T(8,128)(2,1)S(1)} %get-tuple-element.274), channel_id=1, source_target_pairs={{0,8},{8,0},{16,24},{24,16},{1,9},{9,1},{17,25},{25,17},{2,10},{10... | collective-permute-start | bytes 1966088 | tf_op jit(solution)/shard_map/ppermute | solution.py:83
  202.7 18.5 %collective-permute-start.35 = (bf16[1,64,2048]{2,1,0:T(8,128)(2,1)S(1)}, bf16[1,64,2048]{2,1,0:T(8,128)(2,1)S(1)}, u32[]{:S(2)}, u32[]{:S(2)}) collective-permute-start(bf16[1,64,2048]{2,1,0:T(8,128)(2,1)S(1)} %get-tuple-element.276), channel_id=1, source_target_pairs={{0,4},{2,6},{4,0},{6,2},{1,5},{3,7},{5,1},{7,3},{8,12},{10,14},{12... | collective-permute-start | bytes 786440 | tf_op jit(solution)/shard_map/ppermute | solution.py:83
  212.0 25.6 %collective-permute-start.38 = (bf16[8,64,896]{2,1,0:T(8,128)(2,1)S(1)}, bf16[8,64,896]{2,1,0:T(8,128)(2,1)S(1)}, u32[]{:S(2)}, u32[]{:S(2)}) collective-permute-start(bf16[8,64,896]{2,1,0:T(8,128)(2,1)S(1)} %get-tuple-element.287), channel_id=1, source_target_pairs={{0,8},{8,0},{16,24},{24,16},{1,9},{9,1},{17,25},{25,17},{2,10},{10... | collective-permute-start | bytes 2752520 | tf_op jit(solution)/shard_map/ppermute | solution.py:83
  213.5 24.1 %collective-permute-start.39 = (bf16[8,64,768]{2,1,0:T(8,128)(2,1)S(1)}, bf16[8,64,768]{2,1,0:T(8,128)(2,1)S(1)}, u32[]{:S(2)}, u32[]{:S(2)}) collective-permute-start(bf16[8,64,768]{2,1,0:T(8,128)(2,1)S(1)} %get-tuple-element.289), channel_id=1, source_target_pairs={{0,16},{8,24},{16,0},{24,8},{1,17},{9,25},{17,1},{25,9},{2,18},{10... | collective-permute-start | bytes 2359304 | tf_op jit(solution)/shard_map/ppermute | solution.py:83
  222.2 14.6 %collective-permute-start.40 = (bf16[2,64,2560]{2,1,0:T(8,128)(2,1)S(1)}, bf16[2,64,2560]{2,1,0:T(8,128)(2,1)S(1)}, u32[]{:S(2)}, u32[]{:S(2)}) collective-permute-start(bf16[2,64,2560]{2,1,0:T(8,128)(2,1)S(1)} %get-tuple-element.291), channel_id=1, source_target_pairs={{0,2},{2,0},{4,6},{6,4},{1,3},{3,1},{5,7},{7,5},{8,10},{10,8},{12,... | collective-permute-start | bytes 1966088 | tf_op jit(solution)/shard_map/ppermute | solution.py:83
  238.7 21.7 %collective-permute-start.42 = (bf16[4,64,896]{2,1,0:T(8,128)(2,1)S(1)}, bf16[4,64,896]{2,1,0:T(8,128)(2,1)S(1)}, u32[]{:S(2)}, u32[]{:S(2)}) collective-permute-start(bf16[4,64,896]{2,1,0:T(8,128)(2,1)S(1)} %get-tuple-element.301), channel_id=1, source_target_pairs={{0,16},{8,24},{16,0},{24,8},{1,17},{9,25},{17,1},{25,9},{2,18},{10... | collective-permute-start | bytes 1376264 | tf_op jit(solution)/shard_map/ppermute | solution.py:83
  239.8 20.6 %collective-permute-start.43 = (bf16[4,64,768]{2,1,0:T(8,128)(2,1)S(1)}, bf16[4,64,768]{2,1,0:T(8,128)(2,1)S(1)}, u32[]{:S(2)}, u32[]{:S(2)}) collective-permute-start(bf16[4,64,768]{2,1,0:T(8,128)(2,1)S(1)} %get-tuple-element.303), channel_id=1, source_target_pairs={{0,8},{8,0},{16,24},{24,16},{1,9},{9,1},{17,25},{25,17},{2,10},{10... | collective-permute-start | bytes 1179656 | tf_op jit(solution)/shard_map/ppermute | solution.py:83
  240.4 17.4 %collective-permute-start.44 = (bf16[1,64,2560]{2,1,0:T(8,128)(2,1)S(1)}, bf16[1,64,2560]{2,1,0:T(8,128)(2,1)S(1)}, u32[]{:S(2)}, u32[]{:S(2)}) collective-permute-start(bf16[1,64,2560]{2,1,0:T(8,128)(2,1)S(1)} %get-tuple-element.306), channel_id=1, source_target_pairs={{0,4},{2,6},{4,0},{6,2},{1,5},{3,7},{5,1},{7,3},{8,12},{10,14},{12... | collective-permute-start | bytes 983048 | tf_op jit(solution)/shard_map/ppermute | solution.py:83
  257.9 16.6 %collective-permute-start.48 = (bf16[64,4608]{1,0:T(8,128)(2,1)S(1)}, bf16[64,4608]{1,0:T(8,128)(2,1)S(1)}, u32[]{:S(2)}, u32[]{:S(2)}) collective-permute-start(bf16[64,4608]{1,0:T(8,128)(2,1)S(1)} %get-tuple-element.314.refs_1_), channel_id=1, source_target_pairs={{0,16},{8,24},{16,0},{24,8},{1,17},{9,25},{17,1},{25,9},{2,18},{10... | collective-permute-start | bytes 1769480 | tf_op jit(solution)/shard_map/ppermute | solution.py:83
  259.0 15.5 %collective-permute-start.47 = (bf16[64,4608]{1,0:T(8,128)(2,1)S(1)}, bf16[64,4608]{1,0:T(8,128)(2,1)S(1)}, u32[]{:S(2)}, u32[]{:S(2)}) collective-permute-start(bf16[64,4608]{1,0:T(8,128)(2,1)S(1)} %get-tuple-element.314.refs_1_), channel_id=1, source_target_pairs={{0,8},{8,0},{16,24},{24,16},{1,9},{9,1},{17,25},{25,17},{2,10},{10... | collective-permute-start | bytes 1769480 | tf_op jit(solution)/shard_map/ppermute | solution.py:83
  (42 other events, 289.9 us)

commit v5 on v4

--- a/solution.py
+++ b/solution.py
@@ -1267,9 +1267,9 @@
     (tokens_grad,), token = first_norm_backward(
         x, first_own, swap_cores(passed[0]), row_sums, vecs, res_grad, (token,)
     )
+    (joint_rows,), token = first_rows(joint_red, (token,), "joint_rows")
     (ffn_total,), token = row_total(lay, up_rows, (token,), "up_total", [down_total])
     ffn = Spread(lay, rest_sum(lay, ffn_total))
-    (joint_rows,), token = first_rows(joint_red, (token,), "joint_rows")
     joint_rows, token = next_rows(lay, ids, joint_rows, (token,), "joint_rows_2")
     token = ffn.forward((token,), "ffn_pieces")
     (joint_total,), token = row_total(lay, joint_rows, (token,), "joint_total")

time: 298 us -> 298 us (level)
  transfers between devices with their start and end apart: 55 -> 55, of which waited for: 26 -> 28; matrix products, arithmetic and copies ran while one was open for 1% -> 1% of each run, Pallas kernels for 38% -> 38%
where the time goes in v5:
time: 298 us; the launch traced here: 297 us
  Pallas kernels  122 us (41%)
  waiting for transfers between devices  106 us (36%)
  starting transfers between devices  53.3 us (18%)
  local copies, waits for them, and re-layouts  13.3 us (4%)
    pallas_call x44, Pallas kernels, call(): pl.pallas_call(body, grid=grid, in_specs=[spec for _, spec in ins] + [any...  122 us
    ppermute x46, waiting for transfers between devices, swap(): return lax.ppermute(value, axis, [(i, i ^ bit) for i in range(size)])  101 us
    ppermute x46, starting transfers between devices, swap(): return lax.ppermute(value, axis, [(i, i ^ bit) for i in range(size)])  51.6 us
    unnamed x38, local copies, waits for them, and re-layouts  9.4 us
  transfers between devices with their start and end apart: 55, of which 28 were waited for; matrix products, arithmetic and copies ran while one was open for 1% of the time, Pallas kernels for 38%

profile of v5, /device:TPU:0, one launch (start us, length us, event | category | flops | bytes accessed | tf_op | source)
XLA Modules:
  0.0 297.0 jit_solution(2989853820296010388)
XLA Ops:
  5.0 4.7 %collective-permute-start.5 = (bf16[1,64,2048]{2,1,0:T(8,128)(2,1)}, bf16[1,64,2048]{2,1,0:T(8,128)(2,1)S(1)}, u32[]{:S(2)}, u32[]{:S(2)}) collective-permute-start(bf16[1,64,2048]{2,1,0:T(8,128)(2,1)} %maximum_bitcast_fusion), channel_id=1, source_target_pairs={{0,6},{2,4},{4,2},{6,0},{1,7},{3,5},{5,3},{7,1},{8,14},{10,12},{12... | collective-permute-start | bytes 786440 | tf_op jit(solution)/shard_map/ppermute | solution.py:83
  17.5 15.4 %collective-permute-done.4.refs_1_ = bf16[1,64,2048]{2,1,0:T(8,128)(2,1)} collective-permute-done((bf16[1,64,2048]{2,1,0:T(8,128)(2,1)}, bf16[1,64,2048]{2,1,0:T(8,128)(2,1)}, u32[]{:S(2)}, u32[]{:S(2)}) %collective-permute-start.4) | collective-permute-done | bytes 262176 | tf_op jit(solution)/shard_map/ppermute | solution.py:83
  39.8 13.7 %collective-permute-done.8.refs_1_.refs_3_.refs_0_ = bf16[1,64,2048]{2,1,0:T(8,128)(2,1)S(1)} collective-permute-done((bf16[1,64,2048]{2,1,0:T(8,128)(2,1)S(1)}, bf16[1,64,2048]{2,1,0:T(8,128)(2,1)S(1)}, u32[]{:S(2)}, u32[]{:S(2)}) %collective-permute-start.8) | collective-permute-done | bytes 262176 | tf_op jit(solution)/shard_map/ppermute | solution.py:83
  59.5 7.9 %collective-permute-done.9.refs_4_.refs_1_ = bf16[2,64,2048]{2,1,0:T(8,128)(2,1)S(1)} collective-permute-done((bf16[2,64,2048]{2,1,0:T(8,128)(2,1)S(1)}, bf16[2,64,2048]{2,1,0:T(8,128)(2,1)S(1)}, u32[]{:S(2)}, u32[]{:S(2)}) %collective-permute-start.9) | collective-permute-done | bytes 524320 | tf_op jit(solution)/shard_map/ppermute | solution.py:83
  71.3 7.3 %first_norm_project.1 = (bf16[1024,1024]{1,0:T(8,128)(2,1)}, bf16[1024,1536]{1,0:T(8,128)(2,1)S(1)}, f32[8,128]{1,0:T(8,128)S(1)}) custom-call(s32[3]{0:T(128)S(1)} %pad_add_fusion.refs_0_, bf16[1024,1024]{1,0:T(8,128)(2,1)S(1)} %get-tuple-element.174.refs_1_.refs_0_, f32[8,512]{1,0:T(8,128)S(1)} %stack.46.refs_4_.refs_2_.refs_6_, ...), custom_call_target="tpu_custom_call" | custom-call | flops 1 | bytes 8302500 | tf_op jit(solution)/shard_map/first_norm_project/pallas_call | solution.py:127
  78.6 4.0 %collective-permute-done.10.refs_1_.refs_0_ = bf16[1,512,256]{2,1,0:T(8,128)(2,1)S(1)} collective-permute-done((bf16[1,512,256]{2,1,0:T(8,128)(2,1)S(1)}, bf16[1,512,256]{2,1,0:T(8,128)(2,1)S(1)}, u32[]{:S(2)}, u32[]{:S(2)}) %collective-permute-start.10) | collective-permute-done | bytes 262176 | tf_op jit(solution)/shard_map/ppermute | solution.py:83
  83.4 3.2 %attention_first.1 = (bf16[1024,256]{1,0:T(8,128)(2,1)S(1)}, f32[2,1,1024]{2,1,0:T(1,128)S(1)}, f32[8,128]{1,0:T(8,128)S(1)}) custom-call(s32[1]{0:T(128)S(6)} %copy.55.refs_0_.refs_1_, bf16[1024,1536]{1,0:T(8,128)(2,1)S(1)} %get-tuple-element.190.refs_1_.refs_2_, f32[8,128]{1,0:T(8,128)S(1)} %get-tuple-element.191.refs_2_), custom_call_target="tpu_custom_call" | custom-call | flops 1 | bytes 4612500 | tf_op jit(solution)/shard_map/attention_first/pallas_call | solution.py:127
  89.9 5.4 %attention_second.1 = (bf16[1024,256]{1,0:T(8,128)(2,1)S(1)}, f32[2,1,1024]{2,1,0:T(1,128)S(1)}, bf16[1024,1024]{1,0:T(8,128)(2,1)S(1)}, f32[8,128]{1,0:T(8,128)S(1)}) custom-call(s32[3]{0:T(128)S(1)} %pad_add_fusion.refs_0_, s32[1]{0:T(128)S(6)} %copy.55.refs_0_.refs_1_, bf16[1024,1536]{1,0:T(8,128)(2,1)S(1)} %get-tuple-element.190.refs_1_.refs_2_, ...), custom_call_target="tpu_custom_call" | custom-call | flops 1 | bytes 6457500 | tf_op jit(solution)/shard_map/attention_second/pallas_call | solution.py:127
  95.5 2.1 collective-permute-done.16.refs_4_.refs_10_.refs_6_
  101.0 2.2 collective-permute-done.18.refs_3_
  103.3 12.3 %second_norm_up.1 = (f32[1024,512]{1,0:T(8,128)}, bf16[1024,1024]{1,0:T(8,128)(2,1)}, f32[1024,1]{1,0:T(8,128)}, bf16[1024,1024]{1,0:T(8,128)(2,1)}, bf16[1024,2...) custom-call(s32[3]{0:T(128)S(1)} %pad_add_fusion.refs_0_, ...), custom_call_target="tpu_custom_call" | custom-call | flops 1 | bytes 13837500 | tf_op jit(solution)/shard_map/second_norm_up/pallas_call | solution.py:127
  115.5 3.5 %collective-permute-done.20.refs_1_.refs_3_.refs_11_.refs_4_ = bf16[3,512,256]{2,1,0:T(8,128)(2,1)S(1)} collective-permute-done((bf16[3,512,256]{2,1,0:T(8,128)(2,1)S(1)}, bf16[3,512,256]{2,1,0:T(8,128)(2,1)S(1)}, u32[]{:S(2)}, u32[]{:S(2)}) %collective-permute-start.20) | collective-permute-done | bytes 786464 | tf_op jit(solution)/shard_map/ppermute | solution.py:83
  122.5 6.7 %down_grad.1 = (bf16[8,64,1024]{2,1,0:T(8,128)(2,1)S(1)}, bf16[8,64,1024]{2,1,0:T(8,128)(2,1)S(1)}, bf16[8,64,1024]{2,1,0:T(8,128)(2,1)S(1)}, bf16[8,64,1024]{2,1,0:T(8,128)(2,1)S(1)}, f32[8,128]{1,0:T(8,128)S(1)}) custom-call(s32[3]{0:T(128)S(1)} %pad_add_fusion.refs_0_, bf16[1024,1024]{1,0:T(8,128)(2,1)S(1)} %copy-done.1, ...), custom_call_target="tpu_custom_call" | custom-call | flops 1 | bytes 8302500 | tf_op jit(solution)/shard_map/down_grad/pallas_call | solution.py:127
  133.1 13.0 %hidden_backward.1 = (bf16[1024,2048]{1,0:T(8,128)(2,1)}, bf16[1024,1024]{1,0:T(8,128)(2,1)S(1)}, f32[1,2048]{1,0:T(1,128)S(1)}, f32[8,128]{1,0:T(8,128)S(1)}) custom-call(s32[3]{0:T(128)S(1)} %pad_add_fusion.refs_0_, bf16[1024,1024]{1,0:T(8,128)(2,1)S(1)} %copy-done.1, bf16[1024,2048]{1,0:T(8,128)(2,1)S(1)} %get-tuple-element.221.refs_2_, ...), custom_call_target="tpu_custom_call" | custom-call | flops 1 | bytes 15682500 | tf_op jit(solution)/shard_map/hidden_backward/pallas_call | solution.py:127
  146.2 2.2 copy-done.6
  148.4 6.7 %up_grad.1 = (bf16[8,64,1024]{2,1,0:T(8,128)(2,1)S(1)}, bf16[8,64,1024]{2,1,0:T(8,128)(2,1)S(1)}, bf16[8,64,1024]{2,1,0:T(8,128)(2,1)S(1)}, bf16[8,64,1024]{2,1,0:T(8,128)(2,1)S(1)}, f32[8,128]{1,0:T(8,128)S(1)}) custom-call(s32[3]{0:T(128)S(1)} %pad_add_fusion.refs_0_, bf16[1024,1024]{1,0:T(8,128)(2,1)S(1)} %copy-done.10, bf16[1024,2048]{1,0:T(8,128)(2,1)S(1)} %copy-done.6, ...), custom_call_target="tpu_custom_call" | custom-call | flops 1 | bytes 8302500 | tf_op jit(solution)/shard_map/up_grad/pallas_call | solution.py:127
  160.8 6.4 %second_norm_backward.1 = (bf16[1024,1024]{1,0:T(8,128)(2,1)S(1)}, f32[1024,512]{1,0:T(8,128)S(1)}, bf16[1024,512]{1,0:T(8,128)(2,1)S(1)}, f32[4,512]{1,0:T(4,128)S(1)}, f32[8,128]{1,0:T(8,128)S(1)}) custom-call(s32[3]{0:T(128)S(1)} %pad_add_fusion.refs_0_, bf16[1024,1024]{1,0:T(8,128)(2,1)S(1)} %copy-done.1, ...), custom_call_target="tpu_custom_call" | custom-call | flops 1 | bytes 8302500 | tf_op jit(solution)/shard_map/second_norm_backward/pallas_call | solution.py:127
  167.2 4.9 %attention_backward.2 = (bf16[1024,768]{1,0:T(8,128)(2,1)S(1)}, f32[2,1,256]{2,1,0:T(1,128)S(1)}, f32[8,128]{1,0:T(8,128)S(1)}) custom-call(s32[1]{0:T(128)S(6)} %copy.55.refs_0_.refs_1_, bf16[1024,1536]{1,0:T(8,128)(2,1)S(1)} %get-tuple-element.190.refs_1_.refs_2_, bf16[1024,512]{1,0:T(8,128)(2,1)S(1)} %get-tuple-element.235.refs_2_, ...), custom_call_target="tpu_custom_call" | custom-call | flops 1 | bytes 5535000 | tf_op jit(solution)/shard_map/attention_backward/pallas_call | solution.py:127
  172.1 4.7 %attention_backward.3 = (bf16[1024,768]{1,0:T(8,128)(2,1)S(1)}, f32[2,1,256]{2,1,0:T(1,128)S(1)}, f32[8,128]{1,0:T(8,128)S(1)}) custom-call(s32[1]{0:T(128)S(6)} %copy.55.refs_0_.refs_1_, bf16[1024,1536]{1,0:T(8,128)(2,1)S(1)} %get-tuple-element.190.refs_1_.refs_2_, bf16[1024,512]{1,0:T(8,128)(2,1)S(1)} %get-tuple-element.235.refs_2_, ...), custom_call_target="tpu_custom_call" | custom-call | flops 1 | bytes 5535000 | tf_op jit(solution)/shard_map/attention_backward/pallas_call | solution.py:127
  179.5 4.7 %output_grad.1 = (bf16[8,64,256]{2,1,0:T(8,128)(2,1)S(1)}, bf16[8,64,256]{2,1,0:T(8,128)(2,1)S(1)}, bf16[8,64,256]{2,1,0:T(8,128)(2,1)S(1)}, bf16[8,64,256]{2,1,0:T(8,128)(2,1)S(1)}, f32[8,128]{1,0:T(8,128)S(1)}) custom-call(s32[3]{0:T(128)S(1)} %pad_add_fusion.refs_0_, bf16[1024,1024]{1,0:T(8,128)(2,1)S(1)} %get-tuple-element.247.refs_1_, ...), custom_call_target="tpu_custom_call" | custom-call | flops 1 | bytes 1845000 | tf_op jit(solution)/shard_map/output_grad/pallas_call | solution.py:127
  185.9 7.8 %project_backward.1 = (bf16[1024,512]{1,0:T(8,128)(2,1)S(1)}, bf16[1024,640]{1,0:T(8,128)(2,1)S(1)}, f32[1024,128]{1,0:T(8,128)S(1)}, f32[8,1024]{1,0:T(8,128)S(1)}, f32[8,128]{1,0:T(8,128)S(1)}) custom-call(s32[3]{0:T(128)S(1)} %pad_add_fusion.refs_0_, bf16[1024,1024]{1,0:T(8,128)(2,1)S(1)} %get-tuple-element.174.refs_1_.refs_0_, ...), custom_call_target="tpu_custom_call" | custom-call | flops 1 | bytes 7380000 | tf_op jit(solution)/shard_map/project_backward/pallas_call | solution.py:127
  195.1 4.8 %collective-permute-done.29 = bf16[8,64,256]{2,1,0:T(8,128)(2,1)S(1)} collective-permute-done((bf16[8,64,256]{2,1,0:T(8,128)(2,1)S(1)}, bf16[8,64,256]{2,1,0:T(8,128)(2,1)S(1)}, u32[]{:S(2)}, u32[]{:S(2)}) %collective-permute-start.29) | collective-permute-done | bytes 262176 | tf_op jit(solution)/shard_map/ppermute | solution.py:83
  204.4 7.6 %joint_grad.1 = (bf16[8,64,896]{2,1,0:T(8,128)(2,1)S(1)}, bf16[8,64,896]{2,1,0:T(8,128)(2,1)S(1)}, bf16[8,64,768]{2,1,0:T(8,128)(2,1)S(1)}, bf16[8,64,768]{2,1,0:T(8,128)(2,1)S(1)}, f32[8,128]{1,0:T(8,128)S(1)}) custom-call(s32[3]{0:T(128)S(1)} %pad_add_fusion.refs_0_, bf16[1024,1024]{1,0:T(8,128)(2,1)S(1)} %copy-done.5, ...), custom_call_target="tpu_custom_call" | custom-call | flops 1 | bytes 9225000 | tf_op jit(solution)/shard_map/joint_grad/pallas_call | solution.py:127
  214.6 6.5 %down_project.1 = (bf16[1024,512]{1,0:T(8,128)(2,1)S(1)}, bf16[512,512]{1,0:T(8,128)(2,1)S(1)}, bf16[512,512]{1,0:T(8,128)(2,1)S(1)}, f32[8,128]{1,0:T(8,128)S(1)}) custom-call(s32[3]{0:T(128)S(1)} %pad_add_fusion.refs_0_, bf16[1024,2048]{1,0:T(8,128)(2,1)S(1)} %get-tuple-element.203.refs_2_.refs_1_, ...), custom_call_target="tpu_custom_call" | custom-call | flops 1 | bytes 8302500 | tf_op jit(solution)/shard_map/down_project/pallas_call | solution.py:127
  227.0 9.8 %collective-permute-done.40 = bf16[2,64,2560]{2,1,0:T(8,128)(2,1)S(1)} collective-permute-done((bf16[2,64,2560]{2,1,0:T(8,128)(2,1)S(1)}, bf16[2,64,2560]{2,1,0:T(8,128)(2,1)S(1)}, u32[]{:S(2)}, u32[]{:S(2)}) %collective-permute-start.40) | collective-permute-done | bytes 655392 | tf_op jit(solution)/shard_map/ppermute | solution.py:83
  242.1 3.0 %first_norm_backward.1 = (bf16[1024,512]{1,0:T(8,128)(2,1)}, f32[8,128]{1,0:T(8,128)S(1)}) custom-call(bf16[1024,1024]{1,0:T(8,128)(2,1)S(1)} %get-tuple-element.174.refs_1_.refs_0_, bf16[1024,512]{1,0:T(8,128)(2,1)S(1)} %get-tuple-element.285.refs_1_, bf16[1024,640]{1,0:T(8,128)(2,1)S(1)} %collective-permute-done.41.refs_2_, ...), custom_call_target="tpu_custom_call" | custom-call | flops 1 | bytes 5535000 | tf_op jit(solution)/shard_map/first_norm_backward/pallas_call | solution.py:127
  245.1 6.0 %collective-permute-done.43 = bf16[4,64,768]{2,1,0:T(8,128)(2,1)S(1)} collective-permute-done((bf16[4,64,768]{2,1,0:T(8,128)(2,1)S(1)}, bf16[4,64,768]{2,1,0:T(8,128)(2,1)S(1)}, u32[]{:S(2)}, u32[]{:S(2)}) %collective-permute-start.43) | collective-permute-done | bytes 393248 | tf_op jit(solution)/shard_map/ppermute | solution.py:83
  252.5 5.3 %collective-permute-done.45 = bf16[1,64,2560]{2,1,0:T(8,128)(2,1)S(1)} collective-permute-done((bf16[1,64,2560]{2,1,0:T(8,128)(2,1)S(1)}, bf16[1,64,2560]{2,1,0:T(8,128)(2,1)S(1)}, u32[]{:S(2)}, u32[]{:S(2)}) %collective-permute-start.45) | collective-permute-done | bytes 327712 | tf_op jit(solution)/shard_map/ppermute | solution.py:83
  260.4 10.2 %collective-permute-done.44 = bf16[2,64,1664]{2,1,0:T(8,128)(2,1)S(1)} collective-permute-done((bf16[2,64,1664]{2,1,0:T(8,128)(2,1)S(1)}, bf16[2,64,1664]{2,1,0:T(8,128)(2,1)S(1)}, u32[]{:S(2)}, u32[]{:S(2)}) %collective-permute-start.44) | collective-permute-done | bytes 426016 | tf_op jit(solution)/shard_map/ppermute | solution.py:83
  271.2 2.3 collective-permute-start.46
  275.6 6.8 %collective-permute-done.46 = bf16[1,64,1664]{2,1,0:T(8,128)(2,1)S(1)} collective-permute-done((bf16[1,64,1664]{2,1,0:T(8,128)(2,1)S(1)}, bf16[1,64,1664]{2,1,0:T(8,128)(2,1)S(1)}, u32[]{:S(2)}, u32[]{:S(2)}) %collective-permute-start.46) | collective-permute-done | bytes 213024 | tf_op jit(solution)/shard_map/ppermute | solution.py:83
  286.0 3.6 %finish_ffn.1 = (f32[2048,256]{1,0:T(8,128)}, f32[256,2048]{1,0:T(8,128)}, f32[512,256]{1,0:T(8,128)}, f32[8,128]{1,0:T(8,128)S(1)}) custom-call(s32[3]{0:T(128)S(1)} %pad_add_fusion.refs_0_, bf16[64,4608]{1,0:T(8,128)(2,1)S(1)} %get-tuple-element.314.refs_1_, bf16[64,4608]{1,0:T(8,128)(2,1)S(1)} %collective-permute-done.47.refs_2_, ...), custom_call_target="tpu_custom_call" | custom-call | flops 1 | bytes 1845000 | tf_op jit(solution)/shard_map/finish_ffn/pallas_call | solution.py:127
  (173 shorter events, 90.3 us)
Async XLA Ops:
  5.0 12.5 %collective-permute-start.5 = (bf16[1,64,2048]{2,1,0:T(8,128)(2,1)}, bf16[1,64,2048]{2,1,0:T(8,128)(2,1)S(1)}, u32[]{:S(2)}, u32[]{:S(2)}) collective-permute-start(bf16[1,64,2048]{2,1,0:T(8,128)(2,1)} %maximum_bitcast_fusion), channel_id=1, source_target_pairs={{0,6},{2,4},{4,2},{6,0},{1,7},{3,5},{5,3},{7,1},{8,14},{10,12},{12... | collective-permute-start | bytes 786440 | tf_op jit(solution)/shard_map/ppermute | solution.py:83
  9.6 23.2 %collective-permute-start.4 = (bf16[1,64,2048]{2,1,0:T(8,128)(2,1)}, bf16[1,64,2048]{2,1,0:T(8,128)(2,1)}, u32[]{:S(2)}, u32[]{:S(2)}) collective-permute-start(bf16[1,64,2048]{2,1,0:T(8,128)(2,1)} %maximum_bitcast_fusion), channel_id=1, source_target_pairs={{0,4},{2,6},{4,0},{6,2},{1,5},{3,7},{5,1},{7,3},{8,12},{10,14},{12... | collective-permute-start | bytes 786440 | tf_op jit(solution)/shard_map/ppermute | solution.py:83
  9.6 23.2 %collective-permute-start.3 = (bf16[1,64,2048]{2,1,0:T(8,128)(2,1)}, bf16[1,64,2048]{2,1,0:T(8,128)(2,1)}, u32[]{:S(2)}, u32[]{:S(2)}) collective-permute-start(bf16[1,64,2048]{2,1,0:T(8,128)(2,1)} %maximum_bitcast_fusion), channel_id=1, source_target_pairs={{0,2},{2,0},{4,6},{6,4},{1,3},{3,1},{5,7},{7,5},{8,10},{10,8},{12,... | collective-permute-start | bytes 786440 | tf_op jit(solution)/shard_map/ppermute | solution.py:83
  34.8 19.3 %collective-permute-start.7 = (bf16[3,64,2048]{2,1,0:T(8,128)(2,1)}, bf16[3,64,2048]{2,1,0:T(8,128)(2,1)S(1)}, u32[]{:S(2)}, u32[]{:S(2)}) collective-permute-start(bf16[3,64,2048]{2,1,0:T(8,128)(2,1)} %get-tuple-element.176.refs_3_.refs_5_.refs_4_.refs_8_.refs_6_), channel_id=1, source_target_pairs={{0,16},{8,24},{16,0},{24,8},{1,17},{9,25},{17,1},{25,9},{2,18},{10... | collective-permute-start | bytes 2359304 | tf_op jit(solution)/shard_map/ppermute | solution.py:83
  36.4 19.1 %collective-permute-start.6 = (bf16[3,64,2048]{2,1,0:T(8,128)(2,1)}, bf16[3,64,2048]{2,1,0:T(8,128)(2,1)}, u32[]{:S(2)}, u32[]{:S(2)}) collective-permute-start(bf16[3,64,2048]{2,1,0:T(8,128)(2,1)} %get-tuple-element.176.refs_3_.refs_5_.refs_4_.refs_8_.refs_6_), channel_id=1, source_target_pairs={{0,8},{8,0},{16,24},{24,16},{1,9},{9,1},{17,25},{25,17},{2,10},{10... | collective-permute-start | bytes 2359304 | tf_op jit(solution)/shard_map/ppermute | solution.py:83
  39.7 13.7 %collective-permute-start.8 = (bf16[1,64,2048]{2,1,0:T(8,128)(2,1)S(1)}, bf16[1,64,2048]{2,1,0:T(8,128)(2,1)S(1)}, u32[]{:S(2)}, u32[]{:S(2)}) collective-permute-start(bf16[1,64,2048]{2,1,0:T(8,128)(2,1)S(1)} %bitcast.112), channel_id=1, source_target_pairs={{0,4},{2,6},{4,0},{6,2},{1,5},{3,7},{5,1},{7,3},{8,12},{10,14},{12... | collective-permute-start | bytes 786440 | tf_op jit(solution)/shard_map/ppermute | solution.py:83
  53.5 13.9 %collective-permute-start.9 = (bf16[2,64,2048]{2,1,0:T(8,128)(2,1)S(1)}, bf16[2,64,2048]{2,1,0:T(8,128)(2,1)S(1)}, u32[]{:S(2)}, u32[]{:S(2)}) collective-permute-start(bf16[2,64,2048]{2,1,0:T(8,128)(2,1)S(1)} %get-tuple-element.182), channel_id=1, source_target_pairs={{0,2},{2,0},{4,6},{6,4},{1,3},{3,1},{5,7},{7,5},{8,10},{10,8},{12,... | collective-permute-start | bytes 1572872 | tf_op jit(solution)/shard_map/ppermute | solution.py:83
  67.5 19.1 %collective-permute-start.15 = (bf16[3,64,2048]{2,1,0:T(8,128)(2,1)S(1)}, bf16[3,64,2048]{2,1,0:T(8,128)(2,1)S(1)}, u32[]{:S(2)}, u32[]{:S(2)}) collective-permute-start(bf16[3,64,2048]{2,1,0:T(8,128)(2,1)S(1)} %get-tuple-element.186.refs_11_.refs_1_.refs_7_.refs_3_), channel_id=1, source_target_pairs={{0,16},{8,24},{16,0},{24,8},{1,17},{9,25},{17,1},{25,9},{2,18},{10... | collective-permute-start | bytes 2359304 | tf_op jit(solution)/shard_map/ppermute | solution.py:83
  68.8 17.8 %collective-permute-start.14 = (bf16[3,64,2048]{2,1,0:T(8,128)(2,1)S(1)}, bf16[3,64,2048]{2,1,0:T(8,128)(2,1)S(1)}, u32[]{:S(2)}, u32[]{:S(2)}) collective-permute-start(bf16[3,64,2048]{2,1,0:T(8,128)(2,1)S(1)} %get-tuple-element.186.refs_11_.refs_1_.refs_7_.refs_3_), channel_id=1, source_target_pairs={{0,8},{8,0},{16,24},{24,16},{1,9},{9,1},{17,25},{25,17},{2,10},{10... | collective-permute-start | bytes 2359304 | tf_op jit(solution)/shard_map/ppermute | solution.py:83
  82.6 12.8 %collective-permute-start.13 = (bf16[2,512,256]{2,1,0:T(8,128)(2,1)S(1)}, bf16[2,512,256]{2,1,0:T(8,128)(2,1)S(1)}, u32[]{:S(2)}, u32[]{:S(2)}) collective-permute-start(bf16[2,512,256]{2,1,0:T(8,128)(2,1)S(1)} %get-tuple-element.189), channel_id=1, source_target_pairs={{0,2},{2,0},{4,6},{6,4},{1,3},{3,1},{5,7},{7,5},{8,10},{10,8},{12,... | collective-permute-start | bytes 1572872 | tf_op jit(solution)/shard_map/ppermute | solution.py:83
  99.1 20.0 %collective-permute-start.20 = (bf16[3,512,256]{2,1,0:T(8,128)(2,1)S(1)}, bf16[3,512,256]{2,1,0:T(8,128)(2,1)S(1)}, u32[]{:S(2)}, u32[]{:S(2)}) collective-permute-start(bf16[3,512,256]{2,1,0:T(8,128)(2,1)S(1)} %get-tuple-element.204.refs_1_.refs_9_.refs_2_), channel_id=1, source_target_pairs={{0,16},{8,24},{16,0},{24,8},{1,17},{9,25},{17,1},{25,9},{2,18},{10... | collective-permute-start | bytes 2359304 | tf_op jit(solution)/shard_map/ppermute | solution.py:83
  99.5 19.6 %collective-permute-start.19 = (bf16[3,512,256]{2,1,0:T(8,128)(2,1)S(1)}, bf16[3,512,256]{2,1,0:T(8,128)(2,1)S(1)}, u32[]{:S(2)}, u32[]{:S(2)}) collective-permute-start(bf16[3,512,256]{2,1,0:T(8,128)(2,1)S(1)} %get-tuple-element.204.refs_1_.refs_9_.refs_2_), channel_id=1, source_target_pairs={{0,8},{8,0},{16,24},{24,16},{1,9},{9,1},{17,25},{25,17},{2,10},{10... | collective-permute-start | bytes 2359304 | tf_op jit(solution)/shard_map/ppermute | solution.py:83
  131.0 24.1 %collective-permute-start.23 = (bf16[8,64,1024]{2,1,0:T(8,128)(2,1)S(1)}, bf16[8,64,1024]{2,1,0:T(8,128)(2,1)S(1)}, u32[]{:S(2)}, u32[]{:S(2)}) collective-permute-start(bf16[8,64,1024]{2,1,0:T(8,128)(2,1)S(1)} %get-tuple-element.217), channel_id=1, source_target_pairs={{0,8},{8,0},{16,24},{24,16},{1,9},{9,1},{17,25},{25,17},{2,10},{10... | collective-permute-start | bytes 3145736 | tf_op jit(solution)/shard_map/ppermute | solution.py:83
  132.5 22.9 %collective-permute-start.24 = (bf16[8,64,1024]{2,1,0:T(8,128)(2,1)S(1)}, bf16[8,64,1024]{2,1,0:T(8,128)(2,1)S(1)}, u32[]{:S(2)}, u32[]{:S(2)}) collective-permute-start(bf16[8,64,1024]{2,1,0:T(8,128)(2,1)S(1)} %get-tuple-element.219), channel_id=1, source_target_pairs={{0,16},{8,24},{16,0},{24,8},{1,17},{9,25},{17,1},{25,9},{2,18},{10... | collective-permute-start | bytes 3145736 | tf_op jit(solution)/shard_map/ppermute | solution.py:83
  156.7 20.2 %collective-permute-start.26 = (bf16[4,64,1024]{2,1,0:T(8,128)(2,1)S(1)}, bf16[4,64,1024]{2,1,0:T(8,128)(2,1)S(1)}, u32[]{:S(2)}, u32[]{:S(2)}) collective-permute-start(bf16[4,64,1024]{2,1,0:T(8,128)(2,1)S(1)} %get-tuple-element.249), channel_id=1, source_target_pairs={{0,16},{8,24},{16,0},{24,8},{1,17},{9,25},{17,1},{25,9},{2,18},{10... | collective-permute-start | bytes 1572872 | tf_op jit(solution)/shard_map/ppermute | solution.py:83
  157.9 19.0 %collective-permute-start.27 = (bf16[4,64,1024]{2,1,0:T(8,128)(2,1)S(1)}, bf16[4,64,1024]{2,1,0:T(8,128)(2,1)S(1)}, u32[]{:S(2)}, u32[]{:S(2)}) collective-permute-start(bf16[4,64,1024]{2,1,0:T(8,128)(2,1)S(1)} %get-tuple-element.251), channel_id=1, source_target_pairs={{0,8},{8,0},{16,24},{24,16},{1,9},{9,1},{17,25},{25,17},{2,10},{10... | collective-permute-start | bytes 1572872 | tf_op jit(solution)/shard_map/ppermute | solution.py:83
  158.4 36.7 %collective-permute-start.28 = (bf16[8,64,1024]{2,1,0:T(8,128)(2,1)S(1)}, bf16[8,64,1024]{2,1,0:T(8,128)(2,1)S(1)}, u32[]{:S(2)}, u32[]{:S(2)}) collective-permute-start(bf16[8,64,1024]{2,1,0:T(8,128)(2,1)S(1)} %get-tuple-element.257), channel_id=1, source_target_pairs={{0,8},{8,0},{16,24},{24,16},{1,9},{9,1},{17,25},{25,17},{2,10},{10... | collective-permute-start | bytes 3145736 | tf_op jit(solution)/shard_map/ppermute | solution.py:83
  159.9 35.2 %collective-permute-start.30 = (bf16[8,64,1024]{2,1,0:T(8,128)(2,1)S(1)}, bf16[8,64,1024]{2,1,0:T(8,128)(2,1)S(1)}, u32[]{:S(2)}, u32[]{:S(2)}) collective-permute-start(bf16[8,64,1024]{2,1,0:T(8,128)(2,1)S(1)} %get-tuple-element.261), channel_id=1, source_target_pairs={{0,16},{8,24},{16,0},{24,8},{1,17},{9,25},{17,1},{25,9},{2,18},{10... | collective-permute-start | bytes 3145736 | tf_op jit(solution)/shard_map/ppermute | solution.py:83
  177.7 16.0 %collective-permute-start.32 = (bf16[2,64,2048]{2,1,0:T(8,128)(2,1)S(1)}, bf16[2,64,2048]{2,1,0:T(8,128)(2,1)S(1)}, u32[]{:S(2)}, u32[]{:S(2)}) collective-permute-start(bf16[2,64,2048]{2,1,0:T(8,128)(2,1)S(1)} %get-tuple-element.265), channel_id=1, source_target_pairs={{0,2},{2,0},{4,6},{6,4},{1,3},{3,1},{5,7},{7,5},{8,10},{10,8},{12,... | collective-permute-start | bytes 1572872 | tf_op jit(solution)/shard_map/ppermute | solution.py:83
  184.2 15.7 %collective-permute-start.29 = (bf16[8,64,256]{2,1,0:T(8,128)(2,1)S(1)}, bf16[8,64,256]{2,1,0:T(8,128)(2,1)S(1)}, u32[]{:S(2)}, u32[]{:S(2)}) collective-permute-start(bf16[8,64,256]{2,1,0:T(8,128)(2,1)S(1)} %get-tuple-element.259), channel_id=1, source_target_pairs={{0,8},{8,0},{16,24},{24,16},{1,9},{9,1},{17,25},{25,17},{2,10},{10... | collective-permute-start | bytes 786440 | tf_op jit(solution)/shard_map/ppermute | solution.py:83
  184.8 15.1 %collective-permute-start.31 = (bf16[8,64,256]{2,1,0:T(8,128)(2,1)S(1)}, bf16[8,64,256]{2,1,0:T(8,128)(2,1)S(1)}, u32[]{:S(2)}, u32[]{:S(2)}) collective-permute-start(bf16[8,64,256]{2,1,0:T(8,128)(2,1)S(1)} %get-tuple-element.263), channel_id=1, source_target_pairs={{0,16},{8,24},{16,0},{24,8},{1,17},{9,25},{17,1},{25,9},{2,18},{10... | collective-permute-start | bytes 786440 | tf_op jit(solution)/shard_map/ppermute | solution.py:83
  201.2 20.1 %collective-permute-start.33 = (bf16[4,64,1280]{2,1,0:T(8,128)(2,1)S(1)}, bf16[4,64,1280]{2,1,0:T(8,128)(2,1)S(1)}, u32[]{:S(2)}, u32[]{:S(2)}) collective-permute-start(bf16[4,64,1280]{2,1,0:T(8,128)(2,1)S(1)} %get-tuple-element.272), channel_id=1, source_target_pairs={{0,16},{8,24},{16,0},{24,8},{1,17},{9,25},{17,1},{25,9},{2,18},{10... | collective-permute-start | bytes 1966088 | tf_op jit(solution)/shard_map/ppermute | solution.py:83
  202.2 19.1 %collective-permute-start.34 = (bf16[4,64,1280]{2,1,0:T(8,128)(2,1)S(1)}, bf16[4,64,1280]{2,1,0:T(8,128)(2,1)S(1)}, u32[]{:S(2)}, u32[]{:S(2)}) collective-permute-start(bf16[4,64,1280]{2,1,0:T(8,128)(2,1)S(1)} %get-tuple-element.274), channel_id=1, source_target_pairs={{0,8},{8,0},{16,24},{24,16},{1,9},{9,1},{17,25},{25,17},{2,10},{10... | collective-permute-start | bytes 1966088 | tf_op jit(solution)/shard_map/ppermute | solution.py:83
  202.7 18.5 %collective-permute-start.35 = (bf16[1,64,2048]{2,1,0:T(8,128)(2,1)S(1)}, bf16[1,64,2048]{2,1,0:T(8,128)(2,1)S(1)}, u32[]{:S(2)}, u32[]{:S(2)}) collective-permute-start(bf16[1,64,2048]{2,1,0:T(8,128)(2,1)S(1)} %get-tuple-element.276), channel_id=1, source_target_pairs={{0,4},{2,6},{4,0},{6,2},{1,5},{3,7},{5,1},{7,3},{8,12},{10,14},{12... | collective-permute-start | bytes 786440 | tf_op jit(solution)/shard_map/ppermute | solution.py:83
  212.0 25.6 %collective-permute-start.38 = (bf16[8,64,896]{2,1,0:T(8,128)(2,1)S(1)}, bf16[8,64,896]{2,1,0:T(8,128)(2,1)S(1)}, u32[]{:S(2)}, u32[]{:S(2)}) collective-permute-start(bf16[8,64,896]{2,1,0:T(8,128)(2,1)S(1)} %get-tuple-element.287), channel_id=1, source_target_pairs={{0,8},{8,0},{16,24},{24,16},{1,9},{9,1},{17,25},{25,17},{2,10},{10... | collective-permute-start | bytes 2752520 | tf_op jit(solution)/shard_map/ppermute | solution.py:83
  213.5 24.1 %collective-permute-start.39 = (bf16[8,64,768]{2,1,0:T(8,128)(2,1)S(1)}, bf16[8,64,768]{2,1,0:T(8,128)(2,1)S(1)}, u32[]{:S(2)}, u32[]{:S(2)}) collective-permute-start(bf16[8,64,768]{2,1,0:T(8,128)(2,1)S(1)} %get-tuple-element.289), channel_id=1, source_target_pairs={{0,16},{8,24},{16,0},{24,8},{1,17},{9,25},{17,1},{25,9},{2,18},{10... | collective-permute-start | bytes 2359304 | tf_op jit(solution)/shard_map/ppermute | solution.py:83
  222.2 14.6 %collective-permute-start.40 = (bf16[2,64,2560]{2,1,0:T(8,128)(2,1)S(1)}, bf16[2,64,2560]{2,1,0:T(8,128)(2,1)S(1)}, u32[]{:S(2)}, u32[]{:S(2)}) collective-permute-start(bf16[2,64,2560]{2,1,0:T(8,128)(2,1)S(1)} %get-tuple-element.291), channel_id=1, source_target_pairs={{0,2},{2,0},{4,6},{6,4},{1,3},{3,1},{5,7},{7,5},{8,10},{10,8},{12,... | collective-permute-start | bytes 1966088 | tf_op jit(solution)/shard_map/ppermute | solution.py:83
  238.7 12.9 %collective-permute-start.42 = (bf16[4,64,896]{2,1,0:T(8,128)(2,1)S(1)}, bf16[4,64,896]{2,1,0:T(8,128)(2,1)S(1)}, u32[]{:S(2)}, u32[]{:S(2)}) collective-permute-start(bf16[4,64,896]{2,1,0:T(8,128)(2,1)S(1)} %get-tuple-element.301), channel_id=1, source_target_pairs={{0,16},{8,24},{16,0},{24,8},{1,17},{9,25},{17,1},{25,9},{2,18},{10... | collective-permute-start | bytes 1376264 | tf_op jit(solution)/shard_map/ppermute | solution.py:83
  240.4 17.4 %collective-permute-start.45 = (bf16[1,64,2560]{2,1,0:T(8,128)(2,1)S(1)}, bf16[1,64,2560]{2,1,0:T(8,128)(2,1)S(1)}, u32[]{:S(2)}, u32[]{:S(2)}) collective-permute-start(bf16[1,64,2560]{2,1,0:T(8,128)(2,1)S(1)} %get-tuple-element.309), channel_id=1, source_target_pairs={{0,4},{2,6},{4,0},{6,2},{1,5},{3,7},{5,1},{7,3},{8,12},{10,14},{12... | collective-permute-start | bytes 983048 | tf_op jit(solution)/shard_map/ppermute | solution.py:83
  257.9 15.7 %collective-permute-start.48 = (bf16[64,4608]{1,0:T(8,128)(2,1)S(1)}, bf16[64,4608]{1,0:T(8,128)(2,1)S(1)}, u32[]{:S(2)}, u32[]{:S(2)}) collective-permute-start(bf16[64,4608]{1,0:T(8,128)(2,1)S(1)} %get-tuple-element.314.refs_1_), channel_id=1, source_target_pairs={{0,16},{8,24},{16,0},{24,8},{1,17},{9,25},{17,1},{25,9},{2,18},{10... | collective-permute-start | bytes 1769480 | tf_op jit(solution)/shard_map/ppermute | solution.py:83
  259.0 14.6 %collective-permute-start.47 = (bf16[64,4608]{1,0:T(8,128)(2,1)S(1)}, bf16[64,4608]{1,0:T(8,128)(2,1)S(1)}, u32[]{:S(2)}, u32[]{:S(2)}) collective-permute-start(bf16[64,4608]{1,0:T(8,128)(2,1)S(1)} %get-tuple-element.314.refs_1_), channel_id=1, source_target_pairs={{0,8},{8,0},{16,24},{24,16},{1,9},{9,1},{17,25},{25,17},{2,10},{10... | collective-permute-start | bytes 1769480 | tf_op jit(solution)/shard_map/ppermute | solution.py:83
  273.6 12.4 %collective-permute-start.52 = (bf16[64,2304]{1,0:T(8,128)(2,1)S(1)}, bf16[64,2304]{1,0:T(8,128)(2,1)S(1)}, u32[]{:S(2)}, u32[]{:S(2)}) collective-permute-start(bf16[64,2304]{1,0:T(8,128)(2,1)S(1)} %bitcast.119), channel_id=1, source_target_pairs={{0,16},{8,24},{16,0},{24,8},{1,17},{9,25},{17,1},{25,9},{2,18},{10... | collective-permute-start | bytes 884744 | tf_op jit(solution)/shard_map/ppermute | solution.py:83
  (42 other events, 288.6 us)
